TPU v7x, 256 devices: a whole 4x4x8 slice. The times are simulated.
256 devices in a mesh: row: 16 (over x, y), col: 16 (over z, core).
Axes of the slice: x: 4, y: 4, z: 8, core: 2. Of those that a mesh axis runs over, the one named last changes fastest.
Arguments:
- incident: bfloat16 [65536, 256], P(('col', 'row')), may hold values from -6 to 6
- perm: int32 [512, 128], P(('col', 'row')), may hold values from 0 to 127, as said below
- far_u: bfloat16 [8192, 2, 128, 64], P(('row', 'col')), may hold values from -0.09375 to 0.09375
- far_v: bfloat16 [8192, 2, 128, 64], P(('row', 'col')), may hold values from -0.375 to 0.375
- far_rank: int32 [8192], P(('row', 'col')), may hold values from 16 to 64, as said below
- far_rows: int32 [8192], P(('row', 'col')), may hold values from 0 to 511, as said below
- far_cols: int32 [8192], P(('row', 'col')), may hold values from 0 to 511, as said below
- near_block: bfloat16 [7168, 2, 128, 128], P(('row', 'col')), may hold values from -0.0625 to 0.0625
- near_rows: int32 [7168], P(('row', 'col')), may hold values from 0 to 511, as said below
- near_cols: int32 [7168], P(('row', 'col')), may hold values from 0 to 511, as said below
Outputs:
- scattered: bfloat16 [65536, 256], P(('row', 'col'))
Inputs may be any that keep to these rules, and one draw needn't show every extreme that they name: `perm`: each row is a permutation of 0 to 127. `far_rank`: each value is 16, 32 or 64. `far_rows`: block g lies on mesh device d = g // 32 (row index d // number of col devices, col index d % number of col devices); its row cluster lies among the 2 * (col devices) clusters of that row index's slab of the output. `far_cols`: block g lies on device d = g // 32; its column cluster lies among the 2 * (row devices) clusters that the devices of its col index hold of incident. `near_rows`: as for far_rows, with 28 blocks a device. `near_cols`: as for far_cols, with 28 blocks a device.
All inputs are finite; a program needn't handle non-finite values.
Results may differ from a plain program's by a relative error of at most 0.0035.
Values may be sent and summed in bfloat16 or wider, within the bound.
No kernel may reach another device: no remote copies, remote signals or barrier semaphores. Data moves between devices by JAX's collectives and lax.ppermute only.
A program may use at most 64 MiB of HBM per device.

v0:
```python
import jax
import jax.numpy as jnp
from jax import lax
from jax.sharding import PartitionSpec as P


def swap_parts(values):
    half = values.shape[-1] // 2
    return jnp.concatenate([-values[..., half:], values[..., :half]], axis=-1)


def collect_rows(terms, targets, first, count):
    segment = targets - first
    inside = (segment >= 0) & (segment < count)
    segment = jnp.where(inside, segment, count)
    summed = jax.ops.segment_sum(terms, segment, num_segments=count + 1)[:count]
    return summed.reshape(count * terms.shape[1], terms.shape[2])


def body(
    incident, perm, far_u, far_v, far_rank, far_rows, far_cols, near_block, near_rows, near_cols
):
    clusters = perm.shape[0]
    leaf_size = perm.shape[1]
    width = incident.shape[1]
    ranks = far_u.shape[3]
    local = jnp.take_along_axis(
        incident.reshape(clusters, leaf_size, width), perm[:, :, None], axis=1
    )
    slab = lax.all_gather(local.reshape(clusters * leaf_size, width), "row", axis=0, tiled=True)
    slabs = slab.reshape(-1, leaf_size, width)
    col_base = lax.axis_index("col") * slabs.shape[0]
    row_count = clusters * lax.axis_size("col")
    row_base = lax.axis_index("row") * row_count
    trial = slabs[far_cols - col_base]
    coeff = jnp.einsum("blr,blc->brc", far_v[:, 0], trial, preferred_element_type=jnp.float32)
    coeff = coeff + jnp.einsum(
        "blr,blc->brc", far_v[:, 1], swap_parts(trial), preferred_element_type=jnp.float32
    )
    keep = (jnp.arange(ranks, dtype=jnp.int32)[None, :] < far_rank[:, None]).astype(jnp.float32)
    coeff = (coeff * keep[:, :, None]).astype(jnp.bfloat16)
    term = jnp.einsum("blr,brc->blc", far_u[:, 0], coeff, preferred_element_type=jnp.float32)
    trial = slabs[near_cols - col_base]
    near_term = jnp.einsum(
        "blm,bmc->blc", near_block[:, 0], trial, preferred_element_type=jnp.float32
    )
    terms = jnp.concatenate(
        [
            term
            + jnp.einsum(
                "blr,brc->blc", far_u[:, 1], swap_parts(coeff), preferred_element_type=jnp.float32
            ),
            near_term
            + jnp.einsum(
                "blm,bmc->blc",
                near_block[:, 1],
                swap_parts(trial),
                preferred_element_type=jnp.float32,
            ),
        ],
        axis=0,
    )
    targets = jnp.concatenate([far_rows, near_rows], axis=0)
    result = lax.psum_scatter(
        collect_rows(terms, targets, row_base, row_count), "col", scatter_dimension=0, tiled=True
    )
    return result.astype(jnp.bfloat16)


def solution(mesh):
    placed = (
        P(("col", "row"), None),
        P(("col", "row"), None),
        P(("row", "col"), None, None, None),
        P(("row", "col"), None, None, None),
        P(("row", "col")),
        P(("row", "col")),
        P(("row", "col")),
        P(("row", "col"), None, None, None),
        P(("row", "col")),
        P(("row", "col")),
    )
    return jax.shard_map(
        body, mesh=mesh, in_specs=placed, out_specs=P(("row", "col"), None), check_vma=False
    )
```

profile of v0, /device:TPU:1, one launch (start us, length us, event | category | flops | bytes accessed | tf_op | source)
XLA Modules:
  0.0 193.5 jit_solution(28104364799617180)
XLA Ops:
  6.5 0.0 copy-start
  6.5 0.0 all-gather.2.cloned.1.call-start
  6.5 0.7 and_bitcast_fusion
  7.3 0.7 fusion.28
  7.9 0.0 copy-done
  7.9 1.7 gather_fusion.2
  9.6 0.8 broadcast_select_fusion
  10.4 0.0 all-gather.2.cloned.1.call-update
  10.4 0.0 reduce-scatter.2.cloned.1.call-start
  10.4 0.8 fusion.29
  11.2 0.7 compare_select_fusion.1
  11.9 0.7 compare_select_fusion.2
  12.5 0.7 fusion.27
  13.3 50.2 %all-gather.2.cloned.1.call-done = bf16[4096,256]{1,0:T(8,128)(2,1)} async-done(((bf16[256,256]{1,0:T(8,128)(2,1)}), bf16[4096,256]{1,0:T(8,128)(2,1)}) %all-gather.2.cloned.1.call-update) | async-done | bytes 2097168 | tf_op jit(solution)/shard_map/all_gather | solution.py:30
  63.5 3.5 %gather_fusion.1 = bf16[28,128,256]{2,1,0:T(8,128)(2,1)} fusion(bf16[32,128,256]{2,1,0:T(8,128)(2,1)} %bitcast.56, s32[1024]{0:T(1024)S(1)} %pad_clamp_fusion), kind=kCustom, calls=%fused_computation.1 | custom fusion | bytes 3670128 | tf_op jit(solution)/shard_map/gather | solution.py:43
  67.0 2.3 %gather_fusion = bf16[32,128,256]{2,1,0:T(8,128)(2,1)S(1)} fusion(bf16[32,128,256]{2,1,0:T(8,128)(2,1)} %bitcast.57, s32[1024]{0:T(1024)S(1)} %pad_clamp_fusion.1), kind=kCustom, calls=%fused_computation | custom fusion | bytes 4194432 | tf_op jit(solution)/shard_map/gather | solution.py:35
  69.2 2.6 %fusion.33 = (bf16[28,128,128]{2,1,0:T(8,128)(2,1)S(1)}, bf16[28,128,128]{2,1,0:T(8,128)(2,1)}) fusion(bf16[28,128,256]{2,1,0:T(8,128)(2,1)} %gather_fusion.1), kind=kLoop, calls=%fused_computation.52 | loop fusion | bytes 3670016 | tf_op jit(solution)/shard_map/slice | solution.py:9
  71.8 1.3 copy.33
  73.1 1.4 neg.11
  74.5 2.2 %copy.34 = bf16[28,128,128]{1,2,0:T(8,128)(2,1)} copy(bf16[28,128,128]{2,1,0:T(8,128)(2,1)} %get-tuple-element.8) | data formatting | bytes 1835008
  76.7 2.4 %fusion.13 = f32[28,256,128]{2,1,0:T(8,128)S(1)} fusion(bf16[28,128,256]{2,1,0:T(8,128)(2,1)} %gather_fusion.1, bf16[28,2,128,128]{3,2,1,0:T(8,128)(2,1)} %param.17), kind=kOutput, calls=%fused_computation.20 | convolution fusion | flops 234881024 | bytes 6422528 | tf_op jit(solution)/shard_map/blm,bmc->blc/dot_general | solution.py:44
  79.1 0.0 copy-start.3
  79.1 0.2 slice_negate_fusion
  79.4 1.0 copy-done.3
  80.3 0.5 fusion.21
  80.8 0.6 multiply_convert_fusion
  81.4 0.0 copy-start.4
  81.4 0.1 slice_negate_fusion.1
  81.5 1.1 copy-done.4
  82.6 0.0 copy-start.1
  82.6 0.0 copy-start.2
  82.6 0.8 fusion.18
  83.4 0.4 copy-done.1
  83.8 0.6 copy-done.2
  84.4 0.7 add_bitcast_fusion.1
  85.1 0.8 add_bitcast_fusion
  85.9 4.1 %pad_maximum_fusion = f32[60,128,256]{1,2,0:T(8,128)} fusion(f32[28,128,256]{1,2,0:T(8,128)S(1)} %add_bitcast_fusion.1, f32[32,128,256]{1,2,0:T(8,128)S(1)} %add_bitcast_fusion), kind=kLoop, calls=%fused_computation.4 | loop fusion | flops 1966080 | bytes 15728640 | tf_op jit(solution)/shard_map/concatenate | solution.py:47
  89.9 9.1 %copy.26 = f32[60,128,256]{2,1,0:T(8,128)} copy(f32[60,128,256]{1,2,0:T(8,128)} %pad_maximum_fusion) | data formatting | bytes 15728640 | tf_op jit(solution)/shard_map/concatenate | solution.py:47
  99.0 2.5 %broadcast_in_dim.26 = f32[33,128,256]{2,1,0:T(8,128)} broadcast(f32[]{:T(128)} %constant.8.clone.1), dimensions={} | broadcast | bytes 4325380 | tf_op jit(solution)/shard_map/broadcast_in_dim | solution.py:16
  101.5 19.1 %scatter_fusion = f32[33,128,256]{2,1,0:T(8,128)} fusion(f32[33,128,256]{2,1,0:T(8,128)} %broadcast_in_dim.26, s32[60]{0:T(128)S(1)} %fusion.29, f32[60,128,256]{2,1,0:T(8,128)} %copy.26), kind=kCustom, calls=%fused_computation.3 | custom fusion | flops 1966080 | bytes 23593200 | tf_op jit(solution)/shard_map/scatter-add | solution.py:16
  120.7 4.6 %slice.64 = f32[32,128,256]{2,1,0:T(8,128)} slice(f32[33,128,256]{2,1,0:T(8,128)} %scatter_fusion), slice={[0:32], [0:128], [0:256]} | slice | bytes 8388608 | tf_op jit(solution)/shard_map/slice | solution.py:16
  125.2 0.0 reduce-scatter.2.cloned.1.call-update
  125.3 59.8 %reduce-scatter.2.cloned.1.call-done = f32[256,256]{1,0:T(8,128)} async-done(((f32[4096,256]{1,0:T(8,128)}), f32[256,256]{1,0:T(8,128)}) %reduce-scatter.2.cloned.1.call-update) | async-done | bytes 262160 | tf_op jit(solution)/shard_map/reduce_scatter | solution.py:64
  185.1 1.6 convert_element_type.19
  (2 shorter events, 0.0 us)
Async XLA Ops:
  6.5 1.4 copy-start
  6.5 56.9 %all-gather.2.cloned.1.call-start = ((), (), s32[]{:S(2)}) async-start(), calls=%async_computation.1 | async-start | bytes 2228224 | tf_op jit(solution)/shard_map/all_gather | solution.py:30
  10.4 174.7 %reduce-scatter.2.cloned.1.call-start = ((), (), s32[]{:S(2)}) async-start(), calls=%async_computation.2 | async-start | bytes 4456448 | tf_op jit(solution)/shard_map/reduce_scatter | solution.py:64
  79.1 1.2 copy-start.3
  81.4 1.2 copy-start.4
  82.6 1.2 copy-start.1
  82.6 1.8 copy-start.2
Sparse Core Ops, SparseCore 0:
  10.5 52.8 all-gather.1
  125.4 59.6 reduce-scatter.1
where the time goes:
time: 197 us; the launch traced here: 194 us
  waiting for transfers between devices  110 us (56%)
  local copies, waits for them, and re-layouts  32.7 us (17%)
  other arithmetic  31.6 us (16%)
  between operations  13.5 us (7%)
  matrix products  5.66 us (3%)
    reduce_scatter x1, waiting for transfers between devices, body(): lax.psum_scatter(collect_rows(terms, targets, row_base, row_count), 'col'...  59.8 us
    all_gather x1, waiting for transfers between devices, body(): lax.all_gather(local.reshape(clusters * leaf_size, width), 'row', axis=0,...  50.2 us
    scatter-add x1, other arithmetic, collect_rows(): summed = jax.ops.segment_sum(terms, segment, num_segments=count + 1)[:count]  19.1 us
    concatenate x1, local copies, waits for them, and re-layouts, body(): jnp.concatenate([term + jnp.einsum('blr,brc->blc', far_u[:, 1], swap_part...  9.05 us
    unnamed x12, local copies, waits for them, and re-layouts  6.55 us
    slice x1, local copies, waits for them, and re-layouts, collect_rows(): summed = jax.ops.segment_sum(terms, segment, num_segments=count + 1)[:count]  4.58 us
    concatenate x1, other arithmetic, body(): jnp.concatenate([term + jnp.einsum('blr,brc->blc', far_u[:, 1], swap_part...  4.06 us
  transfers between devices with their start and end apart: 2, of which 2 were waited for; matrix products, arithmetic and copies ran while one was open for 1% of the time, Pallas kernels for 0%

commit v1 on v0

v1 whole, which is shorter than its diff:
```python
import jax
import jax.numpy as jnp
from jax import lax
from jax.experimental import pallas as pl
from jax.experimental.pallas import tpu as pltpu
from jax.sharding import PartitionSpec as P

LEAF = 128
COLS = 256
HALF = 128
RMAX = 64
NB = 32
NN = 28
NX = 4
NY = 4
NZ = 8
NCORE = 2
SLAB = 32
F32 = jnp.float32
BF16 = jnp.bfloat16
VMEM = pl.BlockSpec(memory_space=pltpu.VMEM)
SMEM = pl.BlockSpec(memory_space=pltpu.SMEM)


def row_pairs(dx, dy):
    return [
        (x * NY + y, (x + dx) % NX * NY + (y + dy) % NY) for x in range(NX) for y in range(NY)
    ]


def along_x(step, value):
    return lax.ppermute(value, "row", row_pairs(step, 0))


def along_y(step, value):
    return lax.ppermute(value, "row", row_pairs(0, step))


def swap_parts(values):
    return jnp.concatenate([-values[:, HALF:], values[:, :HALF]], axis=1)


def order_kernel(perm_ref, x_ref, even_ref, odd_ref):
    source = lax.broadcasted_iota(jnp.int32, (LEAF, LEAF), 0)
    for k, out in enumerate((even_ref, odd_ref)):
        chosen = (source == perm_ref[k : k + 1, :]).astype(F32).astype(BF16)
        out[...] = lax.dot_general(
            chosen,
            x_ref[k * LEAF : (k + 1) * LEAF, :],
            (((0,), (0,)), ((), ())),
            preferred_element_type=F32,
        ).astype(BF16)


def order(perm, incident):
    shape = jax.ShapeDtypeStruct((LEAF, COLS), BF16)
    return pl.pallas_call(
        order_kernel,
        out_shape=(shape, shape),
        in_specs=[VMEM, VMEM],
        out_specs=(VMEM, VMEM),
    )(perm, incident)


def prepare_kernel(rank_ref, u_ref, v_ref, u_out, v_out):
    line = lax.broadcasted_iota(jnp.int32, (RMAX, LEAF), 0)

    def step(b, carry):
        keep = line < rank_ref[b]
        for k in range(2):
            v = v_ref[b, k]
            v_out[b, :, k * LEAF : (k + 1) * LEAF] = jnp.where(keep, v.astype(F32), 0.0).astype(BF16)
        u_out[b] = jnp.concatenate([u_ref[b, 0], u_ref[b, 1]], axis=0).T
        return carry

    lax.fori_loop(0, NB, step, 0, unroll=4)


def prepare(rank, u, v):
    return pl.pallas_call(
        prepare_kernel,
        out_shape=(
            jax.ShapeDtypeStruct((NB, LEAF, 2 * RMAX), BF16),
            jax.ShapeDtypeStruct((NB, RMAX, 2 * LEAF), BF16),
        ),
        in_specs=[SMEM, VMEM, VMEM],
        out_specs=(VMEM, VMEM),
        cost_estimate=pl.CostEstimate(flops=0, bytes_accessed=8 << 20, transcendentals=0),
    )(rank, u, v)


def block_kernel(
    place_ref, far_rows, far_cols, near_rows, near_cols, *refs
):
    pieces = refs[:8]
    u_ref, v_ref, near_ref, other_ref, own_ref, trial, total = refs[8:]
    my_x, my_y, my_core = place_ref[0], place_ref[1], place_ref[2]

    def gray(d):
        return d ^ (d >> 1)

    def slot_of(cluster):
        k = cluster & (SLAB - 1)
        r = k >> 1
        dx = gray((my_x - (r >> 2)) & 3)
        dy = gray((my_y - (r & 3)) & 3)
        return jnp.where((k & 1) == 0, dy * 4 + dx, 16 + dx * 4 + dy)

    for p, piece in enumerate(pieces):
        for q in range(4):
            x = piece[q * LEAF : (q + 1) * LEAF, :]
            trial[p * 4 + q, :LEAF, :] = x
            trial[p * 4 + q, LEAF:, :] = swap_parts(x)
    total[...] = jnp.zeros_like(total)

    def add(row, term):
        total[row & (SLAB - 1)] += term

    def far_step(b, carry):
        x = trial[slot_of(far_cols[b])]
        coeff = jnp.dot(v_ref[b], x, preferred_element_type=F32).astype(BF16)
        both = jnp.concatenate([coeff, swap_parts(coeff)], axis=0)
        add(far_rows[b], jnp.dot(u_ref[b], both, preferred_element_type=F32))
        return carry

    def near_step(n, carry):
        x = trial[slot_of(near_cols[n])]
        block = jnp.concatenate([near_ref[n, 0], near_ref[n, 1]], axis=1)
        add(near_rows[n], jnp.dot(block, x, preferred_element_type=F32))
        return carry

    lax.fori_loop(0, NB, far_step, 0, unroll=4)
    lax.fori_loop(0, NN, near_step, 0, unroll=4)

    for z in range(NZ):
        for k in range(2):
            rows = slice((z * 2 + k) * LEAF, (z * 2 + k + 1) * LEAF)
            other_ref[rows, :] = total[z * 4 + (1 - my_core) * 2 + k].astype(BF16)
            own_ref[rows, :] = total[z * 4 + my_core * 2 + k]


def blocks(place, far_rows, far_cols, near_rows, near_cols, pieces, u, v, near):
    rows = NZ * 2 * LEAF
    return pl.pallas_call(
        block_kernel,
        out_shape=(
            jax.ShapeDtypeStruct((rows, COLS), BF16),
            jax.ShapeDtypeStruct((rows, COLS), F32),
        ),
        in_specs=[SMEM] * 5 + [VMEM] * 11,
        out_specs=(VMEM, VMEM),
        scratch_shapes=[
            pltpu.VMEM((SLAB, 2 * LEAF, COLS), BF16),
            pltpu.VMEM((SLAB, LEAF, COLS), F32),
        ],
        compiler_params=pltpu.CompilerParams(vmem_limit_bytes=40 << 20),
    )(place, far_rows, far_cols, near_rows, near_cols, *pieces, u, v, near)


def body(
    incident, perm, far_u, far_v, far_rank, far_rows, far_cols, near_block, near_rows, near_cols
):
    row, col = lax.axis_index("row"), lax.axis_index("col")
    place = jnp.stack([row // NY, row % NY, col % NCORE]).astype(jnp.int32)
    even, odd = order(perm, incident)
    u, v = prepare(far_rank, jnp.swapaxes(far_u, 2, 3), jnp.swapaxes(far_v, 2, 3))
    even_x = jnp.concatenate([even] + [along_x(s, even) for s in (1, -1, 2)], axis=0)
    odd_y = jnp.concatenate([odd] + [along_y(s, odd) for s in (1, -1, 2)], axis=0)
    pieces = [even_x] + [along_y(s, even_x) for s in (1, -1, 2)]
    pieces += [odd_y] + [along_x(s, odd_y) for s in (1, -1, 2)]
    other, own = blocks(
        place, far_rows, far_cols, near_rows, near_cols, pieces, u, v, near_block
    )
    swapped = lax.ppermute(other, "col", [(d, d ^ 1) for d in range(NZ * NCORE)])
    chip = (own + swapped.astype(F32)).astype(BF16)
    groups = [[z * NCORE + c for z in range(NZ)] for c in range(NCORE)]
    parts = lax.all_to_all(
        chip.reshape(NZ, 2 * LEAF, COLS), "col", 0, 0, tiled=True, axis_index_groups=groups
    )
    return jnp.sum(parts.astype(F32), axis=0).astype(BF16)


def solution(mesh):
    placed = (
        P(("col", "row"), None),
        P(("col", "row"), None),
        P(("row", "col"), None, None, None),
        P(("row", "col"), None, None, None),
        P(("row", "col")),
        P(("row", "col")),
        P(("row", "col")),
        P(("row", "col"), None, None, None),
        P(("row", "col")),
        P(("row", "col")),
    )
    return jax.shard_map(
        body, mesh=mesh, in_specs=placed, out_specs=P(("row", "col"), None), check_vma=False
    )
```

time: 197 us -> 91.7 us (0.47); the launches traced: 194 us -> 91.4 us
  waiting for transfers between devices: 110 us -> 15.9 us
  blocking collectives: 0 us -> 35.9 us
  other arithmetic: 31.6 us -> 1.15 us
  local copies, waits for them, and re-layouts: 32.7 us -> 4.19 us
  starting transfers between devices: 0.04 us -> 18.2 us
  Pallas kernels: 0 us -> 15.9 us
  between operations: 13.5 us -> 0.13 us
  matrix products: 5.66 us -> 0 us
    reduce_scatter x1 -> x0, waiting for transfers between devices: 59.8 us -> none  [body(): lax.psum_scatter(collect_rows(terms, targets, row_base, row_count), 'col'...]
    all_gather x1 -> x0, waiting for transfers between devices: 50.2 us -> none  [body(): lax.all_gather(local.reshape(clusters * leaf_size, width), 'row', axis=0,...]
    all_to_all x0 -> x1, blocking collectives: none -> 35.9 us  [body(): lax.all_to_all(chip.reshape(NZ, 2 * LEAF, COLS), 'col', 0, 0, tiled=True,...]
    scatter-add x1 -> x0, other arithmetic: 19.1 us -> none  [collect_rows(): summed = jax.ops.segment_sum(terms, segment, num_segments=count + 1)[:count]]
    ppermute x0 -> x13, starting transfers between devices: none -> 18.2 us  [the longest x6 7.83 us: along_x(): return lax.ppermute(value, 'row', row_pairs(step, 0))]
    pallas_call x0 -> x3, Pallas kernels: none -> 15.9 us  [the longest x1 10.4 us: blocks(): pl.pallas_call(block_kernel, out_shape=(jax.ShapeDtypeStruct((rows, COLS)...]
    ppermute x0 -> x13, waiting for transfers between devices: none -> 15.9 us  [the longest x6 10.1 us: along_y(): return lax.ppermute(value, 'row', row_pairs(0, step))]
    concatenate x1 -> x2, local copies, waits for them, and re-layouts: 9.05 us -> 0.01 us  [the longest x1 0.01 us: body(): jnp.concatenate([odd] + [along_y(s, odd) for s in (1, -1, 2)], axis=0)]
  transfers between devices with their start and end apart: 2 -> 13, of which waited for: 2 -> 7; matrix products, arithmetic and copies ran while one was open for 1% -> 2% of each run, Pallas kernels for 0% -> 4%
where the time goes in v1:
time: 91.7 us; the launch traced here: 91.4 us
  blocking collectives  35.9 us (39%)
  starting transfers between devices  18.2 us (20%)
  Pallas kernels  15.9 us (17%)
  waiting for transfers between devices  15.9 us (17%)
  local copies, waits for them, and re-layouts  4.19 us (5%)
  other arithmetic  1.15 us (1%)
    all_to_all x1, blocking collectives, body(): lax.all_to_all(chip.reshape(NZ, 2 * LEAF, COLS), 'col', 0, 0, tiled=True,...  35.9 us
    pallas_call x1, Pallas kernels, blocks(): pl.pallas_call(block_kernel, out_shape=(jax.ShapeDtypeStruct((rows, COLS)...  10.4 us
    ppermute x6, waiting for transfers between devices, along_y(): return lax.ppermute(value, 'row', row_pairs(0, step))  10.1 us
    ppermute x6, starting transfers between devices, along_x(): return lax.ppermute(value, 'row', row_pairs(step, 0))  7.83 us
    ppermute x6, starting transfers between devices, along_y(): return lax.ppermute(value, 'row', row_pairs(0, step))  5.58 us
    ppermute x1, starting transfers between devices, body(): lax.ppermute(other, 'col', [(d, d ^ 1) for d in range(NZ * NCORE)])  4.8 us
    unnamed x20, local copies, waits for them, and re-layouts  4.17 us
    pallas_call x1, Pallas kernels, prepare(): pl.pallas_call(prepare_kernel, out_shape=(jax.ShapeDtypeStruct((NB, LEAF,...  3.55 us
  transfers between devices with their start and end apart: 13, of which 7 were waited for; matrix products, arithmetic and copies ran while one was open for 2% of the time, Pallas kernels for 4%

profile of v1, /device:TPU:1, one launch (start us, length us, event | category | flops | bytes accessed | tf_op | source)
XLA Modules:
  0.0 91.4 jit_solution(7891132407480086563)
XLA Ops:
  0.0 0.0 copy-start.6
  0.0 0.0 copy-start.5
  0.0 0.0 copy-start
  0.0 0.0 copy-start.4
  0.0 0.0 copy-start.3
  0.0 1.9 %shard_map.100 = (bf16[128,256]{1,0:T(8,128)(2,1)}, bf16[128,256]{1,0:T(8,128)(2,1)}) custom-call(s32[2,128]{1,0:T(2,128)} %perm_ref.1, bf16[256,256]{1,0:T(8,128)(2,1)} %x_ref.1), custom_call_target="tpu_custom_call" | custom-call | tf_op jit(solution)/shard_map/pallas_call | solution.py:57
  2.0 3.6 %collective-permute-start.2 = (bf16[128,256]{1,0:T(8,128)(2,1)}, bf16[128,256]{1,0:T(8,128)(2,1)S(1)}, u32[]{:S(2)}, u32[]{:S(2)}) collective-permute-start(bf16[128,256]{1,0:T(8,128)(2,1)} %get-tuple-element.11), channel_id=1, source_target_pairs={{0,128},{16,144},{32,160},{48,176},{64,192},{80,208},{96,224},{112... | collective-permute-start | bytes 196616 | tf_op jit(solution)/shard_map/ppermute | solution.py:32
  5.5 0.9 collective-permute-start.1
  6.4 0.6 collective-permute-start
  7.0 2.9 %collective-permute-start.8 = (bf16[128,256]{1,0:T(8,128)(2,1)}, bf16[128,256]{1,0:T(8,128)(2,1)S(1)}, u32[]{:S(2)}, u32[]{:S(2)}) collective-permute-start(bf16[128,256]{1,0:T(8,128)(2,1)} %get-tuple-element.12), channel_id=1, source_target_pairs={{0,32},{16,48},{32,0},{48,16},{64,96},{80,112},{96,64},{112,80},{1... | collective-permute-start | bytes 196616 | tf_op jit(solution)/shard_map/ppermute | solution.py:36
  9.9 0.4 collective-permute-start.6
  10.3 0.8 constant_dynamic-update-slice_fusion.3
  11.2 0.8 constant_dynamic-update-slice_fusion.7
  12.0 2.8 %collective-permute-done.6 = bf16[128,256]{1,0:T(8,128)(2,1)S(1)} collective-permute-done((bf16[128,256]{1,0:T(8,128)(2,1)}, bf16[128,256]{1,0:T(8,128)(2,1)S(1)}, u32[]{:S(2)}, u32[]{:S(2)}) %collective-permute-start.6) | collective-permute-done | bytes 65568 | tf_op jit(solution)/shard_map/ppermute | solution.py:36
  14.8 0.0 collective-permute-start.7
  14.8 3.3 %collective-permute-done.7 = bf16[128,256]{1,0:T(8,128)(2,1)S(1)} collective-permute-done((bf16[128,256]{1,0:T(8,128)(2,1)}, bf16[128,256]{1,0:T(8,128)(2,1)S(1)}, u32[]{:S(2)}, u32[]{:S(2)}) %collective-permute-start.7) | collective-permute-done | bytes 65568 | tf_op jit(solution)/shard_map/ppermute | solution.py:36
  18.2 0.0 collective-permute-done.8
  18.2 0.7 collective-permute-start.11
  18.8 2.1 %collective-permute-start.10 = (bf16[512,256]{1,0:T(8,128)(2,1)S(1)}, bf16[512,256]{1,0:T(8,128)(2,1)S(1)}, u32[]{:S(2)}, u32[]{:S(2)}) collective-permute-start(bf16[512,256]{1,0:T(8,128)(2,1)S(1)} %constant_dynamic-update-slice_fusion.4.refs_4_), channel_id=1, source_target_pairs={{0,192},{16,208},{32,224},{48,240},{64,0},{80,16},{96,32},{112,48}... | collective-permute-start | bytes 786440 | tf_op jit(solution)/shard_map/ppermute | solution.py:32
  21.0 0.0 collective-permute-done
  21.0 0.0 collective-permute-start.9
  21.0 0.0 collective-permute-done.1
  21.0 0.0 collective-permute-done.2
  21.0 0.1 collective-permute-start.5
  21.1 2.2 %collective-permute-start.4 = (bf16[512,256]{1,0:T(8,128)(2,1)S(1)}, bf16[512,256]{1,0:T(8,128)(2,1)}, u32[]{:S(2)}, u32[]{:S(2)}) collective-permute-start(bf16[512,256]{1,0:T(8,128)(2,1)S(1)} %constant_dynamic-update-slice_fusion.refs_0_), channel_id=1, source_target_pairs={{0,48},{16,0},{32,16},{48,32},{64,112},{80,64},{96,80},{112,96},{1... | collective-permute-start | bytes 786440 | tf_op jit(solution)/shard_map/ppermute | solution.py:36
  23.3 1.7 %collective-permute-done.11.refs_7_ = bf16[512,256]{1,0:T(8,128)(2,1)S(1)} collective-permute-done((bf16[512,256]{1,0:T(8,128)(2,1)S(1)}, bf16[512,256]{1,0:T(8,128)(2,1)S(1)}, u32[]{:S(2)}, u32[]{:S(2)}) %collective-permute-start.11) | collective-permute-done | bytes 262176 | tf_op jit(solution)/shard_map/ppermute | solution.py:32
  25.0 0.0 collective-permute-start.3
  25.0 3.5 %shard_map.101 = (bf16[32,128,128]{2,1,0:T(8,128)(2,1)}, bf16[32,64,256]{2,1,0:T(8,128)(2,1)}) custom-call(s32[32]{0:T(128)} %rank_ref.1, bf16[32,2,64,128]{3,2,1,0:T(8,128)(2,1)} %bitcast.7, bf16[32,2,64,128]{3,2,1,0:T(8,128)(2,1)} %bitcast.8), custom_call_target="tpu_custom_call" | custom-call | bytes 8388608 | tf_op jit(solution)/shard_map/pallas_call | solution.py:80
  28.6 0.1 pad_add_fusion.place_ref
  28.7 1.8 %collective-permute-done.10.refs_6_ = bf16[512,256]{1,0:T(8,128)(2,1)S(1)} collective-permute-done((bf16[512,256]{1,0:T(8,128)(2,1)S(1)}, bf16[512,256]{1,0:T(8,128)(2,1)S(1)}, u32[]{:S(2)}, u32[]{:S(2)}) %collective-permute-start.10) | collective-permute-done | bytes 262176 | tf_op jit(solution)/shard_map/ppermute | solution.py:32
  30.5 0.0 collective-permute-done.9.refs_5_
  30.5 0.0 collective-permute-done.5.refs_3_
  30.5 1.6 %collective-permute-done.4.refs_2_ = bf16[512,256]{1,0:T(8,128)(2,1)} collective-permute-done((bf16[512,256]{1,0:T(8,128)(2,1)S(1)}, bf16[512,256]{1,0:T(8,128)(2,1)}, u32[]{:S(2)}, u32[]{:S(2)}) %collective-permute-start.4) | collective-permute-done | bytes 262176 | tf_op jit(solution)/shard_map/ppermute | solution.py:36
  32.0 2.4 %collective-permute-done.3.refs_1_ = bf16[512,256]{1,0:T(8,128)(2,1)} collective-permute-done((bf16[512,256]{1,0:T(8,128)(2,1)S(1)}, bf16[512,256]{1,0:T(8,128)(2,1)}, u32[]{:S(2)}, u32[]{:S(2)}) %collective-permute-start.3) | collective-permute-done | bytes 262176 | tf_op jit(solution)/shard_map/ppermute | solution.py:36
  34.4 0.0 copy-done.6
  34.4 0.0 copy-done.5
  34.4 0.0 copy-done
  34.4 0.0 copy-done.4
  34.4 0.0 copy-done.3
  34.4 0.0 copy-start.1
  34.4 1.2 %copy-done.1 = bf16[32,128,128]{2,1,0:T(8,128)(2,1)S(1)} copy-done((bf16[32,128,128]{2,1,0:T(8,128)(2,1)S(1)}, bf16[32,128,128]{2,1,0:T(8,128)(2,1)}, u32[]{:S(2)}) %copy-start.1) | copy-done | bytes 1048600
  35.6 1.2 %copy-done.2 = bf16[32,64,256]{2,1,0:T(8,128)(2,1)S(1)} copy-done((bf16[32,64,256]{2,1,0:T(8,128)(2,1)S(1)}, bf16[32,64,256]{2,1,0:T(8,128)(2,1)}, u32[]{:S(2)}) %copy-start.2) | copy-done | bytes 1048600
  36.9 10.4 %shard_map.102 = (bf16[2048,256]{1,0:T(8,128)(2,1)S(1)}, f32[2048,256]{1,0:T(8,128)S(1)}) custom-call(s32[3]{0:T(128)S(1)} %pad_add_fusion.place_ref, s32[32]{0:T(128)S(1)} %copy-done.3, s32[32]{0:T(128)S(1)} %copy-done.4, s32[28]{0:T(128)S(1)} %copy-done.5, s32[28]{0:T(128)S(1)} %copy-done.6, ...), custom_call_target="tpu_custom_call" | custom-call | tf_op jit(solution)/shard_map/pallas_call | solution.py:144
  47.3 4.8 %collective-permute-start.12 = (bf16[2048,256]{1,0:T(8,128)(2,1)S(1)}, bf16[2048,256]{1,0:T(8,128)(2,1)S(1)}, u32[]{:S(2)}, u32[]{:S(2)}) collective-permute-start(bf16[2048,256]{1,0:T(8,128)(2,1)S(1)} %get-tuple-element.16), channel_id=1, source_target_pairs={{0,1},{1,0},{2,3},{3,2},{4,5},{5,4},{6,7},{7,6},{8,9},{9,8},{10,11... | collective-permute-start | bytes 3145736 | tf_op jit(solution)/shard_map/ppermute | solution.py:174
  52.1 2.3 %collective-permute-done.12 = bf16[2048,256]{1,0:T(8,128)(2,1)S(1)} collective-permute-done((bf16[2048,256]{1,0:T(8,128)(2,1)S(1)}, bf16[2048,256]{1,0:T(8,128)(2,1)S(1)}, u32[]{:S(2)}, u32[]{:S(2)}) %collective-permute-start.12) | collective-permute-done | bytes 1048608 | tf_op jit(solution)/shard_map/ppermute | solution.py:174
  54.4 0.3 add_convert_fusion
  54.7 35.9 %all_to_all.5 = bf16[8,256,256]{2,1,0:T(8,128)(2,1)S(1)} all-to-all(bf16[8,256,256]{2,1,0:T(8,128)(2,1)S(1)} %bitcast.6), channel_id=1, replica_groups={{0,2,4,6,8,10,12,14},{1,3,5,7,9,11,13,15},{16,18,20,22,24,26,28,30},{17..., dimensions={0} | all-to-all | bytes 2097152 | tf_op jit(solution)/shard_map/all_to_all | solution.py:177
  90.6 0.8 reduce_sum.12
  (7 shorter events, 0.0 us)
Async XLA Ops:
  0.0 34.4 %copy-start.6 = (s32[28]{0:T(128)S(1)}, s32[28]{0:T(128)}, u32[]{:S(2)}) copy-start(s32[28]{0:T(128)} %near_cols.1) | copy-start | bytes 340
  0.0 34.4 %copy-start.5 = (s32[28]{0:T(128)S(1)}, s32[28]{0:T(128)}, u32[]{:S(2)}) copy-start(s32[28]{0:T(128)} %near_rows.1) | copy-start | bytes 340
  0.0 34.4 %copy-start = (bf16[28,2,128,128]{3,2,1,0:T(8,128)(2,1)S(1)}, bf16[28,2,128,128]{3,2,1,0:T(8,128)(2,1)}, u32[]{:S(2)}) copy-start(bf16[28,2,128,128]{3,2,1,0:T(8,128)(2,1)} %refs_10_.1) | copy-start | bytes 5505028
  0.0 34.4 %copy-start.4 = (s32[32]{0:T(128)S(1)}, s32[32]{0:T(128)}, u32[]{:S(2)}) copy-start(s32[32]{0:T(128)} %far_cols.1) | copy-start | bytes 388
  0.0 34.4 %copy-start.3 = (s32[32]{0:T(128)S(1)}, s32[32]{0:T(128)}, u32[]{:S(2)}) copy-start(s32[32]{0:T(128)} %far_rows.1) | copy-start | bytes 388
  2.0 19.1 %collective-permute-start.2 = (bf16[128,256]{1,0:T(8,128)(2,1)}, bf16[128,256]{1,0:T(8,128)(2,1)S(1)}, u32[]{:S(2)}, u32[]{:S(2)}) collective-permute-start(bf16[128,256]{1,0:T(8,128)(2,1)} %get-tuple-element.11), channel_id=1, source_target_pairs={{0,128},{16,144},{32,160},{48,176},{64,192},{80,208},{96,224},{112... | collective-permute-start | bytes 196616 | tf_op jit(solution)/shard_map/ppermute | solution.py:32
  5.5 15.5 %collective-permute-start.1 = (bf16[128,256]{1,0:T(8,128)(2,1)}, bf16[128,256]{1,0:T(8,128)(2,1)S(1)}, u32[]{:S(2)}, u32[]{:S(2)}) collective-permute-start(bf16[128,256]{1,0:T(8,128)(2,1)} %get-tuple-element.11), channel_id=1, source_target_pairs={{0,192},{16,208},{32,224},{48,240},{64,0},{80,16},{96,32},{112,48}... | collective-permute-start | bytes 196616 | tf_op jit(solution)/shard_map/ppermute | solution.py:32
  6.4 14.6 %collective-permute-start = (bf16[128,256]{1,0:T(8,128)(2,1)}, bf16[128,256]{1,0:T(8,128)(2,1)S(1)}, u32[]{:S(2)}, u32[]{:S(2)}) collective-permute-start(bf16[128,256]{1,0:T(8,128)(2,1)} %get-tuple-element.11), channel_id=1, source_target_pairs={{0,64},{16,80},{32,96},{48,112},{64,128},{80,144},{96,160},{112,17... | collective-permute-start | bytes 196616 | tf_op jit(solution)/shard_map/ppermute | solution.py:32
  7.0 11.2 %collective-permute-start.8 = (bf16[128,256]{1,0:T(8,128)(2,1)}, bf16[128,256]{1,0:T(8,128)(2,1)S(1)}, u32[]{:S(2)}, u32[]{:S(2)}) collective-permute-start(bf16[128,256]{1,0:T(8,128)(2,1)} %get-tuple-element.12), channel_id=1, source_target_pairs={{0,32},{16,48},{32,0},{48,16},{64,96},{80,112},{96,64},{112,80},{1... | collective-permute-start | bytes 196616 | tf_op jit(solution)/shard_map/ppermute | solution.py:36
  9.9 4.9 %collective-permute-start.6 = (bf16[128,256]{1,0:T(8,128)(2,1)}, bf16[128,256]{1,0:T(8,128)(2,1)S(1)}, u32[]{:S(2)}, u32[]{:S(2)}) collective-permute-start(bf16[128,256]{1,0:T(8,128)(2,1)} %get-tuple-element.12), channel_id=1, source_target_pairs={{0,16},{16,32},{32,48},{48,0},{64,80},{80,96},{96,112},{112,64},{1... | collective-permute-start | bytes 196616 | tf_op jit(solution)/shard_map/ppermute | solution.py:36
  14.8 3.3 %collective-permute-start.7 = (bf16[128,256]{1,0:T(8,128)(2,1)}, bf16[128,256]{1,0:T(8,128)(2,1)S(1)}, u32[]{:S(2)}, u32[]{:S(2)}) collective-permute-start(bf16[128,256]{1,0:T(8,128)(2,1)} %get-tuple-element.12), channel_id=1, source_target_pairs={{0,48},{16,0},{32,16},{48,32},{64,112},{80,64},{96,80},{112,96},{1... | collective-permute-start | bytes 196616 | tf_op jit(solution)/shard_map/ppermute | solution.py:36
  18.2 6.9 %collective-permute-start.11 = (bf16[512,256]{1,0:T(8,128)(2,1)S(1)}, bf16[512,256]{1,0:T(8,128)(2,1)S(1)}, u32[]{:S(2)}, u32[]{:S(2)}) collective-permute-start(bf16[512,256]{1,0:T(8,128)(2,1)S(1)} %constant_dynamic-update-slice_fusion.4.refs_4_), channel_id=1, source_target_pairs={{0,128},{16,144},{32,160},{48,176},{64,192},{80,208},{96,224},{112... | collective-permute-start | bytes 786440 | tf_op jit(solution)/shard_map/ppermute | solution.py:32
  18.8 11.6 %collective-permute-start.10 = (bf16[512,256]{1,0:T(8,128)(2,1)S(1)}, bf16[512,256]{1,0:T(8,128)(2,1)S(1)}, u32[]{:S(2)}, u32[]{:S(2)}) collective-permute-start(bf16[512,256]{1,0:T(8,128)(2,1)S(1)} %constant_dynamic-update-slice_fusion.4.refs_4_), channel_id=1, source_target_pairs={{0,192},{16,208},{32,224},{48,240},{64,0},{80,16},{96,32},{112,48}... | collective-permute-start | bytes 786440 | tf_op jit(solution)/shard_map/ppermute | solution.py:32
  21.0 9.5 %collective-permute-start.9 = (bf16[512,256]{1,0:T(8,128)(2,1)S(1)}, bf16[512,256]{1,0:T(8,128)(2,1)S(1)}, u32[]{:S(2)}, u32[]{:S(2)}) collective-permute-start(bf16[512,256]{1,0:T(8,128)(2,1)S(1)} %constant_dynamic-update-slice_fusion.4.refs_4_), channel_id=1, source_target_pairs={{0,64},{16,80},{32,96},{48,112},{64,128},{80,144},{96,160},{112,17... | collective-permute-start | bytes 786440 | tf_op jit(solution)/shard_map/ppermute | solution.py:32
  21.0 9.4 %collective-permute-start.5 = (bf16[512,256]{1,0:T(8,128)(2,1)S(1)}, bf16[512,256]{1,0:T(8,128)(2,1)S(1)}, u32[]{:S(2)}, u32[]{:S(2)}) collective-permute-start(bf16[512,256]{1,0:T(8,128)(2,1)S(1)} %constant_dynamic-update-slice_fusion.refs_0_), channel_id=1, source_target_pairs={{0,32},{16,48},{32,0},{48,16},{64,96},{80,112},{96,64},{112,80},{1... | collective-permute-start | bytes 786440 | tf_op jit(solution)/shard_map/ppermute | solution.py:36
  21.1 10.9 %collective-permute-start.4 = (bf16[512,256]{1,0:T(8,128)(2,1)S(1)}, bf16[512,256]{1,0:T(8,128)(2,1)}, u32[]{:S(2)}, u32[]{:S(2)}) collective-permute-start(bf16[512,256]{1,0:T(8,128)(2,1)S(1)} %constant_dynamic-update-slice_fusion.refs_0_), channel_id=1, source_target_pairs={{0,48},{16,0},{32,16},{48,32},{64,112},{80,64},{96,80},{112,96},{1... | collective-permute-start | bytes 786440 | tf_op jit(solution)/shard_map/ppermute | solution.py:36
  25.0 9.3 %collective-permute-start.3 = (bf16[512,256]{1,0:T(8,128)(2,1)S(1)}, bf16[512,256]{1,0:T(8,128)(2,1)}, u32[]{:S(2)}, u32[]{:S(2)}) collective-permute-start(bf16[512,256]{1,0:T(8,128)(2,1)S(1)} %constant_dynamic-update-slice_fusion.refs_0_), channel_id=1, source_target_pairs={{0,16},{16,32},{32,48},{48,0},{64,80},{80,96},{96,112},{112,64},{1... | collective-permute-start | bytes 786440 | tf_op jit(solution)/shard_map/ppermute | solution.py:36
  34.4 1.2 %copy-start.1 = (bf16[32,128,128]{2,1,0:T(8,128)(2,1)S(1)}, bf16[32,128,128]{2,1,0:T(8,128)(2,1)}, u32[]{:S(2)}) copy-start(bf16[32,128,128]{2,1,0:T(8,128)(2,1)} %get-tuple-element.13.refs_8_) | copy-start | bytes 3145732
  35.6 1.2 %copy-start.2 = (bf16[32,64,256]{2,1,0:T(8,128)(2,1)S(1)}, bf16[32,64,256]{2,1,0:T(8,128)(2,1)}, u32[]{:S(2)}) copy-start(bf16[32,64,256]{2,1,0:T(8,128)(2,1)} %get-tuple-element.14.refs_9_) | copy-start | bytes 3145732
  47.3 7.1 %collective-permute-start.12 = (bf16[2048,256]{1,0:T(8,128)(2,1)S(1)}, bf16[2048,256]{1,0:T(8,128)(2,1)S(1)}, u32[]{:S(2)}, u32[]{:S(2)}) collective-permute-start(bf16[2048,256]{1,0:T(8,128)(2,1)S(1)} %get-tuple-element.16), channel_id=1, source_target_pairs={{0,1},{1,0},{2,3},{3,2},{4,5},{5,4},{6,7},{7,6},{8,9},{9,8},{10,11... | collective-permute-start | bytes 3145736 | tf_op jit(solution)/shard_map/ppermute | solution.py:174

commit v2 on v1

v2 whole, which is shorter than its diff:
```python
import jax
import jax.numpy as jnp
from jax import lax
from jax.experimental import pallas as pl
from jax.experimental.pallas import tpu as pltpu
from jax.sharding import PartitionSpec as P

LEAF = 128
COLS = 256
HALF = 128
RMAX = 64
NB = 32
NN = 28
NX = 4
NY = 4
NZ = 8
NCORE = 2
SLAB = 32
WAYS = 4
STEPS = (4, 7, 1, 6, 2, 5, 3, 0)
F32 = jnp.float32
BF16 = jnp.bfloat16
VMEM = pl.BlockSpec(memory_space=pltpu.VMEM)
SMEM = pl.BlockSpec(memory_space=pltpu.SMEM)
ANY = pl.BlockSpec(memory_space=pl.ANY)


def limit(mib):
    return pltpu.CompilerParams(vmem_limit_bytes=mib << 20)


def position():
    row, col = lax.axis_index("row"), lax.axis_index("col")
    return row // NY, row % NY, col // NCORE, col % NCORE


def hop(turn, step, value):
    pairs = []
    for d in range(NX * NY * NZ * NCORE):
        row, col = divmod(d, NZ * NCORE)
        x, y = divmod(row, NY)
        if (col + turn) % NCORE == 0:
            x = (x + step) % NX
        else:
            y = (y + step) % NY
        pairs.append((d, (x * NY + y) * NZ * NCORE + col))
    return lax.ppermute(value, ("row", "col"), pairs)


def along_z(step, value):
    pairs = [
        (z * NCORE + c, (z + step) % NZ * NCORE + c) for z in range(NZ) for c in range(NCORE)
    ]
    return lax.ppermute(value, "col", pairs)


def other_core(value):
    return lax.ppermute(value, "col", [(d, d ^ 1) for d in range(NZ * NCORE)])


def after(value, earlier):
    return lax.optimization_barrier((value, earlier))[0]


def swap_parts(values):
    return jnp.concatenate([-values[:, HALF:], values[:, :HALF]], axis=1)


def order_kernel(perm_hbm, x_hbm, out_ref, perm_ref, x_ref, perm_sem, x_sem):
    x_copy = pltpu.make_async_copy(x_hbm, x_ref, x_sem)
    perm_copy = pltpu.make_async_copy(perm_hbm, perm_ref, perm_sem)
    x_copy.start()
    perm_copy.start()
    source = lax.broadcasted_iota(jnp.int32, (LEAF, LEAF), 0)
    perm_copy.wait()
    x_copy.wait()
    for k in range(2):
        rows = slice(k * LEAF, (k + 1) * LEAF)
        chosen = (source == perm_ref[k : k + 1, :]).astype(F32).astype(BF16)
        out_ref[rows, :] = lax.dot_general(
            chosen, x_ref[rows, :], (((0,), (0,)), ((), ())), preferred_element_type=F32
        ).astype(BF16)


def order(perm, incident):
    return pl.pallas_call(
        order_kernel,
        out_shape=pltpu.VMEM((2 * LEAF, COLS), BF16),
        in_specs=[ANY, ANY],
        out_specs=VMEM,
        scratch_shapes=[
            pltpu.VMEM((2, LEAF), jnp.int32),
            pltpu.VMEM((2 * LEAF, COLS), BF16),
            pltpu.SemaphoreType.DMA,
            pltpu.SemaphoreType.DMA,
        ],
    )(perm, incident)


def weave_kernel(*refs):
    for q in range(4):
        refs[4][q * 2 * LEAF : (q + 1) * 2 * LEAF, :] = refs[q][...]


def weave(parts):
    return pl.pallas_call(
        weave_kernel,
        out_shape=pltpu.VMEM((8 * LEAF, COLS), BF16),
        in_specs=[VMEM] * 4,
        out_specs=VMEM,
        compiler_params=limit(4),
    )(*parts)


def prepare_kernel(
    rank_ref, far_rows, far_cols, near_rows, near_cols, u_ref, v_ref, u_out, v_out, lists
):
    my_x, my_y, my_z, my_core = position()

    def gray(d):
        return d ^ (d >> 1)

    def entry(b, row, col):
        k = col & (SLAB - 1)
        r = k >> 1
        dx = gray((my_x - (r >> 2)) & 3)
        dy = gray((my_y - (r & 3)) & 3)
        slot = jnp.where(my_core == 0, dy * 4 + dx, dx * 4 + dy) * 2 + (k & 1)
        dz = (((row & (SLAB - 1)) >> 2) - my_z) & 7
        own = 1 - (((row >> 1) & 1) ^ my_core)
        target = ((0x13506427 >> (dz * 4)) & 15) * 4 + own * 2 + (row & 1)
        return b | (slot << 6) | (target << 11)

    def fill(count, rows, cols, base):
        def step(b, carry):
            lists[base + b] = entry(b, rows[b], cols[b])
            return carry

        lax.fori_loop(0, count, step, 0)

    fill(NB, far_rows, far_cols, 0)
    fill(NN, near_rows, near_cols, NB)

    line = lax.broadcasted_iota(jnp.int32, (RMAX, LEAF), 0)

    def step(b, carry):
        keep = line < rank_ref[b]
        for k in range(2):
            v = v_ref[b, k]
            v_out[b, :, k * LEAF : (k + 1) * LEAF] = jnp.where(keep, v.astype(F32), 0.0).astype(BF16)
        u_out[b] = jnp.concatenate([u_ref[b, 0], u_ref[b, 1]], axis=0).T
        return carry

    lax.fori_loop(0, NB, step, 0, unroll=4)


def prepare(rank, far_rows, far_cols, near_rows, near_cols, u, v):
    return pl.pallas_call(
        prepare_kernel,
        out_shape=(
            pltpu.VMEM((NB, LEAF, 2 * RMAX), BF16),
            pltpu.VMEM((NB, RMAX, 2 * LEAF), BF16),
            pltpu.SMEM((NB + NN,), jnp.int32),
        ),
        in_specs=[SMEM] * 5 + [VMEM] * 2,
        out_specs=(VMEM, VMEM, SMEM),
        compiler_params=limit(4),
        cost_estimate=pl.CostEstimate(flops=0, bytes_accessed=8 << 20, transcendentals=0),
    )(rank, far_rows, far_cols, near_rows, near_cols, u, v)


def block_kernel(lists, *refs):
    pieces = refs[:4]
    u_ref, v_ref, near_ref, other_ref, own_ref, trial, total = refs[4:]
    for p, piece in enumerate(pieces):
        for q in range(8):
            x = piece[q * LEAF : (q + 1) * LEAF, :]
            trial[p * 8 + q, :LEAF, :] = x
            trial[p * 8 + q, LEAF:, :] = swap_parts(x)
    total[...] = jnp.zeros_like(total)

    def entries(base, q):
        found = []
        for k in range(WAYS):
            e = lists[base + q * WAYS + k]
            found.append((e & 63, (e >> 6) & 31, e >> 11))
        return found

    def far_step(q, carry):
        found = entries(0, q)
        coeffs = [
            jnp.dot(v_ref[b], trial[slot], preferred_element_type=F32).astype(BF16)
            for b, slot, _ in found
        ]
        for coeff, (b, _, target) in zip(coeffs, found):
            both = jnp.concatenate([coeff, swap_parts(coeff)], axis=0)
            total[target] += jnp.dot(u_ref[b], both, preferred_element_type=F32)
        return carry

    def near_step(q, carry):
        for n, slot, target in entries(NB, q):
            block = jnp.concatenate([near_ref[n, 0], near_ref[n, 1]], axis=1)
            total[target] += jnp.dot(block, trial[slot], preferred_element_type=F32)
        return carry

    lax.fori_loop(0, NB // WAYS, far_step, 0)
    lax.fori_loop(0, NN // WAYS, near_step, 0)

    for j in range(NZ):
        for k in range(2):
            rows = slice((j * 2 + k) * LEAF, (j * 2 + k + 1) * LEAF)
            other_ref[rows, :] = total[j * 4 + k].astype(BF16)
            own_ref[rows, :] = total[j * 4 + 2 + k]


def blocks(lists, pieces, u, v, near):
    rows = NZ * 2 * LEAF
    return pl.pallas_call(
        block_kernel,
        out_shape=(
            pltpu.VMEM((rows, COLS), BF16),
            pltpu.VMEM((rows, COLS), F32),
        ),
        in_specs=[SMEM] + [VMEM] * 7,
        out_specs=(VMEM, VMEM),
        scratch_shapes=[
            pltpu.VMEM((SLAB, 2 * LEAF, COLS), BF16),
            pltpu.VMEM((NZ * 4, LEAF, COLS), F32),
        ],
        compiler_params=limit(12),
        cost_estimate=pl.CostEstimate(
            flops=1 << 30, bytes_accessed=16 << 20, transcendentals=0
        ),
    )(lists, *pieces, u, v, near)


def gather(mine):
    two, back, ahead = [hop(0, step, mine) for step in (2, -1, 1)]
    first = weave([mine, ahead, back, two])
    two, back, ahead = [hop(1, step, first) for step in (2, -1, 1)]
    return [first, ahead, back, two]


def body(
    incident, perm, far_u, far_v, far_rank, far_rows, far_cols, near_block, near_rows, near_cols
):
    mine = order(perm, incident)
    u, v, lists = prepare(
        far_rank,
        far_rows,
        far_cols,
        near_rows,
        near_cols,
        jnp.swapaxes(far_u, 2, 3),
        jnp.swapaxes(far_v, 2, 3),
    )
    pieces = gather(mine)
    other, own = blocks(lists, pieces, u, v, near_block)
    swapped = other_core(other)
    total, parts = None, []
    for j, step in enumerate(STEPS):
        rows = slice(j * 2 * LEAF, (j + 1) * 2 * LEAF)
        chip = own[rows] + swapped[rows].astype(F32)
        if step == 0:
            total = chip
        else:
            parts.append(along_z(step, chip.astype(BF16)))
    for part in parts:
        total = total + part.astype(F32)
    return total.astype(BF16)


def solution(mesh):
    placed = (
        P(("col", "row"), None),
        P(("col", "row"), None),
        P(("row", "col"), None, None, None),
        P(("row", "col"), None, None, None),
        P(("row", "col")),
        P(("row", "col")),
        P(("row", "col")),
        P(("row", "col"), None, None, None),
        P(("row", "col")),
        P(("row", "col")),
    )
    return jax.shard_map(
        body, mesh=mesh, in_specs=placed, out_specs=P(("row", "col"), None), check_vma=False
    )
```

time: 91.7 us -> 70.4 us (0.77)
  blocking collectives: 35.9 us -> 0 us
  starting transfers between devices: 18.2 us -> 28.9 us
  waiting for transfers between devices: 15.9 us -> 24.9 us
  Pallas kernels: 15.9 us -> 9.56 us
  local copies, waits for them, and re-layouts: 4.19 us -> 5.73 us
    all_to_all x1 -> x0, blocking collectives: 35.9 us -> none  [body(): lax.all_to_all(chip.reshape(NZ, 2 * LEAF, COLS), 'col', 0, 0, tiled=True,...]
    ppermute x13 -> x14, starting transfers between devices: 18.2 us -> 28.9 us  [the longest x7 15.8 us: along_z(): return lax.ppermute(value, 'col', pairs)]
    ppermute x13 -> x14, waiting for transfers between devices: 15.9 us -> 24.9 us  [the longest x7 15.1 us: along_z(): return lax.ppermute(value, 'col', pairs)]
    pallas_call x3 -> x4, Pallas kernels: 15.9 us -> 9.56 us  [the longest x1 5.76 us: blocks(): pl.pallas_call(block_kernel, out_shape=(pltpu.VMEM((rows, COLS), BF16), p...]
    unnamed x20 -> x16, local copies, waits for them, and re-layouts: 4.17 us -> 5.73 us
  transfers between devices with their start and end apart: 13 -> 14, of which waited for: 7 -> 10; matrix products, arithmetic and copies ran while one was open for 2% -> 0% of each run, Pallas kernels for 4% -> 4%
where the time goes in v2:
time: 70.4 us; the launch traced here: 70.1 us
  starting transfers between devices  28.9 us (41%)
  waiting for transfers between devices  24.9 us (35%)
  Pallas kernels  9.56 us (14%)
  local copies, waits for them, and re-layouts  5.73 us (8%)
  other arithmetic  1.04 us (1%)
    ppermute x7, starting transfers between devices, along_z(): return lax.ppermute(value, 'col', pairs)  15.8 us
    ppermute x7, waiting for transfers between devices, along_z(): return lax.ppermute(value, 'col', pairs)  15.1 us
    ppermute x6, starting transfers between devices, hop(): return lax.ppermute(value, ('row', 'col'), pairs)  9.59 us
    ppermute x6, waiting for transfers between devices, hop(): return lax.ppermute(value, ('row', 'col'), pairs)  7.46 us
    pallas_call x1, Pallas kernels, blocks(): pl.pallas_call(block_kernel, out_shape=(pltpu.VMEM((rows, COLS), BF16), p...  5.76 us
    unnamed x16, local copies, waits for them, and re-layouts  5.73 us
    ppermute x1, starting transfers between devices, other_core(): return lax.ppermute(value, 'col', [(d, d ^ 1) for d in range(NZ * NCORE)])  3.5 us
    pallas_call x1, Pallas kernels, prepare(): pl.pallas_call(prepare_kernel, out_shape=(pltpu.VMEM((NB, LEAF, 2 * RMAX)...  2.5 us
  transfers between devices with their start and end apart: 14, of which 10 were waited for; matrix products, arithmetic and copies ran while one was open for 0% of the time, Pallas kernels for 4%

profile of v2, /device:TPU:1, one launch (start us, length us, event | category | flops | bytes accessed | tf_op | source)
XLA Modules:
  0.0 70.1 jit_solution(1715782676240223874)
XLA Ops:
  0.0 0.0 copy-start
  0.0 1.3 %shard_map.101.refs_0_ = bf16[256,256]{1,0:T(8,128)(2,1)S(1)} custom-call(s32[2,128]{1,0:T(2,128)} %perm_hbm.1, bf16[256,256]{1,0:T(8,128)(2,1)} %x_hbm.1), custom_call_target="tpu_custom_call" | custom-call | tf_op jit(solution)/shard_map/pallas_call | solution.py:86
  1.3 3.8 %collective-permute-start.2 = (bf16[256,256]{1,0:T(8,128)(2,1)S(1)}, bf16[256,256]{1,0:T(8,128)(2,1)S(1)}, u32[]{:S(2)}, u32[]{:S(2)}) collective-permute-start(bf16[256,256]{1,0:T(8,128)(2,1)S(1)} %shard_map.101.refs_0_), channel_id=1, source_target_pairs={{0,128},{1,33},{2,130},{3,35},{4,132},{5,37},{6,134},{7,39},{8,136... | collective-permute-start | bytes 393224 | tf_op jit(solution)/shard_map/ppermute | solution.py:47
  5.1 0.8 %collective-permute-start.1 = (bf16[256,256]{1,0:T(8,128)(2,1)S(1)}, bf16[256,256]{1,0:T(8,128)(2,1)S(1)}, u32[]{:S(2)}, u32[]{:S(2)}) collective-permute-start(bf16[256,256]{1,0:T(8,128)(2,1)S(1)} %shard_map.101.refs_0_), channel_id=1, source_target_pairs={{0,192},{1,49},{2,194},{3,51},{4,196},{5,53},{6,198},{7,55},{8,200... | collective-permute-start | bytes 393224 | tf_op jit(solution)/shard_map/ppermute | solution.py:47
  5.9 0.7 collective-permute-start
  6.6 0.9 %collective-permute-done.2.refs_3_ = bf16[256,256]{1,0:T(8,128)(2,1)S(1)} collective-permute-done((bf16[256,256]{1,0:T(8,128)(2,1)S(1)}, bf16[256,256]{1,0:T(8,128)(2,1)S(1)}, u32[]{:S(2)}, u32[]{:S(2)}) %collective-permute-start.2) | collective-permute-done | bytes 131104 | tf_op jit(solution)/shard_map/ppermute | solution.py:47
  7.5 2.1 %collective-permute-done.1.refs_2_ = bf16[256,256]{1,0:T(8,128)(2,1)S(1)} collective-permute-done((bf16[256,256]{1,0:T(8,128)(2,1)S(1)}, bf16[256,256]{1,0:T(8,128)(2,1)S(1)}, u32[]{:S(2)}, u32[]{:S(2)}) %collective-permute-start.1) | collective-permute-done | bytes 131104 | tf_op jit(solution)/shard_map/ppermute | solution.py:47
  9.6 1.4 %collective-permute-done.refs_1_ = bf16[256,256]{1,0:T(8,128)(2,1)S(1)} collective-permute-done((bf16[256,256]{1,0:T(8,128)(2,1)S(1)}, bf16[256,256]{1,0:T(8,128)(2,1)S(1)}, u32[]{:S(2)}, u32[]{:S(2)}) %collective-permute-start) | collective-permute-done | bytes 131104 | tf_op jit(solution)/shard_map/ppermute | solution.py:47
  11.0 2.8 %collective-permute-start.5 = (bf16[1024,256]{1,0:T(8,128)(2,1)S(1)}, bf16[1024,256]{1,0:T(8,128)(2,1)S(1)}, u32[]{:S(2)}, u32[]{:S(2)}) collective-permute-start(bf16[1024,256]{1,0:T(8,128)(2,1)S(1)} %shard_map.102.refs_0_), channel_id=1, source_target_pairs={{0,32},{1,129},{2,34},{3,131},{4,36},{5,133},{6,38},{7,135},{8,40}... | collective-permute-start | bytes 1572872 | tf_op jit(solution)/shard_map/ppermute | solution.py:47
  13.8 0.9 %collective-permute-start.4 = (bf16[1024,256]{1,0:T(8,128)(2,1)S(1)}, bf16[1024,256]{1,0:T(8,128)(2,1)S(1)}, u32[]{:S(2)}, u32[]{:S(2)}) collective-permute-start(bf16[1024,256]{1,0:T(8,128)(2,1)S(1)} %shard_map.102.refs_0_), channel_id=1, source_target_pairs={{0,48},{1,193},{2,50},{3,195},{4,52},{5,197},{6,54},{7,199},{8,56}... | collective-permute-start | bytes 1572872 | tf_op jit(solution)/shard_map/ppermute | solution.py:47
  14.6 0.6 collective-permute-start.3
  15.3 0.0 copy-start.1
  15.3 1.2 %copy-done.1 = bf16[32,2,128,64]{2,3,1,0:T(8,128)(2,1)S(1)} copy-done((bf16[32,2,128,64]{2,3,1,0:T(8,128)(2,1)S(1)}, bf16[32,2,128,64]{2,3,1,0:T(8,128)(2,1)}, u32[]{:S(2)}) %copy-start.1) | copy-done | bytes 1048600
  16.5 0.0 copy-start.2
  16.5 1.2 %copy-done.2 = bf16[32,2,128,64]{2,3,1,0:T(8,128)(2,1)S(1)} copy-done((bf16[32,2,128,64]{2,3,1,0:T(8,128)(2,1)S(1)}, bf16[32,2,128,64]{2,3,1,0:T(8,128)(2,1)}, u32[]{:S(2)}) %copy-start.2) | copy-done | bytes 1048600
  17.7 0.0 copy-start.3
  17.7 0.7 copy-done.3
  18.4 0.0 copy-start.4
  18.4 0.7 copy-done.4
  19.0 0.0 copy-start.5
  19.0 0.7 copy-done.5
  19.7 0.0 copy-start.6
  19.7 0.7 copy-done.6
  20.3 0.7 copy-done.7
  21.0 2.5 %shard_map.100 = (bf16[32,128,128]{2,1,0:T(8,128)(2,1)S(1)}, bf16[32,64,256]{2,1,0:T(8,128)(2,1)S(1)}, s32[60]{0:T(128)S(4)}) custom-call(s32[32]{0:T(128)S(1)} %copy-done.3, s32[32]{0:T(128)S(1)} %copy-done.4, s32[32]{0:T(128)S(1)} %copy-done.5, s32[28]{0:T(128)S(1)} %copy-done.6, s32[28]{0:T(128)S(1)} %copy-done.7, bf16[32,2,64,128]{3,2,1,0:T(8,128)(2,1)S(1)} %bitcast.2, ...), custom_call_target="tpu_custom_call" | custom-call | bytes 8388608 | tf_op jit(solution)/shard_map/pallas_call | solution.py:158
  23.5 0.0 collective-permute-done.5.refs_3_
  23.5 3.1 %collective-permute-done.4.refs_2_ = bf16[1024,256]{1,0:T(8,128)(2,1)S(1)} collective-permute-done((bf16[1024,256]{1,0:T(8,128)(2,1)S(1)}, bf16[1024,256]{1,0:T(8,128)(2,1)S(1)}, u32[]{:S(2)}, u32[]{:S(2)}) %collective-permute-start.4) | collective-permute-done | bytes 524320 | tf_op jit(solution)/shard_map/ppermute | solution.py:47
  26.6 0.0 collective-permute-done.3.refs_1_
  26.6 0.0 copy-done
  26.6 5.8 %shard_map.103 = (bf16[2048,256]{1,0:T(8,128)(2,1)S(1)}, f32[2048,256]{1,0:T(8,128)S(1)}) custom-call(s32[60]{0:T(128)S(4)} %get-tuple-element.10.lists, bf16[1024,256]{1,0:T(8,128)(2,1)S(1)} %shard_map.102.refs_0_, bf16[1024,256]{1,0:T(8,128)(2,1)S(1)} %collective-permute-done.3.refs_1_, bf16[1024,256]{1,0:T(8,128)(2,1)S(1)} %collective-permute-done.4.refs_2_, ...), custom_call_target="tpu_custom_call" | custom-call | flops 1073741824 | bytes 16777216 | tf_op jit(solution)/shard_map/pallas_call | solution.py:218
  32.4 3.5 %collective-permute-start.6 = (bf16[2048,256]{1,0:T(8,128)(2,1)S(1)}, bf16[2048,256]{1,0:T(8,128)(2,1)S(1)}, u32[]{:S(2)}, u32[]{:S(2)}) collective-permute-start(bf16[2048,256]{1,0:T(8,128)(2,1)S(1)} %get-tuple-element.14), channel_id=1, source_target_pairs={{0,1},{1,0},{2,3},{3,2},{4,5},{5,4},{6,7},{7,6},{8,9},{9,8},{10,11... | collective-permute-start | bytes 3145736 | tf_op jit(solution)/shard_map/ppermute | solution.py:58
  35.9 2.3 %collective-permute-done.6 = bf16[2048,256]{1,0:T(8,128)(2,1)S(1)} collective-permute-done((bf16[2048,256]{1,0:T(8,128)(2,1)S(1)}, bf16[2048,256]{1,0:T(8,128)(2,1)S(1)}, u32[]{:S(2)}, u32[]{:S(2)}) %collective-permute-start.6) | collective-permute-done | bytes 1048608 | tf_op jit(solution)/shard_map/ppermute | solution.py:58
  38.2 0.2 add_convert_fusion.7
  38.4 7.0 %collective-permute-start.7 = (bf16[256,256]{1,0:T(8,128)(2,1)S(1)}, bf16[256,256]{1,0:T(8,128)(2,1)S(1)}, u32[]{:S(2)}, u32[]{:S(2)}) collective-permute-start(bf16[256,256]{1,0:T(8,128)(2,1)S(1)} %get-tuple-element.15), channel_id=1, source_target_pairs={{0,8},{1,9},{2,10},{3,11},{4,12},{5,13},{6,14},{7,15},{8,0},{9,1},... | collective-permute-start | bytes 393224 | tf_op jit(solution)/shard_map/ppermute | solution.py:54
  45.4 1.6 %collective-permute-start.13 = (bf16[256,256]{1,0:T(8,128)(2,1)S(1)}, bf16[256,256]{1,0:T(8,128)(2,1)S(1)}, u32[]{:S(2)}, u32[]{:S(2)}) collective-permute-start(bf16[256,256]{1,0:T(8,128)(2,1)S(1)} %get-tuple-element.16), channel_id=1, source_target_pairs={{0,6},{1,7},{2,8},{3,9},{4,10},{5,11},{6,12},{7,13},{8,14},{9,15},... | collective-permute-start | bytes 393224 | tf_op jit(solution)/shard_map/ppermute | solution.py:54
  47.0 2.8 %collective-permute-start.12 = (bf16[256,256]{1,0:T(8,128)(2,1)S(1)}, bf16[256,256]{1,0:T(8,128)(2,1)S(1)}, u32[]{:S(2)}, u32[]{:S(2)}) collective-permute-start(bf16[256,256]{1,0:T(8,128)(2,1)S(1)} %get-tuple-element.17), channel_id=1, source_target_pairs={{0,10},{1,11},{2,12},{3,13},{4,14},{5,15},{6,0},{7,1},{8,2},{9,3},... | collective-permute-start | bytes 393224 | tf_op jit(solution)/shard_map/ppermute | solution.py:54
  49.9 1.2 %collective-permute-start.11 = (bf16[256,256]{1,0:T(8,128)(2,1)S(1)}, bf16[256,256]{1,0:T(8,128)(2,1)S(1)}, u32[]{:S(2)}, u32[]{:S(2)}) collective-permute-start(bf16[256,256]{1,0:T(8,128)(2,1)S(1)} %get-tuple-element.18), channel_id=1, source_target_pairs={{0,4},{1,5},{2,6},{3,7},{4,8},{5,9},{6,10},{7,11},{8,12},{9,13},{1... | collective-permute-start | bytes 393224 | tf_op jit(solution)/shard_map/ppermute | solution.py:54
  51.1 2.4 %collective-permute-start.10 = (bf16[256,256]{1,0:T(8,128)(2,1)S(1)}, bf16[256,256]{1,0:T(8,128)(2,1)S(1)}, u32[]{:S(2)}, u32[]{:S(2)}) collective-permute-start(bf16[256,256]{1,0:T(8,128)(2,1)S(1)} %get-tuple-element.19), channel_id=1, source_target_pairs={{0,12},{1,13},{2,14},{3,15},{4,0},{5,1},{6,2},{7,3},{8,4},{9,5},{1... | collective-permute-start | bytes 393224 | tf_op jit(solution)/shard_map/ppermute | solution.py:54
  53.5 0.0 collective-permute-done.7
  53.5 0.7 %collective-permute-start.9 = (bf16[256,256]{1,0:T(8,128)(2,1)S(1)}, bf16[256,256]{1,0:T(8,128)(2,1)S(1)}, u32[]{:S(2)}, u32[]{:S(2)}) collective-permute-start(bf16[256,256]{1,0:T(8,128)(2,1)S(1)} %get-tuple-element.20), channel_id=1, source_target_pairs={{0,2},{1,3},{2,4},{3,5},{4,6},{5,7},{6,8},{7,9},{8,10},{9,11},{10,... | collective-permute-start | bytes 393224 | tf_op jit(solution)/shard_map/ppermute | solution.py:54
  54.2 7.4 %collective-permute-done.13 = bf16[256,256]{1,0:T(8,128)(2,1)S(1)} collective-permute-done((bf16[256,256]{1,0:T(8,128)(2,1)S(1)}, bf16[256,256]{1,0:T(8,128)(2,1)S(1)}, u32[]{:S(2)}, u32[]{:S(2)}) %collective-permute-start.13) | collective-permute-done | bytes 131104 | tf_op jit(solution)/shard_map/ppermute | solution.py:54
  61.6 0.0 collective-permute-start.8
  61.6 0.0 collective-permute-done.12
  61.6 0.7 %collective-permute-done.11 = bf16[256,256]{1,0:T(8,128)(2,1)S(1)} collective-permute-done((bf16[256,256]{1,0:T(8,128)(2,1)S(1)}, bf16[256,256]{1,0:T(8,128)(2,1)S(1)}, u32[]{:S(2)}, u32[]{:S(2)}) %collective-permute-start.11) | collective-permute-done | bytes 131104 | tf_op jit(solution)/shard_map/ppermute | solution.py:54
  62.3 3.3 %collective-permute-done.10 = bf16[256,256]{1,0:T(8,128)(2,1)S(1)} collective-permute-done((bf16[256,256]{1,0:T(8,128)(2,1)S(1)}, bf16[256,256]{1,0:T(8,128)(2,1)S(1)}, u32[]{:S(2)}, u32[]{:S(2)}) %collective-permute-start.10) | collective-permute-done | bytes 131104 | tf_op jit(solution)/shard_map/ppermute | solution.py:54
  65.6 3.1 %collective-permute-done.9 = bf16[256,256]{1,0:T(8,128)(2,1)S(1)} collective-permute-done((bf16[256,256]{1,0:T(8,128)(2,1)S(1)}, bf16[256,256]{1,0:T(8,128)(2,1)S(1)}, u32[]{:S(2)}, u32[]{:S(2)}) %collective-permute-start.9) | collective-permute-done | bytes 131104 | tf_op jit(solution)/shard_map/ppermute | solution.py:54
  68.7 0.6 collective-permute-done.8
  69.3 0.8 %add_convert_fusion = bf16[256,256]{1,0:T(8,128)(2,1)} fusion(bf16[256,256]{1,0:T(8,128)(2,1)S(1)} %collective-permute-done.13, bf16[256,256]{1,0:T(8,128)(2,1)S(1)} %collective-permute-done.12, bf16[256,256]{1,0:T(8,128)(2,1)S(1)} %collective-permute-done.11, bf16[256,256]{1,0:T(8,128)(2,1)S(1)} %collective-permute-done.10, ...), kind=kLoop, calls=%fused_computation | loop fusion | flops 1114112 | bytes 1441792 | tf_op jit(solution)/shard_map/convert_element_type | solution.py:270
  (2 shorter events, 0.0 us)
Async XLA Ops:
  0.0 26.6 %copy-start = (bf16[28,2,128,128]{3,2,1,0:T(8,128)(2,1)S(1)}, bf16[28,2,128,128]{3,2,1,0:T(8,128)(2,1)}, u32[]{:S(2)}) copy-start(bf16[28,2,128,128]{3,2,1,0:T(8,128)(2,1)} %refs_6_.1) | copy-start | bytes 5505028
  1.3 6.2 %collective-permute-start.2 = (bf16[256,256]{1,0:T(8,128)(2,1)S(1)}, bf16[256,256]{1,0:T(8,128)(2,1)S(1)}, u32[]{:S(2)}, u32[]{:S(2)}) collective-permute-start(bf16[256,256]{1,0:T(8,128)(2,1)S(1)} %shard_map.101.refs_0_), channel_id=1, source_target_pairs={{0,128},{1,33},{2,130},{3,35},{4,132},{5,37},{6,134},{7,39},{8,136... | collective-permute-start | bytes 393224 | tf_op jit(solution)/shard_map/ppermute | solution.py:47
  5.1 4.4 %collective-permute-start.1 = (bf16[256,256]{1,0:T(8,128)(2,1)S(1)}, bf16[256,256]{1,0:T(8,128)(2,1)S(1)}, u32[]{:S(2)}, u32[]{:S(2)}) collective-permute-start(bf16[256,256]{1,0:T(8,128)(2,1)S(1)} %shard_map.101.refs_0_), channel_id=1, source_target_pairs={{0,192},{1,49},{2,194},{3,51},{4,196},{5,53},{6,198},{7,55},{8,200... | collective-permute-start | bytes 393224 | tf_op jit(solution)/shard_map/ppermute | solution.py:47
  5.9 5.0 %collective-permute-start = (bf16[256,256]{1,0:T(8,128)(2,1)S(1)}, bf16[256,256]{1,0:T(8,128)(2,1)S(1)}, u32[]{:S(2)}, u32[]{:S(2)}) collective-permute-start(bf16[256,256]{1,0:T(8,128)(2,1)S(1)} %shard_map.101.refs_0_), channel_id=1, source_target_pairs={{0,64},{1,17},{2,66},{3,19},{4,68},{5,21},{6,70},{7,23},{8,72},{9,... | collective-permute-start | bytes 393224 | tf_op jit(solution)/shard_map/ppermute | solution.py:47
  11.0 12.5 %collective-permute-start.5 = (bf16[1024,256]{1,0:T(8,128)(2,1)S(1)}, bf16[1024,256]{1,0:T(8,128)(2,1)S(1)}, u32[]{:S(2)}, u32[]{:S(2)}) collective-permute-start(bf16[1024,256]{1,0:T(8,128)(2,1)S(1)} %shard_map.102.refs_0_), channel_id=1, source_target_pairs={{0,32},{1,129},{2,34},{3,131},{4,36},{5,133},{6,38},{7,135},{8,40}... | collective-permute-start | bytes 1572872 | tf_op jit(solution)/shard_map/ppermute | solution.py:47
  13.8 12.8 %collective-permute-start.4 = (bf16[1024,256]{1,0:T(8,128)(2,1)S(1)}, bf16[1024,256]{1,0:T(8,128)(2,1)S(1)}, u32[]{:S(2)}, u32[]{:S(2)}) collective-permute-start(bf16[1024,256]{1,0:T(8,128)(2,1)S(1)} %shard_map.102.refs_0_), channel_id=1, source_target_pairs={{0,48},{1,193},{2,50},{3,195},{4,52},{5,197},{6,54},{7,199},{8,56}... | collective-permute-start | bytes 1572872 | tf_op jit(solution)/shard_map/ppermute | solution.py:47
  14.6 12.0 %collective-permute-start.3 = (bf16[1024,256]{1,0:T(8,128)(2,1)S(1)}, bf16[1024,256]{1,0:T(8,128)(2,1)S(1)}, u32[]{:S(2)}, u32[]{:S(2)}) collective-permute-start(bf16[1024,256]{1,0:T(8,128)(2,1)S(1)} %shard_map.102.refs_0_), channel_id=1, source_target_pairs={{0,16},{1,65},{2,18},{3,67},{4,20},{5,69},{6,22},{7,71},{8,24},{9,... | collective-permute-start | bytes 1572872 | tf_op jit(solution)/shard_map/ppermute | solution.py:47
  15.3 1.2 %copy-start.1 = (bf16[32,2,128,64]{2,3,1,0:T(8,128)(2,1)S(1)}, bf16[32,2,128,64]{2,3,1,0:T(8,128)(2,1)}, u32[]{:S(2)}) copy-start(bf16[32,2,128,64]{2,3,1,0:T(8,128)(2,1)} %param.12) | copy-start | bytes 3145732
  16.5 1.2 %copy-start.2 = (bf16[32,2,128,64]{2,3,1,0:T(8,128)(2,1)S(1)}, bf16[32,2,128,64]{2,3,1,0:T(8,128)(2,1)}, u32[]{:S(2)}) copy-start(bf16[32,2,128,64]{2,3,1,0:T(8,128)(2,1)} %param.13) | copy-start | bytes 3145732
  17.7 0.7 copy-start.3
  18.4 0.7 copy-start.4
  19.0 0.7 copy-start.5
  19.7 0.7 copy-start.6
  20.3 0.7 copy-start.7
  32.4 5.8 %collective-permute-start.6 = (bf16[2048,256]{1,0:T(8,128)(2,1)S(1)}, bf16[2048,256]{1,0:T(8,128)(2,1)S(1)}, u32[]{:S(2)}, u32[]{:S(2)}) collective-permute-start(bf16[2048,256]{1,0:T(8,128)(2,1)S(1)} %get-tuple-element.14), channel_id=1, source_target_pairs={{0,1},{1,0},{2,3},{3,2},{4,5},{5,4},{6,7},{7,6},{8,9},{9,8},{10,11... | collective-permute-start | bytes 3145736 | tf_op jit(solution)/shard_map/ppermute | solution.py:58
  38.4 15.1 %collective-permute-start.7 = (bf16[256,256]{1,0:T(8,128)(2,1)S(1)}, bf16[256,256]{1,0:T(8,128)(2,1)S(1)}, u32[]{:S(2)}, u32[]{:S(2)}) collective-permute-start(bf16[256,256]{1,0:T(8,128)(2,1)S(1)} %get-tuple-element.15), channel_id=1, source_target_pairs={{0,8},{1,9},{2,10},{3,11},{4,12},{5,13},{6,14},{7,15},{8,0},{9,1},... | collective-permute-start | bytes 393224 | tf_op jit(solution)/shard_map/ppermute | solution.py:54
  45.4 16.2 %collective-permute-start.13 = (bf16[256,256]{1,0:T(8,128)(2,1)S(1)}, bf16[256,256]{1,0:T(8,128)(2,1)S(1)}, u32[]{:S(2)}, u32[]{:S(2)}) collective-permute-start(bf16[256,256]{1,0:T(8,128)(2,1)S(1)} %get-tuple-element.16), channel_id=1, source_target_pairs={{0,6},{1,7},{2,8},{3,9},{4,10},{5,11},{6,12},{7,13},{8,14},{9,15},... | collective-permute-start | bytes 393224 | tf_op jit(solution)/shard_map/ppermute | solution.py:54
  47.0 14.5 %collective-permute-start.12 = (bf16[256,256]{1,0:T(8,128)(2,1)S(1)}, bf16[256,256]{1,0:T(8,128)(2,1)S(1)}, u32[]{:S(2)}, u32[]{:S(2)}) collective-permute-start(bf16[256,256]{1,0:T(8,128)(2,1)S(1)} %get-tuple-element.17), channel_id=1, source_target_pairs={{0,10},{1,11},{2,12},{3,13},{4,14},{5,15},{6,0},{7,1},{8,2},{9,3},... | collective-permute-start | bytes 393224 | tf_op jit(solution)/shard_map/ppermute | solution.py:54
  49.9 12.4 %collective-permute-start.11 = (bf16[256,256]{1,0:T(8,128)(2,1)S(1)}, bf16[256,256]{1,0:T(8,128)(2,1)S(1)}, u32[]{:S(2)}, u32[]{:S(2)}) collective-permute-start(bf16[256,256]{1,0:T(8,128)(2,1)S(1)} %get-tuple-element.18), channel_id=1, source_target_pairs={{0,4},{1,5},{2,6},{3,7},{4,8},{5,9},{6,10},{7,11},{8,12},{9,13},{1... | collective-permute-start | bytes 393224 | tf_op jit(solution)/shard_map/ppermute | solution.py:54
  51.1 14.5 %collective-permute-start.10 = (bf16[256,256]{1,0:T(8,128)(2,1)S(1)}, bf16[256,256]{1,0:T(8,128)(2,1)S(1)}, u32[]{:S(2)}, u32[]{:S(2)}) collective-permute-start(bf16[256,256]{1,0:T(8,128)(2,1)S(1)} %get-tuple-element.19), channel_id=1, source_target_pairs={{0,12},{1,13},{2,14},{3,15},{4,0},{5,1},{6,2},{7,3},{8,4},{9,5},{1... | collective-permute-start | bytes 393224 | tf_op jit(solution)/shard_map/ppermute | solution.py:54
  53.5 15.2 %collective-permute-start.9 = (bf16[256,256]{1,0:T(8,128)(2,1)S(1)}, bf16[256,256]{1,0:T(8,128)(2,1)S(1)}, u32[]{:S(2)}, u32[]{:S(2)}) collective-permute-start(bf16[256,256]{1,0:T(8,128)(2,1)S(1)} %get-tuple-element.20), channel_id=1, source_target_pairs={{0,2},{1,3},{2,4},{3,5},{4,6},{5,7},{6,8},{7,9},{8,10},{9,11},{10,... | collective-permute-start | bytes 393224 | tf_op jit(solution)/shard_map/ppermute | solution.py:54
  61.6 7.8 %collective-permute-start.8 = (bf16[256,256]{1,0:T(8,128)(2,1)S(1)}, bf16[256,256]{1,0:T(8,128)(2,1)S(1)}, u32[]{:S(2)}, u32[]{:S(2)}) collective-permute-start(bf16[256,256]{1,0:T(8,128)(2,1)S(1)} %get-tuple-element.21), channel_id=1, source_target_pairs={{0,14},{1,15},{2,0},{3,1},{4,2},{5,3},{6,4},{7,5},{8,6},{9,7},{10,... | collective-permute-start | bytes 393224 | tf_op jit(solution)/shard_map/ppermute | solution.py:54

commit v3 on v2

--- a/solution.py
+++ b/solution.py
@@ -17,6 +17,10 @@
 NCORE = 2
 SLAB = 32
 WAYS = 4
+GROUPS = 4
+LIST = 36
+COUNTS = 2 * GROUPS * LIST
+ORDER_OF_STEP = 0x13506427
 STEPS = (4, 7, 1, 6, 2, 5, 3, 0)
 F32 = jnp.float32
 BF16 = jnp.bfloat16
@@ -113,8 +117,37 @@
 
 
 def prepare_kernel(
-    rank_ref, far_rows, far_cols, near_rows, near_cols, u_ref, v_ref, u_out, v_out, lists
+    rank_hbm,
+    far_rows_hbm,
+    far_cols_hbm,
+    near_rows_hbm,
+    near_cols_hbm,
+    u_hbm,
+    v_hbm,
+    u_out,
+    v_out,
+    lists,
+    rank,
+    far_rows,
+    far_cols,
+    near_rows,
+    near_cols,
+    u_ref,
+    v_ref,
+    sems,
 ):
+    pairs = (
+        (far_rows_hbm, far_rows),
+        (far_cols_hbm, far_cols),
+        (near_rows_hbm, near_rows),
+        (near_cols_hbm, near_cols),
+        (rank_hbm, rank),
+        (v_hbm, v_ref),
+        (u_hbm, u_ref),
+    )
+    copies = [pltpu.make_async_copy(a, b, sems.at[k]) for k, (a, b) in enumerate(pairs)]
+    for copy in copies:
+        copy.start()
     my_x, my_y, my_z, my_core = position()
 
     def gray(d):
@@ -125,26 +158,46 @@
         r = k >> 1
         dx = gray((my_x - (r >> 2)) & 3)
         dy = gray((my_y - (r & 3)) & 3)
-        slot = jnp.where(my_core == 0, dy * 4 + dx, dx * 4 + dy) * 2 + (k & 1)
+        piece = jnp.where(my_core == 0, dy, dx)
+        place = jnp.where(my_core == 0, dx, dy) * 2 + (k & 1)
         dz = (((row & (SLAB - 1)) >> 2) - my_z) & 7
         own = 1 - (((row >> 1) & 1) ^ my_core)
-        target = ((0x13506427 >> (dz * 4)) & 15) * 4 + own * 2 + (row & 1)
-        return b | (slot << 6) | (target << 11)
-
-    def fill(count, rows, cols, base):
+        target = own * 16 + ((ORDER_OF_STEP >> (dz * 4)) & 15) * 2 + (row & 1)
+        late = (piece == 1) | (piece == 2)
+        group = jnp.where(late, 2 + own, jnp.where(piece == 0, 0, 1))
+        slot = jnp.where(piece == 2, 8 + place, place)
+        return group, b | (slot << 6) | (target << 11)
+
+    def fill(count, rows, cols, kind):
+        for g in range(GROUPS):
+            lists[COUNTS + kind * GROUPS + g] = 0
+
         def step(b, carry):
-            lists[base + b] = entry(b, rows[b], cols[b])
+            group, value = entry(b, rows[b], cols[b])
+            at = COUNTS + kind * GROUPS + group
+            used = lists[at]
+            lists[(kind * GROUPS + group) * LIST + used] = value
+            lists[at] = used + 1
             return carry
 
         lax.fori_loop(0, count, step, 0)
-
+        for g in range(GROUPS):
+            at = COUNTS + kind * GROUPS + g
+            used = lists[at]
+            for k in range(WAYS - 1):
+                lists[(kind * GROUPS + g) * LIST + used + k] = SLAB << 11
+            lists[at] = (used + WAYS - 1) // WAYS
+
+    for copy in copies[:4]:
+        copy.wait()
     fill(NB, far_rows, far_cols, 0)
-    fill(NN, near_rows, near_cols, NB)
-
+    fill(NN, near_rows, near_cols, 1)
+    for copy in copies[4:]:
+        copy.wait()
     line = lax.broadcasted_iota(jnp.int32, (RMAX, LEAF), 0)
 
     def step(b, carry):
-        keep = line < rank_ref[b]
+        keep = line < rank[b]
         for k in range(2):
             v = v_ref[b, k]
             v_out[b, :, k * LEAF : (k + 1) * LEAF] = jnp.where(keep, v.astype(F32), 0.0).astype(BF16)
@@ -155,34 +208,48 @@
 
 
 def prepare(rank, far_rows, far_cols, near_rows, near_cols, u, v):
+    operands = (rank, far_rows, far_cols, near_rows, near_cols, u, v)
+    operands = [pltpu.with_memory_space_constraint(x, pltpu.HBM) for x in operands]
     return pl.pallas_call(
         prepare_kernel,
         out_shape=(
             pltpu.VMEM((NB, LEAF, 2 * RMAX), BF16),
             pltpu.VMEM((NB, RMAX, 2 * LEAF), BF16),
-            pltpu.SMEM((NB + NN,), jnp.int32),
+            pltpu.SMEM((COUNTS + 2 * GROUPS,), jnp.int32),
         ),
-        in_specs=[SMEM] * 5 + [VMEM] * 2,
+        in_specs=[ANY] * 7,
         out_specs=(VMEM, VMEM, SMEM),
+        scratch_shapes=[
+            pltpu.SMEM((NB,), jnp.int32),
+            pltpu.SMEM((NB,), jnp.int32),
+            pltpu.SMEM((NB,), jnp.int32),
+            pltpu.SMEM((NN,), jnp.int32),
+            pltpu.SMEM((NN,), jnp.int32),
+            pltpu.VMEM((NB, 2, RMAX, LEAF), BF16),
+            pltpu.VMEM((NB, 2, RMAX, LEAF), BF16),
+            pltpu.SemaphoreType.DMA((7,)),
+        ],
         compiler_params=limit(4),
-        cost_estimate=pl.CostEstimate(flops=0, bytes_accessed=8 << 20, transcendentals=0),
-    )(rank, far_rows, far_cols, near_rows, near_cols, u, v)
-
-
-def block_kernel(lists, *refs):
-    pieces = refs[:4]
-    u_ref, v_ref, near_ref, other_ref, own_ref, trial, total = refs[4:]
-    for p, piece in enumerate(pieces):
-        for q in range(8):
-            x = piece[q * LEAF : (q + 1) * LEAF, :]
-            trial[p * 8 + q, :LEAF, :] = x
-            trial[p * 8 + q, LEAF:, :] = swap_parts(x)
-    total[...] = jnp.zeros_like(total)
-
-    def entries(base, q):
+        cost_estimate=cost(8),
+    )(*operands)
+
+
+def cost(mib):
+    return pl.CostEstimate(flops=0, bytes_accessed=mib << 20, transcendentals=0)
+
+
+def load(piece, trial, base):
+    for q in range(8):
+        x = piece[q * LEAF : (q + 1) * LEAF, :]
+        trial[base + q, :LEAF, :] = x
+        trial[base + q, LEAF:, :] = swap_parts(x)
+
+
+def work(group, lists, u_ref, v_ref, near_ref, trial, total):
+    def entries(kind, q):
         found = []
         for k in range(WAYS):
-            e = lists[base + q * WAYS + k]
+            e = lists[(kind * GROUPS + group) * LIST + q * WAYS + k]
             found.append((e & 63, (e >> 6) & 31, e >> 11))
         return found
 
@@ -198,40 +265,86 @@
         return carry
 
     def near_step(q, carry):
-        for n, slot, target in entries(NB, q):
+        for n, slot, target in entries(1, q):
             block = jnp.concatenate([near_ref[n, 0], near_ref[n, 1]], axis=1)
             total[target] += jnp.dot(block, trial[slot], preferred_element_type=F32)
         return carry
 
-    lax.fori_loop(0, NB // WAYS, far_step, 0)
-    lax.fori_loop(0, NN // WAYS, near_step, 0)
-
-    for j in range(NZ):
-        for k in range(2):
-            rows = slice((j * 2 + k) * LEAF, (j * 2 + k + 1) * LEAF)
-            other_ref[rows, :] = total[j * 4 + k].astype(BF16)
-            own_ref[rows, :] = total[j * 4 + 2 + k]
-
-
-def blocks(lists, pieces, u, v, near):
-    rows = NZ * 2 * LEAF
-    return pl.pallas_call(
-        block_kernel,
+    lax.fori_loop(0, lists[COUNTS + group], far_step, 0)
+    lax.fori_loop(0, lists[COUNTS + GROUPS + group], near_step, 0)
+
+
+TOTAL = pltpu.VMEM((SLAB + 1, LEAF, COLS), F32)
+
+
+def first_kernel(lists, u_ref, v_ref, near_ref, piece, total, trial):
+    total[...] = jnp.zeros_like(total)
+    load(piece, trial, 0)
+    work(0, lists, u_ref, v_ref, near_ref, trial, total)
+
+
+def second_kernel(lists, u_ref, v_ref, near_ref, piece, _, total, trial):
+    load(piece, trial, 0)
+    work(1, lists, u_ref, v_ref, near_ref, trial, total)
+
+
+def third_kernel(lists, u_ref, v_ref, near_ref, ahead, back, _, total, trial, other_ref):
+    load(ahead, trial, 0)
+    load(back, trial, 8)
+    work(2, lists, u_ref, v_ref, near_ref, trial, total)
+    for t in range(SLAB // 2):
+        other_ref[t * LEAF : (t + 1) * LEAF, :] = total[t].astype(BF16)
+
+
+def fourth_kernel(lists, u_ref, v_ref, near_ref, trial, _, total):
+    work(3, lists, u_ref, v_ref, near_ref, trial, total)
+
+
+def blocks(common, pieces):
+    first, ahead, back, two = pieces
+    scratch = [pltpu.VMEM((8, 2 * LEAF, COLS), BF16)]
+    total = pl.pallas_call(
+        first_kernel,
+        out_shape=TOTAL,
+        in_specs=[SMEM] + [VMEM] * 4,
+        out_specs=VMEM,
+        scratch_shapes=scratch,
+        compiler_params=limit(6),
+        cost_estimate=cost(8),
+    )(*common, first)
+    total = pl.pallas_call(
+        second_kernel,
+        out_shape=TOTAL,
+        in_specs=[SMEM] + [VMEM] * 5,
+        out_specs=VMEM,
+        scratch_shapes=scratch,
+        input_output_aliases={5: 0},
+        compiler_params=limit(6),
+        cost_estimate=cost(6),
+    )(*common, two, total)
+    total, trial, other = pl.pallas_call(
+        third_kernel,
         out_shape=(
-            pltpu.VMEM((rows, COLS), BF16),
-            pltpu.VMEM((rows, COLS), F32),
+            TOTAL,
+            pltpu.VMEM((16, 2 * LEAF, COLS), BF16),
+            pltpu.VMEM((SLAB // 2 * LEAF, COLS), BF16),
         ),
-        in_specs=[SMEM] + [VMEM] * 7,
-        out_specs=(VMEM, VMEM),
-        scratch_shapes=[
-            pltpu.VMEM((SLAB, 2 * LEAF, COLS), BF16),
-            pltpu.VMEM((NZ * 4, LEAF, COLS), F32),
-        ],
-        compiler_params=limit(12),
-        cost_estimate=pl.CostEstimate(
-            flops=1 << 30, bytes_accessed=16 << 20, transcendentals=0
-        ),
-    )(lists, *pieces, u, v, near)
+        in_specs=[SMEM] + [VMEM] * 6,
+        out_specs=(VMEM, VMEM, VMEM),
+        input_output_aliases={6: 0},
+        compiler_params=limit(6),
+        cost_estimate=cost(8),
+    )(*common, ahead, back, total)
+    total = pl.pallas_call(
+        fourth_kernel,
+        out_shape=TOTAL,
+        in_specs=[SMEM] + [VMEM] * 5,
+        out_specs=VMEM,
+        input_output_aliases={5: 0},
+        compiler_params=limit(6),
+        cost_estimate=cost(6),
+    )(*common, trial, total)
+    return other, total
 
 
 def gather(mine):
@@ -255,12 +368,13 @@
         jnp.swapaxes(far_v, 2, 3),
     )
     pieces = gather(mine)
-    other, own = blocks(lists, pieces, u, v, near_block)
+    other, own = blocks((lists, u, v, near_block), pieces)
     swapped = other_core(other)
     total, parts = None, []
     for j, step in enumerate(STEPS):
         rows = slice(j * 2 * LEAF, (j + 1) * 2 * LEAF)
-        chip = own[rows] + swapped[rows].astype(F32)
+        mine = own[SLAB // 2 + 2 * j : SLAB // 2 + 2 * j + 2].reshape(2 * LEAF, COLS)
+        chip = mine + swapped[rows].astype(F32)
         if step == 0:
             total = chip
         else:

time: 70.4 us -> 66.5 us (0.945)
  local copies, waits for them, and re-layouts: 5.73 us -> 0.19 us
  waiting for transfers between devices: 24.9 us -> 26.1 us
  Pallas kernels: 9.56 us -> 10.6 us
    unnamed x16 -> x2, local copies, waits for them, and re-layouts: 5.73 us -> 0.01 us
    ppermute x6, waiting for transfers between devices: 7.46 us -> 8.98 us  [hop(): return lax.ppermute(value, ('row', 'col'), pairs)]
    ppermute x1, waiting for transfers between devices: 2.29 us -> 1.05 us  [other_core(): return lax.ppermute(value, 'col', [(d, d ^ 1) for d in range(NZ * NCORE)])]
    ppermute x7, waiting for transfers between devices: 15.1 us -> 16 us  [along_z(): return lax.ppermute(value, 'col', pairs)]
    pallas_call x1 -> x4, Pallas kernels: 5.76 us -> 6.32 us  [the longest x1 2.03 us: blocks(): pl.pallas_call(second_kernel, out_shape=TOTAL, in_specs=[SMEM] + [VMEM] *...]
  transfers between devices with their start and end apart: 14 -> 14, of which waited for: 10 -> 9; matrix products, arithmetic and copies ran while one was open for 0% -> 0% of each run, Pallas kernels for 4% -> 12%
where the time goes in v3:
time: 66.5 us; the launch traced here: 66.7 us
  starting transfers between devices  28.7 us (43%)
  waiting for transfers between devices  26.1 us (39%)
  Pallas kernels  10.6 us (16%)
  other arithmetic  1.07 us (2%)
    ppermute x7, waiting for transfers between devices, along_z(): return lax.ppermute(value, 'col', pairs)  16 us
    ppermute x7, starting transfers between devices, along_z(): return lax.ppermute(value, 'col', pairs)  15.6 us
    ppermute x6, starting transfers between devices, hop(): return lax.ppermute(value, ('row', 'col'), pairs)  9.59 us
    ppermute x6, waiting for transfers between devices, hop(): return lax.ppermute(value, ('row', 'col'), pairs)  8.98 us
    ppermute x1, starting transfers between devices, other_core(): return lax.ppermute(value, 'col', [(d, d ^ 1) for d in range(NZ * NCORE)])  3.5 us
    pallas_call x1, Pallas kernels, prepare(): pl.pallas_call(prepare_kernel, out_shape=(pltpu.VMEM((NB, LEAF, 2 * RMAX)...  2.99 us
    pallas_call x1, Pallas kernels, blocks(): pl.pallas_call(second_kernel, out_shape=TOTAL, in_specs=[SMEM] + [VMEM] *...  2.03 us
    pallas_call x1, Pallas kernels, blocks(): pl.pallas_call(first_kernel, out_shape=TOTAL, in_specs=[SMEM] + [VMEM] *...  1.67 us
  transfers between devices with their start and end apart: 14, of which 9 were waited for; matrix products, arithmetic and copies ran while one was open for 0% of the time, Pallas kernels for 12%

profile of v3, /device:TPU:1, one launch (start us, length us, event | category | flops | bytes accessed | tf_op | source)
XLA Modules:
  0.0 66.7 jit_solution(9043827911057331523)
XLA Ops:
  0.0 0.0 copy-start
  0.0 1.3 %shard_map.101.refs_0_ = bf16[256,256]{1,0:T(8,128)(2,1)S(1)} custom-call(s32[2,128]{1,0:T(2,128)} %perm_hbm.1, bf16[256,256]{1,0:T(8,128)(2,1)} %x_hbm.1), custom_call_target="tpu_custom_call" | custom-call | tf_op jit(solution)/shard_map/pallas_call | solution.py:90
  1.3 3.8 %collective-permute-start.2 = (bf16[256,256]{1,0:T(8,128)(2,1)S(1)}, bf16[256,256]{1,0:T(8,128)(2,1)S(1)}, u32[]{:S(2)}, u32[]{:S(2)}) collective-permute-start(bf16[256,256]{1,0:T(8,128)(2,1)S(1)} %shard_map.101.refs_0_), channel_id=1, source_target_pairs={{0,128},{1,33},{2,130},{3,35},{4,132},{5,37},{6,134},{7,39},{8,136... | collective-permute-start | bytes 393224 | tf_op jit(solution)/shard_map/ppermute | solution.py:51
  5.1 0.8 %collective-permute-start.1 = (bf16[256,256]{1,0:T(8,128)(2,1)S(1)}, bf16[256,256]{1,0:T(8,128)(2,1)S(1)}, u32[]{:S(2)}, u32[]{:S(2)}) collective-permute-start(bf16[256,256]{1,0:T(8,128)(2,1)S(1)} %shard_map.101.refs_0_), channel_id=1, source_target_pairs={{0,192},{1,49},{2,194},{3,51},{4,196},{5,53},{6,198},{7,55},{8,200... | collective-permute-start | bytes 393224 | tf_op jit(solution)/shard_map/ppermute | solution.py:51
  5.9 0.7 %collective-permute-start = (bf16[256,256]{1,0:T(8,128)(2,1)S(1)}, bf16[256,256]{1,0:T(8,128)(2,1)S(1)}, u32[]{:S(2)}, u32[]{:S(2)}) collective-permute-start(bf16[256,256]{1,0:T(8,128)(2,1)S(1)} %shard_map.101.refs_0_), channel_id=1, source_target_pairs={{0,64},{1,17},{2,66},{3,19},{4,68},{5,21},{6,70},{7,23},{8,72},{9,... | collective-permute-start | bytes 393224 | tf_op jit(solution)/shard_map/ppermute | solution.py:51
  6.6 0.9 %collective-permute-done.2.refs_3_ = bf16[256,256]{1,0:T(8,128)(2,1)S(1)} collective-permute-done((bf16[256,256]{1,0:T(8,128)(2,1)S(1)}, bf16[256,256]{1,0:T(8,128)(2,1)S(1)}, u32[]{:S(2)}, u32[]{:S(2)}) %collective-permute-start.2) | collective-permute-done | bytes 131104 | tf_op jit(solution)/shard_map/ppermute | solution.py:51
  7.5 2.1 %collective-permute-done.1.refs_2_ = bf16[256,256]{1,0:T(8,128)(2,1)S(1)} collective-permute-done((bf16[256,256]{1,0:T(8,128)(2,1)S(1)}, bf16[256,256]{1,0:T(8,128)(2,1)S(1)}, u32[]{:S(2)}, u32[]{:S(2)}) %collective-permute-start.1) | collective-permute-done | bytes 131104 | tf_op jit(solution)/shard_map/ppermute | solution.py:51
  9.6 1.4 %collective-permute-done.refs_1_ = bf16[256,256]{1,0:T(8,128)(2,1)S(1)} collective-permute-done((bf16[256,256]{1,0:T(8,128)(2,1)S(1)}, bf16[256,256]{1,0:T(8,128)(2,1)S(1)}, u32[]{:S(2)}, u32[]{:S(2)}) %collective-permute-start) | collective-permute-done | bytes 131104 | tf_op jit(solution)/shard_map/ppermute | solution.py:51
  11.0 2.8 %collective-permute-start.5 = (bf16[1024,256]{1,0:T(8,128)(2,1)S(1)}, bf16[1024,256]{1,0:T(8,128)(2,1)S(1)}, u32[]{:S(2)}, u32[]{:S(2)}) collective-permute-start(bf16[1024,256]{1,0:T(8,128)(2,1)S(1)} %shard_map.102.piece), channel_id=1, source_target_pairs={{0,32},{1,129},{2,34},{3,131},{4,36},{5,133},{6,38},{7,135},{8,40}... | collective-permute-start | bytes 1572872 | tf_op jit(solution)/shard_map/ppermute | solution.py:51
  13.8 0.9 %collective-permute-start.4 = (bf16[1024,256]{1,0:T(8,128)(2,1)S(1)}, bf16[1024,256]{1,0:T(8,128)(2,1)S(1)}, u32[]{:S(2)}, u32[]{:S(2)}) collective-permute-start(bf16[1024,256]{1,0:T(8,128)(2,1)S(1)} %shard_map.102.piece), channel_id=1, source_target_pairs={{0,48},{1,193},{2,50},{3,195},{4,52},{5,197},{6,54},{7,199},{8,56}... | collective-permute-start | bytes 1572872 | tf_op jit(solution)/shard_map/ppermute | solution.py:51
  14.6 0.6 collective-permute-start.3
  15.3 3.0 %shard_map.100 = (bf16[32,128,128]{2,1,0:T(8,128)(2,1)S(1)}, bf16[32,64,256]{2,1,0:T(8,128)(2,1)S(1)}, s32[296]{0:T(512)S(4)}) custom-call(s32[32]{0:T(128)} %rank_hbm.1, s32[32]{0:T(128)} %far_rows_hbm.1, s32[32]{0:T(128)} %far_cols_hbm.1, s32[28]{0:T(128)} %near_rows_hbm.1, s32[28]{0:T(128)} %near_cols_hbm.1, bf16[32,2,64,128]{3,2,1,0:T(8,128)(2,1)} %bitcast.48, ...), custom_call_target="tpu_custom_call" | custom-call | bytes 8388608 | tf_op jit(solution)/shard_map/pallas_call | solution.py:213
  18.2 0.0 copy-done
  18.3 1.7 %shard_map.103._ = f32[33,128,256]{2,1,0:T(8,128)S(1)} custom-call(s32[296]{0:T(512)S(4)} %get-tuple-element.11.lists, bf16[32,128,128]{2,1,0:T(8,128)(2,1)S(1)} %get-tuple-element.12.u_ref, bf16[32,64,256]{2,1,0:T(8,128)(2,1)S(1)} %get-tuple-element.13.v_ref, bf16[28,2,128,128]{3,2,1,0:T(8,128)(2,1)S(1)} %copy-done, bf16[1024,256]{1,0:T(8,128)(2,1)S(1)} %shard_map.102.piece), custom_call_target="tpu_custom_call" | custom-call | bytes 8388608 | tf_op jit(solution)/shard_map/pallas_call | solution.py:306
  19.9 1.0 %collective-permute-done.5.piece = bf16[1024,256]{1,0:T(8,128)(2,1)S(1)} collective-permute-done((bf16[1024,256]{1,0:T(8,128)(2,1)S(1)}, bf16[1024,256]{1,0:T(8,128)(2,1)S(1)}, u32[]{:S(2)}, u32[]{:S(2)}) %collective-permute-start.5) | collective-permute-done | bytes 524320 | tf_op jit(solution)/shard_map/ppermute | solution.py:51
  20.9 2.0 %shard_map.104._ = f32[33,128,256]{2,1,0:T(8,128)S(1)} custom-call(s32[296]{0:T(512)S(4)} %get-tuple-element.11.lists, bf16[32,128,128]{2,1,0:T(8,128)(2,1)S(1)} %get-tuple-element.12.u_ref, bf16[32,64,256]{2,1,0:T(8,128)(2,1)S(1)} %get-tuple-element.13.v_ref, bf16[28,2,128,128]{3,2,1,0:T(8,128)(2,1)S(1)} %copy-done, ...), custom_call_target="tpu_custom_call", output_to_operand_aliasing={{}: (5, {})} | custom-call | bytes 6291456 | tf_op jit(solution)/shard_map/pallas_call | solution.py:315
  23.0 3.7 %collective-permute-done.4.back = bf16[1024,256]{1,0:T(8,128)(2,1)S(1)} collective-permute-done((bf16[1024,256]{1,0:T(8,128)(2,1)S(1)}, bf16[1024,256]{1,0:T(8,128)(2,1)S(1)}, u32[]{:S(2)}, u32[]{:S(2)}) %collective-permute-start.4) | collective-permute-done | bytes 524320 | tf_op jit(solution)/shard_map/ppermute | solution.py:51
  26.6 0.0 collective-permute-done.3.ahead
  26.6 1.6 %shard_map.105 = (f32[33,128,256]{2,1,0:T(8,128)S(1)}, bf16[16,256,256]{2,1,0:T(8,128)(2,1)S(1)}, bf16[2048,256]{1,0:T(8,128)(2,1)S(1)}) custom-call(s32[296]{0:T(512)S(4)} %get-tuple-element.11.lists, bf16[32,128,128]{2,1,0:T(8,128)(2,1)S(1)} %get-tuple-element.12.u_ref, ...), custom_call_target="tpu_custom_call", output_to_operand_aliasing={{0}: (6, {})} | custom-call | bytes 8388608 | tf_op jit(solution)/shard_map/pallas_call | solution.py:325
  28.2 3.5 %collective-permute-start.6 = (bf16[2048,256]{1,0:T(8,128)(2,1)S(1)}, bf16[2048,256]{1,0:T(8,128)(2,1)S(1)}, u32[]{:S(2)}, u32[]{:S(2)}) collective-permute-start(bf16[2048,256]{1,0:T(8,128)(2,1)S(1)} %get-tuple-element.16), channel_id=1, source_target_pairs={{0,1},{1,0},{2,3},{3,2},{4,5},{5,4},{6,7},{7,6},{8,9},{9,8},{10,11... | collective-permute-start | bytes 3145736 | tf_op jit(solution)/shard_map/ppermute | solution.py:62
  31.7 1.0 %shard_map.106 = f32[33,128,256]{2,1,0:T(8,128)S(1)} custom-call(s32[296]{0:T(512)S(4)} %get-tuple-element.11.lists, bf16[32,128,128]{2,1,0:T(8,128)(2,1)S(1)} %get-tuple-element.12.u_ref, bf16[32,64,256]{2,1,0:T(8,128)(2,1)S(1)} %get-tuple-element.13.v_ref, bf16[28,2,128,128]{3,2,1,0:T(8,128)(2,1)S(1)} %copy-done, ...), custom_call_target="tpu_custom_call", output_to_operand_aliasing={{}: (5, {})} | custom-call | bytes 6291456 | tf_op jit(solution)/shard_map/pallas_call | solution.py:338
  32.8 0.2 fusion.15
  32.9 1.0 %collective-permute-done.6 = bf16[2048,256]{1,0:T(8,128)(2,1)S(1)} collective-permute-done((bf16[2048,256]{1,0:T(8,128)(2,1)S(1)}, bf16[2048,256]{1,0:T(8,128)(2,1)S(1)}, u32[]{:S(2)}, u32[]{:S(2)}) %collective-permute-start.6) | collective-permute-done | bytes 1048608 | tf_op jit(solution)/shard_map/ppermute | solution.py:62
  34.0 0.2 fusion.6
  34.2 7.2 %collective-permute-start.7 = (bf16[256,256]{1,0:T(8,128)(2,1)S(1)}, bf16[256,256]{1,0:T(8,128)(2,1)S(1)}, u32[]{:S(2)}, u32[]{:S(2)}) collective-permute-start(bf16[256,256]{1,0:T(8,128)(2,1)S(1)} %get-tuple-element.25), channel_id=1, source_target_pairs={{0,8},{1,9},{2,10},{3,11},{4,12},{5,13},{6,14},{7,15},{8,0},{9,1},... | collective-permute-start | bytes 393224 | tf_op jit(solution)/shard_map/ppermute | solution.py:58
  41.5 1.4 %collective-permute-start.13 = (bf16[256,256]{1,0:T(8,128)(2,1)S(1)}, bf16[256,256]{1,0:T(8,128)(2,1)S(1)}, u32[]{:S(2)}, u32[]{:S(2)}) collective-permute-start(bf16[256,256]{1,0:T(8,128)(2,1)S(1)} %get-tuple-element.26), channel_id=1, source_target_pairs={{0,6},{1,7},{2,8},{3,9},{4,10},{5,11},{6,12},{7,13},{8,14},{9,15},... | collective-permute-start | bytes 393224 | tf_op jit(solution)/shard_map/ppermute | solution.py:58
  42.9 3.1 %collective-permute-start.12 = (bf16[256,256]{1,0:T(8,128)(2,1)S(1)}, bf16[256,256]{1,0:T(8,128)(2,1)S(1)}, u32[]{:S(2)}, u32[]{:S(2)}) collective-permute-start(bf16[256,256]{1,0:T(8,128)(2,1)S(1)} %get-tuple-element.27), channel_id=1, source_target_pairs={{0,10},{1,11},{2,12},{3,13},{4,14},{5,15},{6,0},{7,1},{8,2},{9,3},... | collective-permute-start | bytes 393224 | tf_op jit(solution)/shard_map/ppermute | solution.py:58
  46.0 1.7 %collective-permute-start.11 = (bf16[256,256]{1,0:T(8,128)(2,1)S(1)}, bf16[256,256]{1,0:T(8,128)(2,1)S(1)}, u32[]{:S(2)}, u32[]{:S(2)}) collective-permute-start(bf16[256,256]{1,0:T(8,128)(2,1)S(1)} %get-tuple-element.28), channel_id=1, source_target_pairs={{0,4},{1,5},{2,6},{3,7},{4,8},{5,9},{6,10},{7,11},{8,12},{9,13},{1... | collective-permute-start | bytes 393224 | tf_op jit(solution)/shard_map/ppermute | solution.py:58
  47.7 1.8 %collective-permute-start.10 = (bf16[256,256]{1,0:T(8,128)(2,1)S(1)}, bf16[256,256]{1,0:T(8,128)(2,1)S(1)}, u32[]{:S(2)}, u32[]{:S(2)}) collective-permute-start(bf16[256,256]{1,0:T(8,128)(2,1)S(1)} %get-tuple-element.29), channel_id=1, source_target_pairs={{0,12},{1,13},{2,14},{3,15},{4,0},{5,1},{6,2},{7,3},{8,4},{9,5},{1... | collective-permute-start | bytes 393224 | tf_op jit(solution)/shard_map/ppermute | solution.py:58
  49.5 0.0 collective-permute-done.7
  49.6 0.1 collective-permute-start.9
  49.6 9.5 %collective-permute-done.13 = bf16[256,256]{1,0:T(8,128)(2,1)S(1)} collective-permute-done((bf16[256,256]{1,0:T(8,128)(2,1)S(1)}, bf16[256,256]{1,0:T(8,128)(2,1)S(1)}, u32[]{:S(2)}, u32[]{:S(2)}) %collective-permute-start.13) | collective-permute-done | bytes 131104 | tf_op jit(solution)/shard_map/ppermute | solution.py:58
  59.1 0.2 collective-permute-start.8
  59.3 0.0 collective-permute-done.12
  59.3 0.0 collective-permute-done.11
  59.3 1.9 %collective-permute-done.10 = bf16[256,256]{1,0:T(8,128)(2,1)S(1)} collective-permute-done((bf16[256,256]{1,0:T(8,128)(2,1)S(1)}, bf16[256,256]{1,0:T(8,128)(2,1)S(1)}, u32[]{:S(2)}, u32[]{:S(2)}) %collective-permute-start.10) | collective-permute-done | bytes 131104 | tf_op jit(solution)/shard_map/ppermute | solution.py:58
  61.2 4.7 %collective-permute-done.9 = bf16[256,256]{1,0:T(8,128)(2,1)S(1)} collective-permute-done((bf16[256,256]{1,0:T(8,128)(2,1)S(1)}, bf16[256,256]{1,0:T(8,128)(2,1)S(1)}, u32[]{:S(2)}, u32[]{:S(2)}) %collective-permute-start.9) | collective-permute-done | bytes 131104 | tf_op jit(solution)/shard_map/ppermute | solution.py:58
  65.9 0.0 collective-permute-done.8
  65.9 0.8 %fusion.14 = bf16[256,256]{1,0:T(8,128)(2,1)} fusion(f32[2,128,256]{2,1,0:T(8,128)S(1)} %get-tuple-element.24, bf16[256,256]{1,0:T(8,128)(2,1)S(1)} %collective-permute-done.13, bf16[256,256]{1,0:T(8,128)(2,1)S(1)} %collective-permute-done.12, bf16[256,256]{1,0:T(8,128)(2,1)S(1)} %collective-permute-done.11, ...), kind=kLoop, calls=%fused_computation.22 | loop fusion | flops 1114112 | bytes 1441792 | tf_op jit(solution)/shard_map/convert_element_type | solution.py:384
  (1 shorter events, 0.0 us)
Async XLA Ops:
  0.0 18.2 %copy-start = (bf16[28,2,128,128]{3,2,1,0:T(8,128)(2,1)S(1)}, bf16[28,2,128,128]{3,2,1,0:T(8,128)(2,1)}, u32[]{:S(2)}) copy-start(bf16[28,2,128,128]{3,2,1,0:T(8,128)(2,1)} %near_ref.7) | copy-start | bytes 5505028
  1.3 6.2 %collective-permute-start.2 = (bf16[256,256]{1,0:T(8,128)(2,1)S(1)}, bf16[256,256]{1,0:T(8,128)(2,1)S(1)}, u32[]{:S(2)}, u32[]{:S(2)}) collective-permute-start(bf16[256,256]{1,0:T(8,128)(2,1)S(1)} %shard_map.101.refs_0_), channel_id=1, source_target_pairs={{0,128},{1,33},{2,130},{3,35},{4,132},{5,37},{6,134},{7,39},{8,136... | collective-permute-start | bytes 393224 | tf_op jit(solution)/shard_map/ppermute | solution.py:51
  5.1 4.4 %collective-permute-start.1 = (bf16[256,256]{1,0:T(8,128)(2,1)S(1)}, bf16[256,256]{1,0:T(8,128)(2,1)S(1)}, u32[]{:S(2)}, u32[]{:S(2)}) collective-permute-start(bf16[256,256]{1,0:T(8,128)(2,1)S(1)} %shard_map.101.refs_0_), channel_id=1, source_target_pairs={{0,192},{1,49},{2,194},{3,51},{4,196},{5,53},{6,198},{7,55},{8,200... | collective-permute-start | bytes 393224 | tf_op jit(solution)/shard_map/ppermute | solution.py:51
  5.9 5.0 %collective-permute-start = (bf16[256,256]{1,0:T(8,128)(2,1)S(1)}, bf16[256,256]{1,0:T(8,128)(2,1)S(1)}, u32[]{:S(2)}, u32[]{:S(2)}) collective-permute-start(bf16[256,256]{1,0:T(8,128)(2,1)S(1)} %shard_map.101.refs_0_), channel_id=1, source_target_pairs={{0,64},{1,17},{2,66},{3,19},{4,68},{5,21},{6,70},{7,23},{8,72},{9,... | collective-permute-start | bytes 393224 | tf_op jit(solution)/shard_map/ppermute | solution.py:51
  11.0 10.0 %collective-permute-start.5 = (bf16[1024,256]{1,0:T(8,128)(2,1)S(1)}, bf16[1024,256]{1,0:T(8,128)(2,1)S(1)}, u32[]{:S(2)}, u32[]{:S(2)}) collective-permute-start(bf16[1024,256]{1,0:T(8,128)(2,1)S(1)} %shard_map.102.piece), channel_id=1, source_target_pairs={{0,32},{1,129},{2,34},{3,131},{4,36},{5,133},{6,38},{7,135},{8,40}... | collective-permute-start | bytes 1572872 | tf_op jit(solution)/shard_map/ppermute | solution.py:51
  13.8 12.8 %collective-permute-start.4 = (bf16[1024,256]{1,0:T(8,128)(2,1)S(1)}, bf16[1024,256]{1,0:T(8,128)(2,1)S(1)}, u32[]{:S(2)}, u32[]{:S(2)}) collective-permute-start(bf16[1024,256]{1,0:T(8,128)(2,1)S(1)} %shard_map.102.piece), channel_id=1, source_target_pairs={{0,48},{1,193},{2,50},{3,195},{4,52},{5,197},{6,54},{7,199},{8,56}... | collective-permute-start | bytes 1572872 | tf_op jit(solution)/shard_map/ppermute | solution.py:51
  14.6 12.0 %collective-permute-start.3 = (bf16[1024,256]{1,0:T(8,128)(2,1)S(1)}, bf16[1024,256]{1,0:T(8,128)(2,1)S(1)}, u32[]{:S(2)}, u32[]{:S(2)}) collective-permute-start(bf16[1024,256]{1,0:T(8,128)(2,1)S(1)} %shard_map.102.piece), channel_id=1, source_target_pairs={{0,16},{1,65},{2,18},{3,67},{4,20},{5,69},{6,22},{7,71},{8,24},{9,... | collective-permute-start | bytes 1572872 | tf_op jit(solution)/shard_map/ppermute | solution.py:51
  28.2 5.8 %collective-permute-start.6 = (bf16[2048,256]{1,0:T(8,128)(2,1)S(1)}, bf16[2048,256]{1,0:T(8,128)(2,1)S(1)}, u32[]{:S(2)}, u32[]{:S(2)}) collective-permute-start(bf16[2048,256]{1,0:T(8,128)(2,1)S(1)} %get-tuple-element.16), channel_id=1, source_target_pairs={{0,1},{1,0},{2,3},{3,2},{4,5},{5,4},{6,7},{7,6},{8,9},{9,8},{10,11... | collective-permute-start | bytes 3145736 | tf_op jit(solution)/shard_map/ppermute | solution.py:62
  34.2 15.3 %collective-permute-start.7 = (bf16[256,256]{1,0:T(8,128)(2,1)S(1)}, bf16[256,256]{1,0:T(8,128)(2,1)S(1)}, u32[]{:S(2)}, u32[]{:S(2)}) collective-permute-start(bf16[256,256]{1,0:T(8,128)(2,1)S(1)} %get-tuple-element.25), channel_id=1, source_target_pairs={{0,8},{1,9},{2,10},{3,11},{4,12},{5,13},{6,14},{7,15},{8,0},{9,1},... | collective-permute-start | bytes 393224 | tf_op jit(solution)/shard_map/ppermute | solution.py:58
  41.5 17.6 %collective-permute-start.13 = (bf16[256,256]{1,0:T(8,128)(2,1)S(1)}, bf16[256,256]{1,0:T(8,128)(2,1)S(1)}, u32[]{:S(2)}, u32[]{:S(2)}) collective-permute-start(bf16[256,256]{1,0:T(8,128)(2,1)S(1)} %get-tuple-element.26), channel_id=1, source_target_pairs={{0,6},{1,7},{2,8},{3,9},{4,10},{5,11},{6,12},{7,13},{8,14},{9,15},... | collective-permute-start | bytes 393224 | tf_op jit(solution)/shard_map/ppermute | solution.py:58
  42.9 16.4 %collective-permute-start.12 = (bf16[256,256]{1,0:T(8,128)(2,1)S(1)}, bf16[256,256]{1,0:T(8,128)(2,1)S(1)}, u32[]{:S(2)}, u32[]{:S(2)}) collective-permute-start(bf16[256,256]{1,0:T(8,128)(2,1)S(1)} %get-tuple-element.27), channel_id=1, source_target_pairs={{0,10},{1,11},{2,12},{3,13},{4,14},{5,15},{6,0},{7,1},{8,2},{9,3},... | collective-permute-start | bytes 393224 | tf_op jit(solution)/shard_map/ppermute | solution.py:58
  46.0 13.4 %collective-permute-start.11 = (bf16[256,256]{1,0:T(8,128)(2,1)S(1)}, bf16[256,256]{1,0:T(8,128)(2,1)S(1)}, u32[]{:S(2)}, u32[]{:S(2)}) collective-permute-start(bf16[256,256]{1,0:T(8,128)(2,1)S(1)} %get-tuple-element.28), channel_id=1, source_target_pairs={{0,4},{1,5},{2,6},{3,7},{4,8},{5,9},{6,10},{7,11},{8,12},{9,13},{1... | collective-permute-start | bytes 393224 | tf_op jit(solution)/shard_map/ppermute | solution.py:58
  47.7 13.5 %collective-permute-start.10 = (bf16[256,256]{1,0:T(8,128)(2,1)S(1)}, bf16[256,256]{1,0:T(8,128)(2,1)S(1)}, u32[]{:S(2)}, u32[]{:S(2)}) collective-permute-start(bf16[256,256]{1,0:T(8,128)(2,1)S(1)} %get-tuple-element.29), channel_id=1, source_target_pairs={{0,12},{1,13},{2,14},{3,15},{4,0},{5,1},{6,2},{7,3},{8,4},{9,5},{1... | collective-permute-start | bytes 393224 | tf_op jit(solution)/shard_map/ppermute | solution.py:58
  49.6 16.3 %collective-permute-start.9 = (bf16[256,256]{1,0:T(8,128)(2,1)S(1)}, bf16[256,256]{1,0:T(8,128)(2,1)S(1)}, u32[]{:S(2)}, u32[]{:S(2)}) collective-permute-start(bf16[256,256]{1,0:T(8,128)(2,1)S(1)} %get-tuple-element.30), channel_id=1, source_target_pairs={{0,2},{1,3},{2,4},{3,5},{4,6},{5,7},{6,8},{7,9},{8,10},{9,11},{10,... | collective-permute-start | bytes 393224 | tf_op jit(solution)/shard_map/ppermute | solution.py:58
  59.1 6.8 %collective-permute-start.8 = (bf16[256,256]{1,0:T(8,128)(2,1)S(1)}, bf16[256,256]{1,0:T(8,128)(2,1)S(1)}, u32[]{:S(2)}, u32[]{:S(2)}) collective-permute-start(bf16[256,256]{1,0:T(8,128)(2,1)S(1)} %get-tuple-element.31), channel_id=1, source_target_pairs={{0,14},{1,15},{2,0},{3,1},{4,2},{5,3},{6,4},{7,5},{8,6},{9,7},{10,... | collective-permute-start | bytes 393224 | tf_op jit(solution)/shard_map/ppermute | solution.py:58

commit v4 on v3

--- a/solution.py
+++ b/solution.py
@@ -20,8 +20,6 @@
 GROUPS = 4
 LIST = 36
 COUNTS = 2 * GROUPS * LIST
-ORDER_OF_STEP = 0x13506427
-STEPS = (4, 7, 1, 6, 2, 5, 3, 0)
 F32 = jnp.float32
 BF16 = jnp.bfloat16
 VMEM = pl.BlockSpec(memory_space=pltpu.VMEM)
@@ -51,10 +49,12 @@
     return lax.ppermute(value, ("row", "col"), pairs)
 
 
-def along_z(step, value):
-    pairs = [
-        (z * NCORE + c, (z + step) % NZ * NCORE + c) for z in range(NZ) for c in range(NCORE)
-    ]
+def along_z(step, value, turn=0):
+    pairs = []
+    for d in range(NZ * NCORE):
+        z, c = divmod(d, NCORE)
+        z = (z + step * (1 - 2 * c)) % NZ
+        pairs.append((d, z * NCORE + (c + turn) % NCORE))
     return lax.ppermute(value, "col", pairs)
 
 
@@ -160,9 +160,14 @@
         dy = gray((my_y - (r & 3)) & 3)
         piece = jnp.where(my_core == 0, dy, dx)
         place = jnp.where(my_core == 0, dx, dy) * 2 + (k & 1)
+        i, owner = row & 1, (row >> 1) & 1
         dz = (((row & (SLAB - 1)) >> 2) - my_z) & 7
-        own = 1 - (((row >> 1) & 1) ^ my_core)
-        target = own * 16 + ((ORDER_OF_STEP >> (dz * 4)) & 15) * 2 + (row & 1)
+        straight = (dz & 3) == 0
+        handler = jnp.where(straight, owner, dz >> 2)
+        steps = jnp.where(handler == 0, dz, 8 - dz)
+        near = jnp.where(straight, 14 - 14 * (dz >> 2) + i, 14 - 4 * steps + owner * 2 + i)
+        own = jnp.where(handler == my_core, 1, 0)
+        target = own * 16 + near
         late = (piece == 1) | (piece == 2)
         group = jnp.where(late, 2 + own, jnp.where(piece == 0, 0, 1))
         slot = jnp.where(piece == 2, 8 + place, place)
@@ -354,6 +359,48 @@
     return [first, ahead, back, two]
 
 
+def chip_sum(own, swapped, first, count):
+    mine = own[SLAB // 2 + first : SLAB // 2 + first + count].reshape(count * LEAF, COLS)
+    return mine + swapped[first * LEAF : (first + count) * LEAF].astype(F32)
+
+
+def cluster(k):
+    return pl.ds(pl.multiple_of(k * LEAF, LEAF), LEAF)
+
+
+def relay_kernel(own, swapped, close, middle, same_ref, cross_ref):
+    core = position()[3]
+    for owner, out in ((core, same_ref), (1 - core, cross_ref)):
+        for i in range(2):
+            place = owner * 2 + i
+
+            total = own[SLAB // 2 + 10 + place] + swapped[cluster(10 + place), :].astype(F32)
+            total += close[cluster(place), :].astype(F32) + middle[cluster(2 + place), :].astype(F32)
+            out[i * LEAF : (i + 1) * LEAF, :] = total.astype(BF16)
+
+
+def relay(own, swapped, close, middle):
+    shape = pltpu.VMEM((2 * LEAF, COLS), BF16)
+    return pl.pallas_call(
+        relay_kernel,
+        out_shape=(shape, shape),
+        in_specs=[VMEM] * 4,
+        out_specs=(VMEM, VMEM),
+        compiler_params=limit(4),
+    )(own, swapped, close, middle)
+
+
+def scatter(swapped, own):
+    middle = along_z(2, chip_sum(own, swapped, 0, 6).astype(BF16))
+    close = along_z(1, chip_sum(own, swapped, 6, 4).astype(BF16))
+    same, cross = relay(own, swapped, close, middle)
+    far = after(middle[: 2 * LEAF], same)
+    same, cross = along_z(1, same), along_z(1, cross, 1)
+    far = along_z(2, far)
+    total = chip_sum(own, swapped, 14, 2) + far.astype(F32)
+    return (total + same.astype(F32) + cross.astype(F32)).astype(BF16)
+
+
 def body(
     incident, perm, far_u, far_v, far_rank, far_rows, far_cols, near_block, near_rows, near_cols
 ):
@@ -369,19 +416,7 @@
     )
     pieces = gather(mine)
     other, own = blocks((lists, u, v, near_block), pieces)
-    swapped = other_core(other)
-    total, parts = None, []
-    for j, step in enumerate(STEPS):
-        rows = slice(j * 2 * LEAF, (j + 1) * 2 * LEAF)
-        mine = own[SLAB // 2 + 2 * j : SLAB // 2 + 2 * j + 2].reshape(2 * LEAF, COLS)
-        chip = mine + swapped[rows].astype(F32)
-        if step == 0:
-            total = chip
-        else:
-            parts.append(along_z(step, chip.astype(BF16)))
-    for part in parts:
-        total = total + part.astype(F32)
-    return total.astype(BF16)
+    return scatter(other_core(other), own)
 
 
 def solution(mesh):

time: 66.5 us -> 63.2 us (0.950); the launches traced: 66.7 us -> 62.6 us
  starting transfers between devices: 28.7 us -> 25 us
    ppermute x7 -> x5, starting transfers between devices: 15.6 us -> 11.7 us  [along_z(): return lax.ppermute(value, 'col', pairs)]
    ppermute x7 -> x5, waiting for transfers between devices: 16 us -> 15.2 us  [along_z(): return lax.ppermute(value, 'col', pairs)]
  transfers between devices with their start and end apart: 14 -> 12, of which waited for: 9 -> 10; matrix products, arithmetic and copies ran while one was open for 0% -> 0% of each run, Pallas kernels for 12% -> 12%
where the time goes in v4:
time: 63.2 us; the launch traced here: 62.6 us
  waiting for transfers between devices  25.6 us (41%)
  starting transfers between devices  25 us (40%)
  Pallas kernels  10.8 us (17%)
  other arithmetic  0.87 us (1%)
    ppermute x5, waiting for transfers between devices, along_z(): return lax.ppermute(value, 'col', pairs)  15.2 us
    ppermute x5, starting transfers between devices, along_z(): return lax.ppermute(value, 'col', pairs)  11.7 us
    ppermute x6, starting transfers between devices, hop(): return lax.ppermute(value, ('row', 'col'), pairs)  9.59 us
    ppermute x6, waiting for transfers between devices, hop(): return lax.ppermute(value, ('row', 'col'), pairs)  9.27 us
    ppermute x1, starting transfers between devices, other_core(): return lax.ppermute(value, 'col', [(d, d ^ 1) for d in range(NZ * NCORE)])  3.75 us
    pallas_call x1, Pallas kernels, prepare(): pl.pallas_call(prepare_kernel, out_shape=(pltpu.VMEM((NB, LEAF, 2 * RMAX)...  3.12 us
    pallas_call x1, Pallas kernels, blocks(): pl.pallas_call(third_kernel, out_shape=(TOTAL, pltpu.VMEM((16, 2 * LEAF,...  1.97 us
    pallas_call x1, Pallas kernels, blocks(): pl.pallas_call(first_kernel, out_shape=TOTAL, in_specs=[SMEM] + [VMEM] *...  1.66 us
  transfers between devices with their start and end apart: 12, of which 10 were waited for; matrix products, arithmetic and copies ran while one was open for 0% of the time, Pallas kernels for 12%

profile of v4, /device:TPU:1, one launch (start us, length us, event | category | flops | bytes accessed | tf_op | source)
XLA Modules:
  0.0 62.6 jit_solution(17294951807447802749)
XLA Ops:
  0.0 0.0 copy-start
  0.0 1.3 %shard_map.101.refs_0_ = bf16[256,256]{1,0:T(8,128)(2,1)S(1)} custom-call(s32[2,128]{1,0:T(2,128)} %perm_hbm.1, bf16[256,256]{1,0:T(8,128)(2,1)} %x_hbm.1), custom_call_target="tpu_custom_call" | custom-call | tf_op jit(solution)/shard_map/pallas_call | solution.py:90
  1.3 3.8 %collective-permute-start.2 = (bf16[256,256]{1,0:T(8,128)(2,1)S(1)}, bf16[256,256]{1,0:T(8,128)(2,1)S(1)}, u32[]{:S(2)}, u32[]{:S(2)}) collective-permute-start(bf16[256,256]{1,0:T(8,128)(2,1)S(1)} %shard_map.101.refs_0_), channel_id=1, source_target_pairs={{0,128},{1,33},{2,130},{3,35},{4,132},{5,37},{6,134},{7,39},{8,136... | collective-permute-start | bytes 393224 | tf_op jit(solution)/shard_map/ppermute | solution.py:49
  5.1 0.8 %collective-permute-start.1 = (bf16[256,256]{1,0:T(8,128)(2,1)S(1)}, bf16[256,256]{1,0:T(8,128)(2,1)S(1)}, u32[]{:S(2)}, u32[]{:S(2)}) collective-permute-start(bf16[256,256]{1,0:T(8,128)(2,1)S(1)} %shard_map.101.refs_0_), channel_id=1, source_target_pairs={{0,192},{1,49},{2,194},{3,51},{4,196},{5,53},{6,198},{7,55},{8,200... | collective-permute-start | bytes 393224 | tf_op jit(solution)/shard_map/ppermute | solution.py:49
  5.9 0.7 %collective-permute-start = (bf16[256,256]{1,0:T(8,128)(2,1)S(1)}, bf16[256,256]{1,0:T(8,128)(2,1)S(1)}, u32[]{:S(2)}, u32[]{:S(2)}) collective-permute-start(bf16[256,256]{1,0:T(8,128)(2,1)S(1)} %shard_map.101.refs_0_), channel_id=1, source_target_pairs={{0,64},{1,17},{2,66},{3,19},{4,68},{5,21},{6,70},{7,23},{8,72},{9,... | collective-permute-start | bytes 393224 | tf_op jit(solution)/shard_map/ppermute | solution.py:49
  6.6 0.9 %collective-permute-done.2.refs_3_ = bf16[256,256]{1,0:T(8,128)(2,1)S(1)} collective-permute-done((bf16[256,256]{1,0:T(8,128)(2,1)S(1)}, bf16[256,256]{1,0:T(8,128)(2,1)S(1)}, u32[]{:S(2)}, u32[]{:S(2)}) %collective-permute-start.2) | collective-permute-done | bytes 131104 | tf_op jit(solution)/shard_map/ppermute | solution.py:49
  7.5 2.1 %collective-permute-done.1.refs_2_ = bf16[256,256]{1,0:T(8,128)(2,1)S(1)} collective-permute-done((bf16[256,256]{1,0:T(8,128)(2,1)S(1)}, bf16[256,256]{1,0:T(8,128)(2,1)S(1)}, u32[]{:S(2)}, u32[]{:S(2)}) %collective-permute-start.1) | collective-permute-done | bytes 131104 | tf_op jit(solution)/shard_map/ppermute | solution.py:49
  9.6 1.4 %collective-permute-done.refs_1_ = bf16[256,256]{1,0:T(8,128)(2,1)S(1)} collective-permute-done((bf16[256,256]{1,0:T(8,128)(2,1)S(1)}, bf16[256,256]{1,0:T(8,128)(2,1)S(1)}, u32[]{:S(2)}, u32[]{:S(2)}) %collective-permute-start) | collective-permute-done | bytes 131104 | tf_op jit(solution)/shard_map/ppermute | solution.py:49
  11.0 2.8 %collective-permute-start.5 = (bf16[1024,256]{1,0:T(8,128)(2,1)S(1)}, bf16[1024,256]{1,0:T(8,128)(2,1)S(1)}, u32[]{:S(2)}, u32[]{:S(2)}) collective-permute-start(bf16[1024,256]{1,0:T(8,128)(2,1)S(1)} %shard_map.102.piece), channel_id=1, source_target_pairs={{0,32},{1,129},{2,34},{3,131},{4,36},{5,133},{6,38},{7,135},{8,40}... | collective-permute-start | bytes 1572872 | tf_op jit(solution)/shard_map/ppermute | solution.py:49
  13.8 0.9 %collective-permute-start.4 = (bf16[1024,256]{1,0:T(8,128)(2,1)S(1)}, bf16[1024,256]{1,0:T(8,128)(2,1)S(1)}, u32[]{:S(2)}, u32[]{:S(2)}) collective-permute-start(bf16[1024,256]{1,0:T(8,128)(2,1)S(1)} %shard_map.102.piece), channel_id=1, source_target_pairs={{0,48},{1,193},{2,50},{3,195},{4,52},{5,197},{6,54},{7,199},{8,56}... | collective-permute-start | bytes 1572872 | tf_op jit(solution)/shard_map/ppermute | solution.py:49
  14.6 0.6 collective-permute-start.3
  15.3 3.1 %shard_map.100 = (bf16[32,128,128]{2,1,0:T(8,128)(2,1)S(1)}, bf16[32,64,256]{2,1,0:T(8,128)(2,1)S(1)}, s32[296]{0:T(512)S(4)}) custom-call(s32[32]{0:T(128)} %rank_hbm.1, s32[32]{0:T(128)} %far_rows_hbm.1, s32[32]{0:T(128)} %far_cols_hbm.1, s32[28]{0:T(128)} %near_rows_hbm.1, s32[28]{0:T(128)} %near_cols_hbm.1, bf16[32,2,64,128]{3,2,1,0:T(8,128)(2,1)} %bitcast.20, ...), custom_call_target="tpu_custom_call" | custom-call | bytes 8388608 | tf_op jit(solution)/shard_map/pallas_call | solution.py:218
  18.4 0.0 copy-done
  18.4 1.7 %shard_map.103._ = f32[33,128,256]{2,1,0:T(8,128)S(1)} custom-call(s32[296]{0:T(512)S(4)} %get-tuple-element.14.lists, bf16[32,128,128]{2,1,0:T(8,128)(2,1)S(1)} %get-tuple-element.15.u_ref, bf16[32,64,256]{2,1,0:T(8,128)(2,1)S(1)} %get-tuple-element.16.v_ref, bf16[28,2,128,128]{3,2,1,0:T(8,128)(2,1)S(1)} %copy-done, bf16[1024,256]{1,0:T(8,128)(2,1)S(1)} %shard_map.102.piece), custom_call_target="tpu_custom_call" | custom-call | bytes 8388608 | tf_op jit(solution)/shard_map/pallas_call | solution.py:311
  20.1 0.9 %collective-permute-done.5.piece = bf16[1024,256]{1,0:T(8,128)(2,1)S(1)} collective-permute-done((bf16[1024,256]{1,0:T(8,128)(2,1)S(1)}, bf16[1024,256]{1,0:T(8,128)(2,1)S(1)}, u32[]{:S(2)}, u32[]{:S(2)}) %collective-permute-start.5) | collective-permute-done | bytes 524320 | tf_op jit(solution)/shard_map/ppermute | solution.py:49
  20.9 1.6 %shard_map.104._ = f32[33,128,256]{2,1,0:T(8,128)S(1)} custom-call(s32[296]{0:T(512)S(4)} %get-tuple-element.14.lists, bf16[32,128,128]{2,1,0:T(8,128)(2,1)S(1)} %get-tuple-element.15.u_ref, bf16[32,64,256]{2,1,0:T(8,128)(2,1)S(1)} %get-tuple-element.16.v_ref, bf16[28,2,128,128]{3,2,1,0:T(8,128)(2,1)S(1)} %copy-done, ...), custom_call_target="tpu_custom_call", output_to_operand_aliasing={{}: (5, {})} | custom-call | bytes 6291456 | tf_op jit(solution)/shard_map/pallas_call | solution.py:320
  22.5 4.1 %collective-permute-done.4.back = bf16[1024,256]{1,0:T(8,128)(2,1)S(1)} collective-permute-done((bf16[1024,256]{1,0:T(8,128)(2,1)S(1)}, bf16[1024,256]{1,0:T(8,128)(2,1)S(1)}, u32[]{:S(2)}, u32[]{:S(2)}) %collective-permute-start.4) | collective-permute-done | bytes 524320 | tf_op jit(solution)/shard_map/ppermute | solution.py:49
  26.6 0.0 collective-permute-done.3.ahead
  26.6 2.0 %shard_map.105 = (f32[33,128,256]{2,1,0:T(8,128)S(1)}, bf16[16,256,256]{2,1,0:T(8,128)(2,1)S(1)}, bf16[2048,256]{1,0:T(8,128)(2,1)S(1)}) custom-call(s32[296]{0:T(512)S(4)} %get-tuple-element.14.lists, bf16[32,128,128]{2,1,0:T(8,128)(2,1)S(1)} %get-tuple-element.15.u_ref, ...), custom_call_target="tpu_custom_call", output_to_operand_aliasing={{0}: (6, {})} | custom-call | bytes 8388608 | tf_op jit(solution)/shard_map/pallas_call | solution.py:330
  28.6 3.7 %collective-permute-start.6 = (bf16[2048,256]{1,0:T(8,128)(2,1)S(1)}, bf16[2048,256]{1,0:T(8,128)(2,1)S(1)}, u32[]{:S(2)}, u32[]{:S(2)}) collective-permute-start(bf16[2048,256]{1,0:T(8,128)(2,1)S(1)} %get-tuple-element.19), channel_id=1, source_target_pairs={{0,1},{1,0},{2,3},{3,2},{4,5},{5,4},{6,7},{7,6},{8,9},{9,8},{10,11... | collective-permute-start | bytes 3145736 | tf_op jit(solution)/shard_map/ppermute | solution.py:62
  32.4 1.0 %shard_map.106.own = f32[33,128,256]{2,1,0:T(8,128)S(1)} custom-call(s32[296]{0:T(512)S(4)} %get-tuple-element.14.lists, bf16[32,128,128]{2,1,0:T(8,128)(2,1)S(1)} %get-tuple-element.15.u_ref, bf16[32,64,256]{2,1,0:T(8,128)(2,1)S(1)} %get-tuple-element.16.v_ref, bf16[28,2,128,128]{3,2,1,0:T(8,128)(2,1)S(1)} %copy-done, ...), custom_call_target="tpu_custom_call", output_to_operand_aliasing={{}: (5, {})} | custom-call | bytes 6291456 | tf_op jit(solution)/shard_map/pallas_call | solution.py:343
  33.4 0.1 slice.30
  33.5 1.1 %collective-permute-done.6.swapped = bf16[2048,256]{1,0:T(8,128)(2,1)S(1)} collective-permute-done((bf16[2048,256]{1,0:T(8,128)(2,1)S(1)}, bf16[2048,256]{1,0:T(8,128)(2,1)S(1)}, u32[]{:S(2)}, u32[]{:S(2)}) %collective-permute-start.6) | collective-permute-done | bytes 1048608 | tf_op jit(solution)/shard_map/ppermute | solution.py:62
  34.6 0.1 fusion
  34.7 5.4 %collective-permute-start.7 = (bf16[768,256]{1,0:T(8,128)(2,1)S(1)}, bf16[768,256]{1,0:T(8,128)(2,1)S(1)}, u32[]{:S(2)}, u32[]{:S(2)}) collective-permute-start(bf16[768,256]{1,0:T(8,128)(2,1)S(1)} %fusion), channel_id=1, source_target_pairs={{0,4},{1,13},{2,6},{3,15},{4,8},{5,1},{6,10},{7,3},{8,12},{9,5},{1... | collective-permute-start | bytes 1179656 | tf_op jit(solution)/shard_map/ppermute | solution.py:58
  40.2 0.1 fusion.1
  40.2 1.2 %collective-permute-start.8 = (bf16[512,256]{1,0:T(8,128)(2,1)S(1)}, bf16[512,256]{1,0:T(8,128)(2,1)S(1)}, u32[]{:S(2)}, u32[]{:S(2)}) collective-permute-start(bf16[512,256]{1,0:T(8,128)(2,1)S(1)} %fusion.1), channel_id=1, source_target_pairs={{0,2},{1,15},{2,4},{3,1},{4,6},{5,3},{6,8},{7,5},{8,10},{9,7},{10,... | collective-permute-start | bytes 786440 | tf_op jit(solution)/shard_map/ppermute | solution.py:58
  41.4 7.7 %collective-permute-done.7.middle = bf16[768,256]{1,0:T(8,128)(2,1)S(1)} collective-permute-done((bf16[768,256]{1,0:T(8,128)(2,1)S(1)}, bf16[768,256]{1,0:T(8,128)(2,1)S(1)}, u32[]{:S(2)}, u32[]{:S(2)}) %collective-permute-start.7) | collective-permute-done | bytes 393248 | tf_op jit(solution)/shard_map/ppermute | solution.py:58
  49.1 3.4 %collective-permute-done.8.close = bf16[512,256]{1,0:T(8,128)(2,1)S(1)} collective-permute-done((bf16[512,256]{1,0:T(8,128)(2,1)S(1)}, bf16[512,256]{1,0:T(8,128)(2,1)S(1)}, u32[]{:S(2)}, u32[]{:S(2)}) %collective-permute-start.8) | collective-permute-done | bytes 262176 | tf_op jit(solution)/shard_map/ppermute | solution.py:58
  52.5 0.1 shard_map.107
  52.6 2.6 %collective-permute-start.9 = (bf16[256,256]{1,0:T(8,128)(2,1)S(1)}, bf16[256,256]{1,0:T(8,128)(2,1)S(1)}, u32[]{:S(2)}, u32[]{:S(2)}) collective-permute-start(bf16[256,256]{1,0:T(8,128)(2,1)S(1)} %slice.32), channel_id=1, source_target_pairs={{0,4},{1,13},{2,6},{3,15},{4,8},{5,1},{6,10},{7,3},{8,12},{9,5},{1... | collective-permute-start | bytes 393224 | tf_op jit(solution)/shard_map/ppermute | solution.py:58
  55.2 0.0 collective-permute-start.11
  55.2 2.4 %collective-permute-start.10 = (bf16[256,256]{1,0:T(8,128)(2,1)S(1)}, bf16[256,256]{1,0:T(8,128)(2,1)S(1)}, u32[]{:S(2)}, u32[]{:S(2)}) collective-permute-start(bf16[256,256]{1,0:T(8,128)(2,1)S(1)} %get-tuple-element.20), channel_id=1, source_target_pairs={{0,2},{1,15},{2,4},{3,1},{4,6},{5,3},{6,8},{7,5},{8,10},{9,7},{10,... | collective-permute-start | bytes 393224 | tf_op jit(solution)/shard_map/ppermute | solution.py:58
  57.7 0.9 %collective-permute-done.9 = bf16[256,256]{1,0:T(8,128)(2,1)S(1)} collective-permute-done((bf16[256,256]{1,0:T(8,128)(2,1)S(1)}, bf16[256,256]{1,0:T(8,128)(2,1)S(1)}, u32[]{:S(2)}, u32[]{:S(2)}) %collective-permute-start.9) | collective-permute-done | bytes 131104 | tf_op jit(solution)/shard_map/ppermute | solution.py:58
  58.6 3.3 %collective-permute-done.11 = bf16[256,256]{1,0:T(8,128)(2,1)S(1)} collective-permute-done((bf16[256,256]{1,0:T(8,128)(2,1)S(1)}, bf16[256,256]{1,0:T(8,128)(2,1)S(1)}, u32[]{:S(2)}, u32[]{:S(2)}) %collective-permute-start.11) | collective-permute-done | bytes 131104 | tf_op jit(solution)/shard_map/ppermute | solution.py:58
  61.8 0.0 collective-permute-done.10
  61.8 0.7 %fusion.5 = bf16[256,256]{1,0:T(8,128)(2,1)} fusion(f32[2,128,256]{2,1,0:T(8,128)S(1)} %slice.28, bf16[256,256]{1,0:T(8,128)(2,1)S(1)} %collective-permute-done.11, bf16[256,256]{1,0:T(8,128)(2,1)S(1)} %collective-permute-done.10, bf16[256,256]{1,0:T(8,128)(2,1)S(1)} %collective-permute-done.9, bf16[2048,256]{1,0:T(8,128)(2,1)S(1)} %collective-permute-done.6.swapped), kind=kLoop, calls=%fused_computation.8 | loop fusion | flops 589824 | bytes 917504 | tf_op jit(solution)/shard_map/convert_element_type | solution.py:401
  (4 shorter events, 0.1 us)
Async XLA Ops:
  0.0 18.4 %copy-start = (bf16[28,2,128,128]{3,2,1,0:T(8,128)(2,1)S(1)}, bf16[28,2,128,128]{3,2,1,0:T(8,128)(2,1)}, u32[]{:S(2)}) copy-start(bf16[28,2,128,128]{3,2,1,0:T(8,128)(2,1)} %near_ref.7) | copy-start | bytes 5505028
  1.3 6.2 %collective-permute-start.2 = (bf16[256,256]{1,0:T(8,128)(2,1)S(1)}, bf16[256,256]{1,0:T(8,128)(2,1)S(1)}, u32[]{:S(2)}, u32[]{:S(2)}) collective-permute-start(bf16[256,256]{1,0:T(8,128)(2,1)S(1)} %shard_map.101.refs_0_), channel_id=1, source_target_pairs={{0,128},{1,33},{2,130},{3,35},{4,132},{5,37},{6,134},{7,39},{8,136... | collective-permute-start | bytes 393224 | tf_op jit(solution)/shard_map/ppermute | solution.py:49
  5.1 4.4 %collective-permute-start.1 = (bf16[256,256]{1,0:T(8,128)(2,1)S(1)}, bf16[256,256]{1,0:T(8,128)(2,1)S(1)}, u32[]{:S(2)}, u32[]{:S(2)}) collective-permute-start(bf16[256,256]{1,0:T(8,128)(2,1)S(1)} %shard_map.101.refs_0_), channel_id=1, source_target_pairs={{0,192},{1,49},{2,194},{3,51},{4,196},{5,53},{6,198},{7,55},{8,200... | collective-permute-start | bytes 393224 | tf_op jit(solution)/shard_map/ppermute | solution.py:49
  5.9 5.0 %collective-permute-start = (bf16[256,256]{1,0:T(8,128)(2,1)S(1)}, bf16[256,256]{1,0:T(8,128)(2,1)S(1)}, u32[]{:S(2)}, u32[]{:S(2)}) collective-permute-start(bf16[256,256]{1,0:T(8,128)(2,1)S(1)} %shard_map.101.refs_0_), channel_id=1, source_target_pairs={{0,64},{1,17},{2,66},{3,19},{4,68},{5,21},{6,70},{7,23},{8,72},{9,... | collective-permute-start | bytes 393224 | tf_op jit(solution)/shard_map/ppermute | solution.py:49
  11.0 10.0 %collective-permute-start.5 = (bf16[1024,256]{1,0:T(8,128)(2,1)S(1)}, bf16[1024,256]{1,0:T(8,128)(2,1)S(1)}, u32[]{:S(2)}, u32[]{:S(2)}) collective-permute-start(bf16[1024,256]{1,0:T(8,128)(2,1)S(1)} %shard_map.102.piece), channel_id=1, source_target_pairs={{0,32},{1,129},{2,34},{3,131},{4,36},{5,133},{6,38},{7,135},{8,40}... | collective-permute-start | bytes 1572872 | tf_op jit(solution)/shard_map/ppermute | solution.py:49
  13.8 12.8 %collective-permute-start.4 = (bf16[1024,256]{1,0:T(8,128)(2,1)S(1)}, bf16[1024,256]{1,0:T(8,128)(2,1)S(1)}, u32[]{:S(2)}, u32[]{:S(2)}) collective-permute-start(bf16[1024,256]{1,0:T(8,128)(2,1)S(1)} %shard_map.102.piece), channel_id=1, source_target_pairs={{0,48},{1,193},{2,50},{3,195},{4,52},{5,197},{6,54},{7,199},{8,56}... | collective-permute-start | bytes 1572872 | tf_op jit(solution)/shard_map/ppermute | solution.py:49
  14.6 12.0 %collective-permute-start.3 = (bf16[1024,256]{1,0:T(8,128)(2,1)S(1)}, bf16[1024,256]{1,0:T(8,128)(2,1)S(1)}, u32[]{:S(2)}, u32[]{:S(2)}) collective-permute-start(bf16[1024,256]{1,0:T(8,128)(2,1)S(1)} %shard_map.102.piece), channel_id=1, source_target_pairs={{0,16},{1,65},{2,18},{3,67},{4,20},{5,69},{6,22},{7,71},{8,24},{9,... | collective-permute-start | bytes 1572872 | tf_op jit(solution)/shard_map/ppermute | solution.py:49
  28.6 6.0 %collective-permute-start.6 = (bf16[2048,256]{1,0:T(8,128)(2,1)S(1)}, bf16[2048,256]{1,0:T(8,128)(2,1)S(1)}, u32[]{:S(2)}, u32[]{:S(2)}) collective-permute-start(bf16[2048,256]{1,0:T(8,128)(2,1)S(1)} %get-tuple-element.19), channel_id=1, source_target_pairs={{0,1},{1,0},{2,3},{3,2},{4,5},{5,4},{6,7},{7,6},{8,9},{9,8},{10,11... | collective-permute-start | bytes 3145736 | tf_op jit(solution)/shard_map/ppermute | solution.py:62
  34.7 14.4 %collective-permute-start.7 = (bf16[768,256]{1,0:T(8,128)(2,1)S(1)}, bf16[768,256]{1,0:T(8,128)(2,1)S(1)}, u32[]{:S(2)}, u32[]{:S(2)}) collective-permute-start(bf16[768,256]{1,0:T(8,128)(2,1)S(1)} %fusion), channel_id=1, source_target_pairs={{0,4},{1,13},{2,6},{3,15},{4,8},{5,1},{6,10},{7,3},{8,12},{9,5},{1... | collective-permute-start | bytes 1179656 | tf_op jit(solution)/shard_map/ppermute | solution.py:58
  40.2 12.3 %collective-permute-start.8 = (bf16[512,256]{1,0:T(8,128)(2,1)S(1)}, bf16[512,256]{1,0:T(8,128)(2,1)S(1)}, u32[]{:S(2)}, u32[]{:S(2)}) collective-permute-start(bf16[512,256]{1,0:T(8,128)(2,1)S(1)} %fusion.1), channel_id=1, source_target_pairs={{0,2},{1,15},{2,4},{3,1},{4,6},{5,3},{6,8},{7,5},{8,10},{9,7},{10,... | collective-permute-start | bytes 786440 | tf_op jit(solution)/shard_map/ppermute | solution.py:58
  52.6 5.9 %collective-permute-start.9 = (bf16[256,256]{1,0:T(8,128)(2,1)S(1)}, bf16[256,256]{1,0:T(8,128)(2,1)S(1)}, u32[]{:S(2)}, u32[]{:S(2)}) collective-permute-start(bf16[256,256]{1,0:T(8,128)(2,1)S(1)} %slice.32), channel_id=1, source_target_pairs={{0,4},{1,13},{2,6},{3,15},{4,8},{5,1},{6,10},{7,3},{8,12},{9,5},{1... | collective-permute-start | bytes 393224 | tf_op jit(solution)/shard_map/ppermute | solution.py:58
  55.2 6.6 %collective-permute-start.11 = (bf16[256,256]{1,0:T(8,128)(2,1)S(1)}, bf16[256,256]{1,0:T(8,128)(2,1)S(1)}, u32[]{:S(2)}, u32[]{:S(2)}) collective-permute-start(bf16[256,256]{1,0:T(8,128)(2,1)S(1)} %get-tuple-element.22), channel_id=1, source_target_pairs={{0,3},{1,14},{2,5},{3,0},{4,7},{5,2},{6,9},{7,4},{8,11},{9,6},{10,... | collective-permute-start | bytes 393224 | tf_op jit(solution)/shard_map/ppermute | solution.py:58
  55.2 6.6 %collective-permute-start.10 = (bf16[256,256]{1,0:T(8,128)(2,1)S(1)}, bf16[256,256]{1,0:T(8,128)(2,1)S(1)}, u32[]{:S(2)}, u32[]{:S(2)}) collective-permute-start(bf16[256,256]{1,0:T(8,128)(2,1)S(1)} %get-tuple-element.20), channel_id=1, source_target_pairs={{0,2},{1,15},{2,4},{3,1},{4,6},{5,3},{6,8},{7,5},{8,10},{9,7},{10,... | collective-permute-start | bytes 393224 | tf_op jit(solution)/shard_map/ppermute | solution.py:58

commit v5 on v4

--- a/solution.py
+++ b/solution.py
@@ -20,6 +20,7 @@
 GROUPS = 4
 LIST = 36
 COUNTS = 2 * GROUPS * LIST
+FIRST = 6
 F32 = jnp.float32
 BF16 = jnp.bfloat16
 VMEM = pl.BlockSpec(memory_space=pltpu.VMEM)
@@ -293,12 +294,14 @@
     work(1, lists, u_ref, v_ref, near_ref, trial, total)
 
 
-def third_kernel(lists, u_ref, v_ref, near_ref, ahead, back, _, total, trial, other_ref):
+def third_kernel(lists, u_ref, v_ref, near_ref, ahead, back, _, total, trial, one_ref, two_ref):
     load(ahead, trial, 0)
     load(back, trial, 8)
     work(2, lists, u_ref, v_ref, near_ref, trial, total)
-    for t in range(SLAB // 2):
-        other_ref[t * LEAF : (t + 1) * LEAF, :] = total[t].astype(BF16)
+    for t in range(FIRST):
+        one_ref[t * LEAF : (t + 1) * LEAF, :] = total[t].astype(BF16)
+    for t in range(SLAB // 2 - FIRST):
+        two_ref[t * LEAF : (t + 1) * LEAF, :] = total[FIRST + t].astype(BF16)
 
 
 def fourth_kernel(lists, u_ref, v_ref, near_ref, trial, _, total):
@@ -327,15 +330,16 @@
         compiler_params=limit(6),
         cost_estimate=cost(6),
     )(*common, two, total)
-    total, trial, other = pl.pallas_call(
+    total, trial, one, other = pl.pallas_call(
         third_kernel,
         out_shape=(
             TOTAL,
             pltpu.VMEM((16, 2 * LEAF, COLS), BF16),
-            pltpu.VMEM((SLAB // 2 * LEAF, COLS), BF16),
+            pltpu.VMEM((FIRST * LEAF, COLS), BF16),
+            pltpu.VMEM(((SLAB // 2 - FIRST) * LEAF, COLS), BF16),
         ),
         in_specs=[SMEM] + [VMEM] * 6,
-        out_specs=(VMEM, VMEM, VMEM),
+        out_specs=(VMEM, VMEM, VMEM, VMEM),
         input_output_aliases={6: 0},
         compiler_params=limit(6),
         cost_estimate=cost(8),
@@ -349,7 +353,7 @@
         compiler_params=limit(6),
         cost_estimate=cost(6),
     )(*common, trial, total)
-    return other, total
+    return (one, other), total
 
 
 def gather(mine):
@@ -361,7 +365,8 @@
 
 def chip_sum(own, swapped, first, count):
     mine = own[SLAB // 2 + first : SLAB // 2 + first + count].reshape(count * LEAF, COLS)
-    return mine + swapped[first * LEAF : (first + count) * LEAF].astype(F32)
+    theirs, first = (swapped[0], first) if first < FIRST else (swapped[1], first - FIRST)
+    return mine + theirs[first * LEAF : (first + count) * LEAF].astype(F32)
 
 
 def cluster(k):
@@ -374,7 +379,7 @@
         for i in range(2):
             place = owner * 2 + i
 
-            total = own[SLAB // 2 + 10 + place] + swapped[cluster(10 + place), :].astype(F32)
+            total = own[SLAB // 2 + 10 + place] + swapped[cluster(10 - FIRST + place), :].astype(F32)
             total += close[cluster(place), :].astype(F32) + middle[cluster(2 + place), :].astype(F32)
             out[i * LEAF : (i + 1) * LEAF, :] = total.astype(BF16)
 
@@ -393,7 +398,7 @@
 def scatter(swapped, own):
     middle = along_z(2, chip_sum(own, swapped, 0, 6).astype(BF16))
     close = along_z(1, chip_sum(own, swapped, 6, 4).astype(BF16))
-    same, cross = relay(own, swapped, close, middle)
+    same, cross = relay(own, swapped[1], close, middle)
     far = after(middle[: 2 * LEAF], same)
     same, cross = along_z(1, same), along_z(1, cross, 1)
     far = along_z(2, far)
@@ -416,7 +421,7 @@
     )
     pieces = gather(mine)
     other, own = blocks((lists, u, v, near_block), pieces)
-    return scatter(other_core(other), own)
+    return scatter([other_core(part) for part in other], own)
 
 
 def solution(mesh):

time: 63.2 us -> 62.6 us (level)
  waiting for transfers between devices: 25.6 us -> 23.6 us
  starting transfers between devices: 25 us -> 25.9 us
    ppermute x5, starting transfers between devices: 11.7 us -> 13.9 us  [along_z(): return lax.ppermute(value, 'col', pairs)]
    ppermute x1 -> x2, starting transfers between devices: 3.75 us -> 2.41 us  [other_core(): return lax.ppermute(value, 'col', [(d, d ^ 1) for d in range(NZ * NCORE)])]
    ppermute x1 -> x2, waiting for transfers between devices: 1.11 us -> 0.01 us  [other_core(): return lax.ppermute(value, 'col', [(d, d ^ 1) for d in range(NZ * NCORE)])]
    ppermute x5, waiting for transfers between devices: 15.2 us -> 14.1 us  [along_z(): return lax.ppermute(value, 'col', pairs)]
  transfers between devices with their start and end apart: 12 -> 13, of which waited for: 10 -> 9; matrix products, arithmetic and copies ran while one was open for 0% -> 0% of each run, Pallas kernels for 12% -> 12%
where the time goes in v5:
time: 62.6 us; the launch traced here: 61.9 us
  starting transfers between devices  25.9 us (41%)
  waiting for transfers between devices  23.6 us (38%)
  Pallas kernels  11.2 us (18%)
  other arithmetic  0.88 us (1%)
    ppermute x5, waiting for transfers between devices, along_z(): return lax.ppermute(value, 'col', pairs)  14.1 us
    ppermute x5, starting transfers between devices, along_z(): return lax.ppermute(value, 'col', pairs)  13.9 us
    ppermute x6, starting transfers between devices, hop(): return lax.ppermute(value, ('row', 'col'), pairs)  9.59 us
    ppermute x6, waiting for transfers between devices, hop(): return lax.ppermute(value, ('row', 'col'), pairs)  9.52 us
    pallas_call x1, Pallas kernels, prepare(): pl.pallas_call(prepare_kernel, out_shape=(pltpu.VMEM((NB, LEAF, 2 * RMAX)...  3.12 us
    ppermute x2, starting transfers between devices, other_core(): return lax.ppermute(value, 'col', [(d, d ^ 1) for d in range(NZ * NCORE)])  2.41 us
    pallas_call x1, Pallas kernels, blocks(): pl.pallas_call(third_kernel, out_shape=(TOTAL, pltpu.VMEM((16, 2 * LEAF,...  2.36 us
    pallas_call x1, Pallas kernels, blocks(): pl.pallas_call(first_kernel, out_shape=TOTAL, in_specs=[SMEM] + [VMEM] *...  1.66 us
  transfers between devices with their start and end apart: 13, of which 9 were waited for; matrix products, arithmetic and copies ran while one was open for 0% of the time, Pallas kernels for 12%

profile of v5, /device:TPU:1, one launch (start us, length us, event | category | flops | bytes accessed | tf_op | source)
XLA Modules:
  0.0 61.9 jit_solution(18053003408523168698)
XLA Ops:
  0.0 0.0 copy-start
  0.0 1.3 %shard_map.101.refs_0_ = bf16[256,256]{1,0:T(8,128)(2,1)S(1)} custom-call(s32[2,128]{1,0:T(2,128)} %perm_hbm.1, bf16[256,256]{1,0:T(8,128)(2,1)} %x_hbm.1), custom_call_target="tpu_custom_call" | custom-call | tf_op jit(solution)/shard_map/pallas_call | solution.py:91
  1.3 3.8 %collective-permute-start.2 = (bf16[256,256]{1,0:T(8,128)(2,1)S(1)}, bf16[256,256]{1,0:T(8,128)(2,1)S(1)}, u32[]{:S(2)}, u32[]{:S(2)}) collective-permute-start(bf16[256,256]{1,0:T(8,128)(2,1)S(1)} %shard_map.101.refs_0_), channel_id=1, source_target_pairs={{0,128},{1,33},{2,130},{3,35},{4,132},{5,37},{6,134},{7,39},{8,136... | collective-permute-start | bytes 393224 | tf_op jit(solution)/shard_map/ppermute | solution.py:50
  5.1 0.8 %collective-permute-start.1 = (bf16[256,256]{1,0:T(8,128)(2,1)S(1)}, bf16[256,256]{1,0:T(8,128)(2,1)S(1)}, u32[]{:S(2)}, u32[]{:S(2)}) collective-permute-start(bf16[256,256]{1,0:T(8,128)(2,1)S(1)} %shard_map.101.refs_0_), channel_id=1, source_target_pairs={{0,192},{1,49},{2,194},{3,51},{4,196},{5,53},{6,198},{7,55},{8,200... | collective-permute-start | bytes 393224 | tf_op jit(solution)/shard_map/ppermute | solution.py:50
  5.9 0.7 %collective-permute-start = (bf16[256,256]{1,0:T(8,128)(2,1)S(1)}, bf16[256,256]{1,0:T(8,128)(2,1)S(1)}, u32[]{:S(2)}, u32[]{:S(2)}) collective-permute-start(bf16[256,256]{1,0:T(8,128)(2,1)S(1)} %shard_map.101.refs_0_), channel_id=1, source_target_pairs={{0,64},{1,17},{2,66},{3,19},{4,68},{5,21},{6,70},{7,23},{8,72},{9,... | collective-permute-start | bytes 393224 | tf_op jit(solution)/shard_map/ppermute | solution.py:50
  6.6 0.9 %collective-permute-done.2.refs_3_ = bf16[256,256]{1,0:T(8,128)(2,1)S(1)} collective-permute-done((bf16[256,256]{1,0:T(8,128)(2,1)S(1)}, bf16[256,256]{1,0:T(8,128)(2,1)S(1)}, u32[]{:S(2)}, u32[]{:S(2)}) %collective-permute-start.2) | collective-permute-done | bytes 131104 | tf_op jit(solution)/shard_map/ppermute | solution.py:50
  7.5 2.1 %collective-permute-done.1.refs_2_ = bf16[256,256]{1,0:T(8,128)(2,1)S(1)} collective-permute-done((bf16[256,256]{1,0:T(8,128)(2,1)S(1)}, bf16[256,256]{1,0:T(8,128)(2,1)S(1)}, u32[]{:S(2)}, u32[]{:S(2)}) %collective-permute-start.1) | collective-permute-done | bytes 131104 | tf_op jit(solution)/shard_map/ppermute | solution.py:50
  9.6 1.4 %collective-permute-done.refs_1_ = bf16[256,256]{1,0:T(8,128)(2,1)S(1)} collective-permute-done((bf16[256,256]{1,0:T(8,128)(2,1)S(1)}, bf16[256,256]{1,0:T(8,128)(2,1)S(1)}, u32[]{:S(2)}, u32[]{:S(2)}) %collective-permute-start) | collective-permute-done | bytes 131104 | tf_op jit(solution)/shard_map/ppermute | solution.py:50
  11.0 2.8 %collective-permute-start.5 = (bf16[1024,256]{1,0:T(8,128)(2,1)S(1)}, bf16[1024,256]{1,0:T(8,128)(2,1)S(1)}, u32[]{:S(2)}, u32[]{:S(2)}) collective-permute-start(bf16[1024,256]{1,0:T(8,128)(2,1)S(1)} %shard_map.102.piece), channel_id=1, source_target_pairs={{0,32},{1,129},{2,34},{3,131},{4,36},{5,133},{6,38},{7,135},{8,40}... | collective-permute-start | bytes 1572872 | tf_op jit(solution)/shard_map/ppermute | solution.py:50
  13.8 0.9 %collective-permute-start.4 = (bf16[1024,256]{1,0:T(8,128)(2,1)S(1)}, bf16[1024,256]{1,0:T(8,128)(2,1)S(1)}, u32[]{:S(2)}, u32[]{:S(2)}) collective-permute-start(bf16[1024,256]{1,0:T(8,128)(2,1)S(1)} %shard_map.102.piece), channel_id=1, source_target_pairs={{0,48},{1,193},{2,50},{3,195},{4,52},{5,197},{6,54},{7,199},{8,56}... | collective-permute-start | bytes 1572872 | tf_op jit(solution)/shard_map/ppermute | solution.py:50
  14.6 0.6 collective-permute-start.3
  15.3 3.1 %shard_map.100 = (bf16[32,128,128]{2,1,0:T(8,128)(2,1)S(1)}, bf16[32,64,256]{2,1,0:T(8,128)(2,1)S(1)}, s32[296]{0:T(512)S(4)}) custom-call(s32[32]{0:T(128)} %rank_hbm.1, s32[32]{0:T(128)} %far_rows_hbm.1, s32[32]{0:T(128)} %far_cols_hbm.1, s32[28]{0:T(128)} %near_rows_hbm.1, s32[28]{0:T(128)} %near_cols_hbm.1, bf16[32,2,64,128]{3,2,1,0:T(8,128)(2,1)} %bitcast.20, ...), custom_call_target="tpu_custom_call" | custom-call | bytes 8388608 | tf_op jit(solution)/shard_map/pallas_call | solution.py:219
  18.4 0.0 copy-done
  18.4 1.7 %shard_map.103._ = f32[33,128,256]{2,1,0:T(8,128)S(1)} custom-call(s32[296]{0:T(512)S(4)} %get-tuple-element.15.lists, bf16[32,128,128]{2,1,0:T(8,128)(2,1)S(1)} %get-tuple-element.16.u_ref, bf16[32,64,256]{2,1,0:T(8,128)(2,1)S(1)} %get-tuple-element.17.v_ref, bf16[28,2,128,128]{3,2,1,0:T(8,128)(2,1)S(1)} %copy-done, bf16[1024,256]{1,0:T(8,128)(2,1)S(1)} %shard_map.102.piece), custom_call_target="tpu_custom_call" | custom-call | bytes 8388608 | tf_op jit(solution)/shard_map/pallas_call | solution.py:314
  20.1 0.9 %collective-permute-done.5.piece = bf16[1024,256]{1,0:T(8,128)(2,1)S(1)} collective-permute-done((bf16[1024,256]{1,0:T(8,128)(2,1)S(1)}, bf16[1024,256]{1,0:T(8,128)(2,1)S(1)}, u32[]{:S(2)}, u32[]{:S(2)}) %collective-permute-start.5) | collective-permute-done | bytes 524320 | tf_op jit(solution)/shard_map/ppermute | solution.py:50
  20.9 1.4 %shard_map.104._ = f32[33,128,256]{2,1,0:T(8,128)S(1)} custom-call(s32[296]{0:T(512)S(4)} %get-tuple-element.15.lists, bf16[32,128,128]{2,1,0:T(8,128)(2,1)S(1)} %get-tuple-element.16.u_ref, bf16[32,64,256]{2,1,0:T(8,128)(2,1)S(1)} %get-tuple-element.17.v_ref, bf16[28,2,128,128]{3,2,1,0:T(8,128)(2,1)S(1)} %copy-done, ...), custom_call_target="tpu_custom_call", output_to_operand_aliasing={{}: (5, {})} | custom-call | bytes 6291456 | tf_op jit(solution)/shard_map/pallas_call | solution.py:323
  22.3 4.3 %collective-permute-done.4.back = bf16[1024,256]{1,0:T(8,128)(2,1)S(1)} collective-permute-done((bf16[1024,256]{1,0:T(8,128)(2,1)S(1)}, bf16[1024,256]{1,0:T(8,128)(2,1)S(1)}, u32[]{:S(2)}, u32[]{:S(2)}) %collective-permute-start.4) | collective-permute-done | bytes 524320 | tf_op jit(solution)/shard_map/ppermute | solution.py:50
  26.6 0.0 collective-permute-done.3.ahead
  26.6 2.4 %shard_map.105 = (f32[33,128,256]{2,1,0:T(8,128)S(1)}, bf16[16,256,256]{2,1,0:T(8,128)(2,1)S(1)}, bf16[768,256]{1,0:T(8,128)(2,1)S(1)}, bf16[1280,256]{1,0:T(8,128)(2,1)S(1)}) custom-call(s32[296]{0:T(512)S(4)} %get-tuple-element.15.lists, bf16[32,128,128]{2,1,0:T(8,128)(2,1)S(1)} %get-tuple-element.16.u_ref, ...), custom_call_target="tpu_custom_call", output_to_operand_aliasing={{0}: (6, {})} | custom-call | bytes 8388608 | tf_op jit(solution)/shard_map/pallas_call | solution.py:333
  29.0 2.3 %collective-permute-start.7 = (bf16[768,256]{1,0:T(8,128)(2,1)S(1)}, bf16[768,256]{1,0:T(8,128)(2,1)S(1)}, u32[]{:S(2)}, u32[]{:S(2)}) collective-permute-start(bf16[768,256]{1,0:T(8,128)(2,1)S(1)} %get-tuple-element.21), channel_id=1, source_target_pairs={{0,1},{1,0},{2,3},{3,2},{4,5},{5,4},{6,7},{7,6},{8,9},{9,8},{10,11... | collective-permute-start | bytes 1179656 | tf_op jit(solution)/shard_map/ppermute | solution.py:63
  31.3 0.1 collective-permute-start.6
  31.4 1.3 %shard_map.106.own = f32[33,128,256]{2,1,0:T(8,128)S(1)} custom-call(s32[296]{0:T(512)S(4)} %get-tuple-element.15.lists, bf16[32,128,128]{2,1,0:T(8,128)(2,1)S(1)} %get-tuple-element.16.u_ref, bf16[32,64,256]{2,1,0:T(8,128)(2,1)S(1)} %get-tuple-element.17.v_ref, bf16[28,2,128,128]{3,2,1,0:T(8,128)(2,1)S(1)} %copy-done, ...), custom_call_target="tpu_custom_call", output_to_operand_aliasing={{}: (5, {})} | custom-call | bytes 6291456 | tf_op jit(solution)/shard_map/pallas_call | solution.py:347
  32.8 0.1 slice.26
  32.8 0.0 collective-permute-done.7
  32.9 0.1 fusion
  32.9 6.0 %collective-permute-start.8 = (bf16[768,256]{1,0:T(8,128)(2,1)S(1)}, bf16[768,256]{1,0:T(8,128)(2,1)S(1)}, u32[]{:S(2)}, u32[]{:S(2)}) collective-permute-start(bf16[768,256]{1,0:T(8,128)(2,1)S(1)} %fusion), channel_id=1, source_target_pairs={{0,4},{1,13},{2,6},{3,15},{4,8},{5,1},{6,10},{7,3},{8,12},{9,5},{1... | collective-permute-start | bytes 1179656 | tf_op jit(solution)/shard_map/ppermute | solution.py:59
  39.0 0.0 collective-permute-done.6.swapped
  39.0 0.1 fusion.1
  39.0 1.7 %collective-permute-start.9 = (bf16[512,256]{1,0:T(8,128)(2,1)S(1)}, bf16[512,256]{1,0:T(8,128)(2,1)S(1)}, u32[]{:S(2)}, u32[]{:S(2)}) collective-permute-start(bf16[512,256]{1,0:T(8,128)(2,1)S(1)} %fusion.1), channel_id=1, source_target_pairs={{0,2},{1,15},{2,4},{3,1},{4,6},{5,3},{6,8},{7,5},{8,10},{9,7},{10,... | collective-permute-start | bytes 786440 | tf_op jit(solution)/shard_map/ppermute | solution.py:59
  40.7 7.2 %collective-permute-done.8.middle = bf16[768,256]{1,0:T(8,128)(2,1)S(1)} collective-permute-done((bf16[768,256]{1,0:T(8,128)(2,1)S(1)}, bf16[768,256]{1,0:T(8,128)(2,1)S(1)}, u32[]{:S(2)}, u32[]{:S(2)}) %collective-permute-start.8) | collective-permute-done | bytes 393248 | tf_op jit(solution)/shard_map/ppermute | solution.py:59
  47.9 2.8 %collective-permute-done.9.close = bf16[512,256]{1,0:T(8,128)(2,1)S(1)} collective-permute-done((bf16[512,256]{1,0:T(8,128)(2,1)S(1)}, bf16[512,256]{1,0:T(8,128)(2,1)S(1)}, u32[]{:S(2)}, u32[]{:S(2)}) %collective-permute-start.9) | collective-permute-done | bytes 262176 | tf_op jit(solution)/shard_map/ppermute | solution.py:59
  50.7 0.1 shard_map.107
  50.8 3.7 %collective-permute-start.10 = (bf16[256,256]{1,0:T(8,128)(2,1)S(1)}, bf16[256,256]{1,0:T(8,128)(2,1)S(1)}, u32[]{:S(2)}, u32[]{:S(2)}) collective-permute-start(bf16[256,256]{1,0:T(8,128)(2,1)S(1)} %slice.27), channel_id=1, source_target_pairs={{0,4},{1,13},{2,6},{3,15},{4,8},{5,1},{6,10},{7,3},{8,12},{9,5},{1... | collective-permute-start | bytes 393224 | tf_op jit(solution)/shard_map/ppermute | solution.py:59
  54.5 0.3 collective-permute-start.12
  54.8 2.3 %collective-permute-start.11 = (bf16[256,256]{1,0:T(8,128)(2,1)S(1)}, bf16[256,256]{1,0:T(8,128)(2,1)S(1)}, u32[]{:S(2)}, u32[]{:S(2)}) collective-permute-start(bf16[256,256]{1,0:T(8,128)(2,1)S(1)} %get-tuple-element.22), channel_id=1, source_target_pairs={{0,2},{1,15},{2,4},{3,1},{4,6},{5,3},{6,8},{7,5},{8,10},{9,7},{10,... | collective-permute-start | bytes 393224 | tf_op jit(solution)/shard_map/ppermute | solution.py:59
  57.1 0.7 %collective-permute-done.10 = bf16[256,256]{1,0:T(8,128)(2,1)S(1)} collective-permute-done((bf16[256,256]{1,0:T(8,128)(2,1)S(1)}, bf16[256,256]{1,0:T(8,128)(2,1)S(1)}, u32[]{:S(2)}, u32[]{:S(2)}) %collective-permute-start.10) | collective-permute-done | bytes 131104 | tf_op jit(solution)/shard_map/ppermute | solution.py:59
  57.8 3.3 %collective-permute-done.12 = bf16[256,256]{1,0:T(8,128)(2,1)S(1)} collective-permute-done((bf16[256,256]{1,0:T(8,128)(2,1)S(1)}, bf16[256,256]{1,0:T(8,128)(2,1)S(1)}, u32[]{:S(2)}, u32[]{:S(2)}) %collective-permute-start.12) | collective-permute-done | bytes 131104 | tf_op jit(solution)/shard_map/ppermute | solution.py:59
  61.2 0.0 collective-permute-done.11
  61.2 0.7 %fusion.5 = bf16[256,256]{1,0:T(8,128)(2,1)} fusion(f32[2,128,256]{2,1,0:T(8,128)S(1)} %slice.24, bf16[256,256]{1,0:T(8,128)(2,1)S(1)} %collective-permute-done.12, bf16[256,256]{1,0:T(8,128)(2,1)S(1)} %collective-permute-done.11, bf16[256,256]{1,0:T(8,128)(2,1)S(1)} %collective-permute-done.10, bf16[1280,256]{1,0:T(8,128)(2,1)S(1)} %collective-permute-done.6.swapped), kind=kLoop, calls=%fused_computation.8 | loop fusion | flops 589824 | bytes 917504 | tf_op jit(solution)/shard_map/convert_element_type | solution.py:406
  (4 shorter events, 0.1 us)
Async XLA Ops:
  0.0 18.4 %copy-start = (bf16[28,2,128,128]{3,2,1,0:T(8,128)(2,1)S(1)}, bf16[28,2,128,128]{3,2,1,0:T(8,128)(2,1)}, u32[]{:S(2)}) copy-start(bf16[28,2,128,128]{3,2,1,0:T(8,128)(2,1)} %near_ref.7) | copy-start | bytes 5505028
  1.3 6.2 %collective-permute-start.2 = (bf16[256,256]{1,0:T(8,128)(2,1)S(1)}, bf16[256,256]{1,0:T(8,128)(2,1)S(1)}, u32[]{:S(2)}, u32[]{:S(2)}) collective-permute-start(bf16[256,256]{1,0:T(8,128)(2,1)S(1)} %shard_map.101.refs_0_), channel_id=1, source_target_pairs={{0,128},{1,33},{2,130},{3,35},{4,132},{5,37},{6,134},{7,39},{8,136... | collective-permute-start | bytes 393224 | tf_op jit(solution)/shard_map/ppermute | solution.py:50
  5.1 4.4 %collective-permute-start.1 = (bf16[256,256]{1,0:T(8,128)(2,1)S(1)}, bf16[256,256]{1,0:T(8,128)(2,1)S(1)}, u32[]{:S(2)}, u32[]{:S(2)}) collective-permute-start(bf16[256,256]{1,0:T(8,128)(2,1)S(1)} %shard_map.101.refs_0_), channel_id=1, source_target_pairs={{0,192},{1,49},{2,194},{3,51},{4,196},{5,53},{6,198},{7,55},{8,200... | collective-permute-start | bytes 393224 | tf_op jit(solution)/shard_map/ppermute | solution.py:50
  5.9 5.0 %collective-permute-start = (bf16[256,256]{1,0:T(8,128)(2,1)S(1)}, bf16[256,256]{1,0:T(8,128)(2,1)S(1)}, u32[]{:S(2)}, u32[]{:S(2)}) collective-permute-start(bf16[256,256]{1,0:T(8,128)(2,1)S(1)} %shard_map.101.refs_0_), channel_id=1, source_target_pairs={{0,64},{1,17},{2,66},{3,19},{4,68},{5,21},{6,70},{7,23},{8,72},{9,... | collective-permute-start | bytes 393224 | tf_op jit(solution)/shard_map/ppermute | solution.py:50
  11.0 10.0 %collective-permute-start.5 = (bf16[1024,256]{1,0:T(8,128)(2,1)S(1)}, bf16[1024,256]{1,0:T(8,128)(2,1)S(1)}, u32[]{:S(2)}, u32[]{:S(2)}) collective-permute-start(bf16[1024,256]{1,0:T(8,128)(2,1)S(1)} %shard_map.102.piece), channel_id=1, source_target_pairs={{0,32},{1,129},{2,34},{3,131},{4,36},{5,133},{6,38},{7,135},{8,40}... | collective-permute-start | bytes 1572872 | tf_op jit(solution)/shard_map/ppermute | solution.py:50
  13.8 12.8 %collective-permute-start.4 = (bf16[1024,256]{1,0:T(8,128)(2,1)S(1)}, bf16[1024,256]{1,0:T(8,128)(2,1)S(1)}, u32[]{:S(2)}, u32[]{:S(2)}) collective-permute-start(bf16[1024,256]{1,0:T(8,128)(2,1)S(1)} %shard_map.102.piece), channel_id=1, source_target_pairs={{0,48},{1,193},{2,50},{3,195},{4,52},{5,197},{6,54},{7,199},{8,56}... | collective-permute-start | bytes 1572872 | tf_op jit(solution)/shard_map/ppermute | solution.py:50
  14.6 12.0 %collective-permute-start.3 = (bf16[1024,256]{1,0:T(8,128)(2,1)S(1)}, bf16[1024,256]{1,0:T(8,128)(2,1)S(1)}, u32[]{:S(2)}, u32[]{:S(2)}) collective-permute-start(bf16[1024,256]{1,0:T(8,128)(2,1)S(1)} %shard_map.102.piece), channel_id=1, source_target_pairs={{0,16},{1,65},{2,18},{3,67},{4,20},{5,69},{6,22},{7,71},{8,24},{9,... | collective-permute-start | bytes 1572872 | tf_op jit(solution)/shard_map/ppermute | solution.py:50
  29.0 3.9 %collective-permute-start.7 = (bf16[768,256]{1,0:T(8,128)(2,1)S(1)}, bf16[768,256]{1,0:T(8,128)(2,1)S(1)}, u32[]{:S(2)}, u32[]{:S(2)}) collective-permute-start(bf16[768,256]{1,0:T(8,128)(2,1)S(1)} %get-tuple-element.21), channel_id=1, source_target_pairs={{0,1},{1,0},{2,3},{3,2},{4,5},{5,4},{6,7},{7,6},{8,9},{9,8},{10,11... | collective-permute-start | bytes 1179656 | tf_op jit(solution)/shard_map/ppermute | solution.py:63
  31.3 7.7 %collective-permute-start.6 = (bf16[1280,256]{1,0:T(8,128)(2,1)S(1)}, bf16[1280,256]{1,0:T(8,128)(2,1)S(1)}, u32[]{:S(2)}, u32[]{:S(2)}) collective-permute-start(bf16[1280,256]{1,0:T(8,128)(2,1)S(1)} %get-tuple-element.20), channel_id=1, source_target_pairs={{0,1},{1,0},{2,3},{3,2},{4,5},{5,4},{6,7},{7,6},{8,9},{9,8},{10,11... | collective-permute-start | bytes 1966088 | tf_op jit(solution)/shard_map/ppermute | solution.py:63
  32.9 15.0 %collective-permute-start.8 = (bf16[768,256]{1,0:T(8,128)(2,1)S(1)}, bf16[768,256]{1,0:T(8,128)(2,1)S(1)}, u32[]{:S(2)}, u32[]{:S(2)}) collective-permute-start(bf16[768,256]{1,0:T(8,128)(2,1)S(1)} %fusion), channel_id=1, source_target_pairs={{0,4},{1,13},{2,6},{3,15},{4,8},{5,1},{6,10},{7,3},{8,12},{9,5},{1... | collective-permute-start | bytes 1179656 | tf_op jit(solution)/shard_map/ppermute | solution.py:59
  39.0 11.7 %collective-permute-start.9 = (bf16[512,256]{1,0:T(8,128)(2,1)S(1)}, bf16[512,256]{1,0:T(8,128)(2,1)S(1)}, u32[]{:S(2)}, u32[]{:S(2)}) collective-permute-start(bf16[512,256]{1,0:T(8,128)(2,1)S(1)} %fusion.1), channel_id=1, source_target_pairs={{0,2},{1,15},{2,4},{3,1},{4,6},{5,3},{6,8},{7,5},{8,10},{9,7},{10,... | collective-permute-start | bytes 786440 | tf_op jit(solution)/shard_map/ppermute | solution.py:59
  50.8 7.0 %collective-permute-start.10 = (bf16[256,256]{1,0:T(8,128)(2,1)S(1)}, bf16[256,256]{1,0:T(8,128)(2,1)S(1)}, u32[]{:S(2)}, u32[]{:S(2)}) collective-permute-start(bf16[256,256]{1,0:T(8,128)(2,1)S(1)} %slice.27), channel_id=1, source_target_pairs={{0,4},{1,13},{2,6},{3,15},{4,8},{5,1},{6,10},{7,3},{8,12},{9,5},{1... | collective-permute-start | bytes 393224 | tf_op jit(solution)/shard_map/ppermute | solution.py:59
  54.5 6.7 %collective-permute-start.12 = (bf16[256,256]{1,0:T(8,128)(2,1)S(1)}, bf16[256,256]{1,0:T(8,128)(2,1)S(1)}, u32[]{:S(2)}, u32[]{:S(2)}) collective-permute-start(bf16[256,256]{1,0:T(8,128)(2,1)S(1)} %get-tuple-element.24), channel_id=1, source_target_pairs={{0,3},{1,14},{2,5},{3,0},{4,7},{5,2},{6,9},{7,4},{8,11},{9,6},{10,... | collective-permute-start | bytes 393224 | tf_op jit(solution)/shard_map/ppermute | solution.py:59
  54.8 6.4 %collective-permute-start.11 = (bf16[256,256]{1,0:T(8,128)(2,1)S(1)}, bf16[256,256]{1,0:T(8,128)(2,1)S(1)}, u32[]{:S(2)}, u32[]{:S(2)}) collective-permute-start(bf16[256,256]{1,0:T(8,128)(2,1)S(1)} %get-tuple-element.22), channel_id=1, source_target_pairs={{0,2},{1,15},{2,4},{3,1},{4,6},{5,3},{6,8},{7,5},{8,10},{9,7},{10,... | collective-permute-start | bytes 393224 | tf_op jit(solution)/shard_map/ppermute | solution.py:59

commit v6 on v5

--- a/solution.py
+++ b/solution.py
@@ -187,17 +187,19 @@
             return carry
 
         lax.fori_loop(0, count, step, 0)
-        for g in range(GROUPS):
-            at = COUNTS + kind * GROUPS + g
-            used = lists[at]
-            for k in range(WAYS - 1):
-                lists[(kind * GROUPS + g) * LIST + used + k] = SLAB << 11
-            lists[at] = (used + WAYS - 1) // WAYS
-
+
+    def blank(k, carry):
+        lists[k] = SLAB << 11
+        return carry
+
+    lax.fori_loop(0, COUNTS, blank, 0, unroll=8)
     for copy in copies[:4]:
         copy.wait()
     fill(NB, far_rows, far_cols, 0)
     fill(NN, near_rows, near_cols, 1)
+    for g in range(GROUPS):
+        used = jnp.maximum(lists[COUNTS + g], lists[COUNTS + GROUPS + g])
+        lists[COUNTS + g] = (used + WAYS - 1) // WAYS
     for copy in copies[4:]:
         copy.wait()
     line = lax.broadcasted_iota(jnp.int32, (RMAX, LEAF), 0)
@@ -259,25 +261,24 @@
             found.append((e & 63, (e >> 6) & 31, e >> 11))
         return found
 
-    def far_step(q, carry):
-        found = entries(0, q)
+    def step(q, carry):
+        far, near = entries(0, q), entries(1, q)
         coeffs = [
             jnp.dot(v_ref[b], trial[slot], preferred_element_type=F32).astype(BF16)
-            for b, slot, _ in found
+            for b, slot, _ in far
         ]
-        for coeff, (b, _, target) in zip(coeffs, found):
+        terms = []
+        for n, slot, _ in near:
+            block = jnp.concatenate([near_ref[n, 0], near_ref[n, 1]], axis=1)
+            terms.append(jnp.dot(block, trial[slot], preferred_element_type=F32))
+        for term, (_, _, target) in zip(terms, near):
+            total[target] += term
+        for coeff, (b, _, target) in zip(coeffs, far):
             both = jnp.concatenate([coeff, swap_parts(coeff)], axis=0)
             total[target] += jnp.dot(u_ref[b], both, preferred_element_type=F32)
         return carry
 
-    def near_step(q, carry):
-        for n, slot, target in entries(1, q):
-            block = jnp.concatenate([near_ref[n, 0], near_ref[n, 1]], axis=1)
-            total[target] += jnp.dot(block, trial[slot], preferred_element_type=F32)
-        return carry
-
-    lax.fori_loop(0, lists[COUNTS + group], far_step, 0)
-    lax.fori_loop(0, lists[COUNTS + GROUPS + group], near_step, 0)
+    lax.fori_loop(0, lists[COUNTS + group], step, 0)
 
 
 TOTAL = pltpu.VMEM((SLAB + 1, LEAF, COLS), F32)

time: 62.6 us -> 61.9 us (0.989)
  waiting for transfers between devices: 23.6 us -> 26.1 us
  Pallas kernels: 11.2 us -> 8.92 us
    ppermute x5, starting transfers between devices: 13.9 us -> 12.3 us  [along_z(): return lax.ppermute(value, 'col', pairs)]
    ppermute x5, waiting for transfers between devices: 14.1 us -> 15.6 us  [along_z(): return lax.ppermute(value, 'col', pairs)]
    pallas_call x1, Pallas kernels: 2.36 us -> 1.09 us  [blocks(): pl.pallas_call(third_kernel, out_shape=(TOTAL, pltpu.VMEM((16, 2 * LEAF,...]
    ppermute x2, starting transfers between devices: 2.41 us -> 3.6 us  [other_core(): return lax.ppermute(value, 'col', [(d, d ^ 1) for d in range(NZ * NCORE)])]
    ppermute x6, waiting for transfers between devices: 9.52 us -> 10.5 us  [hop(): return lax.ppermute(value, ('row', 'col'), pairs)]
  transfers between devices with their start and end apart: 13 -> 13, of which waited for: 9 -> 9; matrix products, arithmetic and copies ran while one was open for 0% -> 0% of each run, Pallas kernels for 12% -> 10%
where the time goes in v6:
time: 61.9 us; the launch traced here: 61.7 us
  waiting for transfers between devices  26.1 us (42%)
  starting transfers between devices  25.5 us (41%)
  Pallas kernels  8.92 us (14%)
  other arithmetic  0.88 us (1%)
    ppermute x5, waiting for transfers between devices, along_z(): return lax.ppermute(value, 'col', pairs)  15.6 us
    ppermute x5, starting transfers between devices, along_z(): return lax.ppermute(value, 'col', pairs)  12.3 us
    ppermute x6, waiting for transfers between devices, hop(): return lax.ppermute(value, ('row', 'col'), pairs)  10.5 us
    ppermute x6, starting transfers between devices, hop(): return lax.ppermute(value, ('row', 'col'), pairs)  9.59 us
    ppermute x2, starting transfers between devices, other_core(): return lax.ppermute(value, 'col', [(d, d ^ 1) for d in range(NZ * NCORE)])  3.6 us
    pallas_call x1, Pallas kernels, prepare(): pl.pallas_call(prepare_kernel, out_shape=(pltpu.VMEM((NB, LEAF, 2 * RMAX)...  3.07 us
    pallas_call x1, Pallas kernels, order(): pl.pallas_call(order_kernel, out_shape=pltpu.VMEM((2 * LEAF, COLS), BF16)...  1.27 us
  transfers between devices with their start and end apart: 13, of which 9 were waited for; matrix products, arithmetic and copies ran while one was open for 0% of the time, Pallas kernels for 10%

profile of v6, /device:TPU:1, one launch (start us, length us, event | category | flops | bytes accessed | tf_op | source)
XLA Modules:
  0.0 61.7 jit_solution(13575547966150354039)
XLA Ops:
  0.0 0.0 copy-start
  0.0 1.3 %shard_map.101.refs_0_ = bf16[256,256]{1,0:T(8,128)(2,1)S(1)} custom-call(s32[2,128]{1,0:T(2,128)} %perm_hbm.1, bf16[256,256]{1,0:T(8,128)(2,1)} %x_hbm.1), custom_call_target="tpu_custom_call" | custom-call | tf_op jit(solution)/shard_map/pallas_call | solution.py:91
  1.3 3.8 %collective-permute-start.2 = (bf16[256,256]{1,0:T(8,128)(2,1)S(1)}, bf16[256,256]{1,0:T(8,128)(2,1)S(1)}, u32[]{:S(2)}, u32[]{:S(2)}) collective-permute-start(bf16[256,256]{1,0:T(8,128)(2,1)S(1)} %shard_map.101.refs_0_), channel_id=1, source_target_pairs={{0,128},{1,33},{2,130},{3,35},{4,132},{5,37},{6,134},{7,39},{8,136... | collective-permute-start | bytes 393224 | tf_op jit(solution)/shard_map/ppermute | solution.py:50
  5.1 0.8 %collective-permute-start.1 = (bf16[256,256]{1,0:T(8,128)(2,1)S(1)}, bf16[256,256]{1,0:T(8,128)(2,1)S(1)}, u32[]{:S(2)}, u32[]{:S(2)}) collective-permute-start(bf16[256,256]{1,0:T(8,128)(2,1)S(1)} %shard_map.101.refs_0_), channel_id=1, source_target_pairs={{0,192},{1,49},{2,194},{3,51},{4,196},{5,53},{6,198},{7,55},{8,200... | collective-permute-start | bytes 393224 | tf_op jit(solution)/shard_map/ppermute | solution.py:50
  5.9 0.7 %collective-permute-start = (bf16[256,256]{1,0:T(8,128)(2,1)S(1)}, bf16[256,256]{1,0:T(8,128)(2,1)S(1)}, u32[]{:S(2)}, u32[]{:S(2)}) collective-permute-start(bf16[256,256]{1,0:T(8,128)(2,1)S(1)} %shard_map.101.refs_0_), channel_id=1, source_target_pairs={{0,64},{1,17},{2,66},{3,19},{4,68},{5,21},{6,70},{7,23},{8,72},{9,... | collective-permute-start | bytes 393224 | tf_op jit(solution)/shard_map/ppermute | solution.py:50
  6.6 0.9 %collective-permute-done.2.refs_3_ = bf16[256,256]{1,0:T(8,128)(2,1)S(1)} collective-permute-done((bf16[256,256]{1,0:T(8,128)(2,1)S(1)}, bf16[256,256]{1,0:T(8,128)(2,1)S(1)}, u32[]{:S(2)}, u32[]{:S(2)}) %collective-permute-start.2) | collective-permute-done | bytes 131104 | tf_op jit(solution)/shard_map/ppermute | solution.py:50
  7.5 2.1 %collective-permute-done.1.refs_2_ = bf16[256,256]{1,0:T(8,128)(2,1)S(1)} collective-permute-done((bf16[256,256]{1,0:T(8,128)(2,1)S(1)}, bf16[256,256]{1,0:T(8,128)(2,1)S(1)}, u32[]{:S(2)}, u32[]{:S(2)}) %collective-permute-start.1) | collective-permute-done | bytes 131104 | tf_op jit(solution)/shard_map/ppermute | solution.py:50
  9.6 1.4 %collective-permute-done.refs_1_ = bf16[256,256]{1,0:T(8,128)(2,1)S(1)} collective-permute-done((bf16[256,256]{1,0:T(8,128)(2,1)S(1)}, bf16[256,256]{1,0:T(8,128)(2,1)S(1)}, u32[]{:S(2)}, u32[]{:S(2)}) %collective-permute-start) | collective-permute-done | bytes 131104 | tf_op jit(solution)/shard_map/ppermute | solution.py:50
  11.0 2.8 %collective-permute-start.5 = (bf16[1024,256]{1,0:T(8,128)(2,1)S(1)}, bf16[1024,256]{1,0:T(8,128)(2,1)S(1)}, u32[]{:S(2)}, u32[]{:S(2)}) collective-permute-start(bf16[1024,256]{1,0:T(8,128)(2,1)S(1)} %shard_map.102.piece), channel_id=1, source_target_pairs={{0,32},{1,129},{2,34},{3,131},{4,36},{5,133},{6,38},{7,135},{8,40}... | collective-permute-start | bytes 1572872 | tf_op jit(solution)/shard_map/ppermute | solution.py:50
  13.8 0.9 %collective-permute-start.4 = (bf16[1024,256]{1,0:T(8,128)(2,1)S(1)}, bf16[1024,256]{1,0:T(8,128)(2,1)S(1)}, u32[]{:S(2)}, u32[]{:S(2)}) collective-permute-start(bf16[1024,256]{1,0:T(8,128)(2,1)S(1)} %shard_map.102.piece), channel_id=1, source_target_pairs={{0,48},{1,193},{2,50},{3,195},{4,52},{5,197},{6,54},{7,199},{8,56}... | collective-permute-start | bytes 1572872 | tf_op jit(solution)/shard_map/ppermute | solution.py:50
  14.6 0.6 collective-permute-start.3
  15.3 3.1 %shard_map.100 = (bf16[32,128,128]{2,1,0:T(8,128)(2,1)S(1)}, bf16[32,64,256]{2,1,0:T(8,128)(2,1)S(1)}, s32[296]{0:T(512)S(4)}) custom-call(s32[32]{0:T(128)} %rank_hbm.1, s32[32]{0:T(128)} %far_rows_hbm.1, s32[32]{0:T(128)} %far_cols_hbm.1, s32[28]{0:T(128)} %near_rows_hbm.1, s32[28]{0:T(128)} %near_cols_hbm.1, bf16[32,2,64,128]{3,2,1,0:T(8,128)(2,1)} %bitcast.20, ...), custom_call_target="tpu_custom_call" | custom-call | bytes 8388608 | tf_op jit(solution)/shard_map/pallas_call | solution.py:221
  18.3 0.0 copy-done
  18.3 1.2 %shard_map.103._ = f32[33,128,256]{2,1,0:T(8,128)S(1)} custom-call(s32[296]{0:T(512)S(4)} %get-tuple-element.15.lists, bf16[32,128,128]{2,1,0:T(8,128)(2,1)S(1)} %get-tuple-element.16.u_ref, bf16[32,64,256]{2,1,0:T(8,128)(2,1)S(1)} %get-tuple-element.17.v_ref, bf16[28,2,128,128]{3,2,1,0:T(8,128)(2,1)S(1)} %copy-done, bf16[1024,256]{1,0:T(8,128)(2,1)S(1)} %shard_map.102.piece), custom_call_target="tpu_custom_call" | custom-call | bytes 8388608 | tf_op jit(solution)/shard_map/pallas_call | solution.py:315
  19.5 1.4 %collective-permute-done.5.piece = bf16[1024,256]{1,0:T(8,128)(2,1)S(1)} collective-permute-done((bf16[1024,256]{1,0:T(8,128)(2,1)S(1)}, bf16[1024,256]{1,0:T(8,128)(2,1)S(1)}, u32[]{:S(2)}, u32[]{:S(2)}) %collective-permute-start.5) | collective-permute-done | bytes 524320 | tf_op jit(solution)/shard_map/ppermute | solution.py:50
  20.9 0.9 %shard_map.104._ = f32[33,128,256]{2,1,0:T(8,128)S(1)} custom-call(s32[296]{0:T(512)S(4)} %get-tuple-element.15.lists, bf16[32,128,128]{2,1,0:T(8,128)(2,1)S(1)} %get-tuple-element.16.u_ref, bf16[32,64,256]{2,1,0:T(8,128)(2,1)S(1)} %get-tuple-element.17.v_ref, bf16[28,2,128,128]{3,2,1,0:T(8,128)(2,1)S(1)} %copy-done, ...), custom_call_target="tpu_custom_call", output_to_operand_aliasing={{}: (5, {})} | custom-call | bytes 6291456 | tf_op jit(solution)/shard_map/pallas_call | solution.py:324
  21.8 4.8 %collective-permute-done.4.back = bf16[1024,256]{1,0:T(8,128)(2,1)S(1)} collective-permute-done((bf16[1024,256]{1,0:T(8,128)(2,1)S(1)}, bf16[1024,256]{1,0:T(8,128)(2,1)S(1)}, u32[]{:S(2)}, u32[]{:S(2)}) %collective-permute-start.4) | collective-permute-done | bytes 524320 | tf_op jit(solution)/shard_map/ppermute | solution.py:50
  26.6 0.0 collective-permute-done.3.ahead
  26.6 1.1 %shard_map.105 = (f32[33,128,256]{2,1,0:T(8,128)S(1)}, bf16[16,256,256]{2,1,0:T(8,128)(2,1)S(1)}, bf16[768,256]{1,0:T(8,128)(2,1)S(1)}, bf16[1280,256]{1,0:T(8,128)(2,1)S(1)}) custom-call(s32[296]{0:T(512)S(4)} %get-tuple-element.15.lists, bf16[32,128,128]{2,1,0:T(8,128)(2,1)S(1)} %get-tuple-element.16.u_ref, ...), custom_call_target="tpu_custom_call", output_to_operand_aliasing={{0}: (6, {})} | custom-call | bytes 8388608 | tf_op jit(solution)/shard_map/pallas_call | solution.py:334
  27.7 3.5 %collective-permute-start.7 = (bf16[768,256]{1,0:T(8,128)(2,1)S(1)}, bf16[768,256]{1,0:T(8,128)(2,1)S(1)}, u32[]{:S(2)}, u32[]{:S(2)}) collective-permute-start(bf16[768,256]{1,0:T(8,128)(2,1)S(1)} %get-tuple-element.21), channel_id=1, source_target_pairs={{0,1},{1,0},{2,3},{3,2},{4,5},{5,4},{6,7},{7,6},{8,9},{9,8},{10,11... | collective-permute-start | bytes 1179656 | tf_op jit(solution)/shard_map/ppermute | solution.py:63
  31.2 0.1 collective-permute-start.6
  31.3 1.2 %shard_map.106.own = f32[33,128,256]{2,1,0:T(8,128)S(1)} custom-call(s32[296]{0:T(512)S(4)} %get-tuple-element.15.lists, bf16[32,128,128]{2,1,0:T(8,128)(2,1)S(1)} %get-tuple-element.16.u_ref, bf16[32,64,256]{2,1,0:T(8,128)(2,1)S(1)} %get-tuple-element.17.v_ref, bf16[28,2,128,128]{3,2,1,0:T(8,128)(2,1)S(1)} %copy-done, ...), custom_call_target="tpu_custom_call", output_to_operand_aliasing={{}: (5, {})} | custom-call | bytes 6291456 | tf_op jit(solution)/shard_map/pallas_call | solution.py:348
  32.6 0.1 slice.26
  32.7 0.0 collective-permute-done.7
  32.7 0.1 fusion
  32.8 6.4 %collective-permute-start.8 = (bf16[768,256]{1,0:T(8,128)(2,1)S(1)}, bf16[768,256]{1,0:T(8,128)(2,1)S(1)}, u32[]{:S(2)}, u32[]{:S(2)}) collective-permute-start(bf16[768,256]{1,0:T(8,128)(2,1)S(1)} %fusion), channel_id=1, source_target_pairs={{0,4},{1,13},{2,6},{3,15},{4,8},{5,1},{6,10},{7,3},{8,12},{9,5},{1... | collective-permute-start | bytes 1179656 | tf_op jit(solution)/shard_map/ppermute | solution.py:59
  39.2 0.0 collective-permute-done.6.swapped
  39.2 0.1 fusion.1
  39.2 0.4 collective-permute-start.9
  39.6 8.5 %collective-permute-done.8.middle = bf16[768,256]{1,0:T(8,128)(2,1)S(1)} collective-permute-done((bf16[768,256]{1,0:T(8,128)(2,1)S(1)}, bf16[768,256]{1,0:T(8,128)(2,1)S(1)}, u32[]{:S(2)}, u32[]{:S(2)}) %collective-permute-start.8) | collective-permute-done | bytes 393248 | tf_op jit(solution)/shard_map/ppermute | solution.py:59
  48.1 2.8 %collective-permute-done.9.close = bf16[512,256]{1,0:T(8,128)(2,1)S(1)} collective-permute-done((bf16[512,256]{1,0:T(8,128)(2,1)S(1)}, bf16[512,256]{1,0:T(8,128)(2,1)S(1)}, u32[]{:S(2)}, u32[]{:S(2)}) %collective-permute-start.9) | collective-permute-done | bytes 262176 | tf_op jit(solution)/shard_map/ppermute | solution.py:59
  50.9 0.1 shard_map.107
  51.0 2.3 %collective-permute-start.10 = (bf16[256,256]{1,0:T(8,128)(2,1)S(1)}, bf16[256,256]{1,0:T(8,128)(2,1)S(1)}, u32[]{:S(2)}, u32[]{:S(2)}) collective-permute-start(bf16[256,256]{1,0:T(8,128)(2,1)S(1)} %slice.27), channel_id=1, source_target_pairs={{0,4},{1,13},{2,6},{3,15},{4,8},{5,1},{6,10},{7,3},{8,12},{9,5},{1... | collective-permute-start | bytes 393224 | tf_op jit(solution)/shard_map/ppermute | solution.py:59
  53.4 0.5 collective-permute-start.12
  53.9 2.7 %collective-permute-start.11 = (bf16[256,256]{1,0:T(8,128)(2,1)S(1)}, bf16[256,256]{1,0:T(8,128)(2,1)S(1)}, u32[]{:S(2)}, u32[]{:S(2)}) collective-permute-start(bf16[256,256]{1,0:T(8,128)(2,1)S(1)} %get-tuple-element.22), channel_id=1, source_target_pairs={{0,2},{1,15},{2,4},{3,1},{4,6},{5,3},{6,8},{7,5},{8,10},{9,7},{10,... | collective-permute-start | bytes 393224 | tf_op jit(solution)/shard_map/ppermute | solution.py:59
  56.6 0.0 collective-permute-done.10
  56.6 3.8 %collective-permute-done.12 = bf16[256,256]{1,0:T(8,128)(2,1)S(1)} collective-permute-done((bf16[256,256]{1,0:T(8,128)(2,1)S(1)}, bf16[256,256]{1,0:T(8,128)(2,1)S(1)}, u32[]{:S(2)}, u32[]{:S(2)}) %collective-permute-start.12) | collective-permute-done | bytes 131104 | tf_op jit(solution)/shard_map/ppermute | solution.py:59
  60.4 0.5 collective-permute-done.11
  60.9 0.7 %fusion.5 = bf16[256,256]{1,0:T(8,128)(2,1)} fusion(f32[2,128,256]{2,1,0:T(8,128)S(1)} %slice.24, bf16[256,256]{1,0:T(8,128)(2,1)S(1)} %collective-permute-done.12, bf16[256,256]{1,0:T(8,128)(2,1)S(1)} %collective-permute-done.11, bf16[256,256]{1,0:T(8,128)(2,1)S(1)} %collective-permute-done.10, bf16[1280,256]{1,0:T(8,128)(2,1)S(1)} %collective-permute-done.6.swapped), kind=kLoop, calls=%fused_computation.8 | loop fusion | flops 589824 | bytes 917504 | tf_op jit(solution)/shard_map/convert_element_type | solution.py:407
  (4 shorter events, 0.1 us)
Async XLA Ops:
  0.0 18.3 %copy-start = (bf16[28,2,128,128]{3,2,1,0:T(8,128)(2,1)S(1)}, bf16[28,2,128,128]{3,2,1,0:T(8,128)(2,1)}, u32[]{:S(2)}) copy-start(bf16[28,2,128,128]{3,2,1,0:T(8,128)(2,1)} %near_ref.7) | copy-start | bytes 5505028
  1.3 6.2 %collective-permute-start.2 = (bf16[256,256]{1,0:T(8,128)(2,1)S(1)}, bf16[256,256]{1,0:T(8,128)(2,1)S(1)}, u32[]{:S(2)}, u32[]{:S(2)}) collective-permute-start(bf16[256,256]{1,0:T(8,128)(2,1)S(1)} %shard_map.101.refs_0_), channel_id=1, source_target_pairs={{0,128},{1,33},{2,130},{3,35},{4,132},{5,37},{6,134},{7,39},{8,136... | collective-permute-start | bytes 393224 | tf_op jit(solution)/shard_map/ppermute | solution.py:50
  5.1 4.4 %collective-permute-start.1 = (bf16[256,256]{1,0:T(8,128)(2,1)S(1)}, bf16[256,256]{1,0:T(8,128)(2,1)S(1)}, u32[]{:S(2)}, u32[]{:S(2)}) collective-permute-start(bf16[256,256]{1,0:T(8,128)(2,1)S(1)} %shard_map.101.refs_0_), channel_id=1, source_target_pairs={{0,192},{1,49},{2,194},{3,51},{4,196},{5,53},{6,198},{7,55},{8,200... | collective-permute-start | bytes 393224 | tf_op jit(solution)/shard_map/ppermute | solution.py:50
  5.9 5.0 %collective-permute-start = (bf16[256,256]{1,0:T(8,128)(2,1)S(1)}, bf16[256,256]{1,0:T(8,128)(2,1)S(1)}, u32[]{:S(2)}, u32[]{:S(2)}) collective-permute-start(bf16[256,256]{1,0:T(8,128)(2,1)S(1)} %shard_map.101.refs_0_), channel_id=1, source_target_pairs={{0,64},{1,17},{2,66},{3,19},{4,68},{5,21},{6,70},{7,23},{8,72},{9,... | collective-permute-start | bytes 393224 | tf_op jit(solution)/shard_map/ppermute | solution.py:50
  11.0 10.0 %collective-permute-start.5 = (bf16[1024,256]{1,0:T(8,128)(2,1)S(1)}, bf16[1024,256]{1,0:T(8,128)(2,1)S(1)}, u32[]{:S(2)}, u32[]{:S(2)}) collective-permute-start(bf16[1024,256]{1,0:T(8,128)(2,1)S(1)} %shard_map.102.piece), channel_id=1, source_target_pairs={{0,32},{1,129},{2,34},{3,131},{4,36},{5,133},{6,38},{7,135},{8,40}... | collective-permute-start | bytes 1572872 | tf_op jit(solution)/shard_map/ppermute | solution.py:50
  13.8 12.8 %collective-permute-start.4 = (bf16[1024,256]{1,0:T(8,128)(2,1)S(1)}, bf16[1024,256]{1,0:T(8,128)(2,1)S(1)}, u32[]{:S(2)}, u32[]{:S(2)}) collective-permute-start(bf16[1024,256]{1,0:T(8,128)(2,1)S(1)} %shard_map.102.piece), channel_id=1, source_target_pairs={{0,48},{1,193},{2,50},{3,195},{4,52},{5,197},{6,54},{7,199},{8,56}... | collective-permute-start | bytes 1572872 | tf_op jit(solution)/shard_map/ppermute | solution.py:50
  14.6 12.0 %collective-permute-start.3 = (bf16[1024,256]{1,0:T(8,128)(2,1)S(1)}, bf16[1024,256]{1,0:T(8,128)(2,1)S(1)}, u32[]{:S(2)}, u32[]{:S(2)}) collective-permute-start(bf16[1024,256]{1,0:T(8,128)(2,1)S(1)} %shard_map.102.piece), channel_id=1, source_target_pairs={{0,16},{1,65},{2,18},{3,67},{4,20},{5,69},{6,22},{7,71},{8,24},{9,... | collective-permute-start | bytes 1572872 | tf_op jit(solution)/shard_map/ppermute | solution.py:50
  27.7 5.0 %collective-permute-start.7 = (bf16[768,256]{1,0:T(8,128)(2,1)S(1)}, bf16[768,256]{1,0:T(8,128)(2,1)S(1)}, u32[]{:S(2)}, u32[]{:S(2)}) collective-permute-start(bf16[768,256]{1,0:T(8,128)(2,1)S(1)} %get-tuple-element.21), channel_id=1, source_target_pairs={{0,1},{1,0},{2,3},{3,2},{4,5},{5,4},{6,7},{7,6},{8,9},{9,8},{10,11... | collective-permute-start | bytes 1179656 | tf_op jit(solution)/shard_map/ppermute | solution.py:63
  31.2 8.0 %collective-permute-start.6 = (bf16[1280,256]{1,0:T(8,128)(2,1)S(1)}, bf16[1280,256]{1,0:T(8,128)(2,1)S(1)}, u32[]{:S(2)}, u32[]{:S(2)}) collective-permute-start(bf16[1280,256]{1,0:T(8,128)(2,1)S(1)} %get-tuple-element.20), channel_id=1, source_target_pairs={{0,1},{1,0},{2,3},{3,2},{4,5},{5,4},{6,7},{7,6},{8,9},{9,8},{10,11... | collective-permute-start | bytes 1966088 | tf_op jit(solution)/shard_map/ppermute | solution.py:63
  32.8 15.3 %collective-permute-start.8 = (bf16[768,256]{1,0:T(8,128)(2,1)S(1)}, bf16[768,256]{1,0:T(8,128)(2,1)S(1)}, u32[]{:S(2)}, u32[]{:S(2)}) collective-permute-start(bf16[768,256]{1,0:T(8,128)(2,1)S(1)} %fusion), channel_id=1, source_target_pairs={{0,4},{1,13},{2,6},{3,15},{4,8},{5,1},{6,10},{7,3},{8,12},{9,5},{1... | collective-permute-start | bytes 1179656 | tf_op jit(solution)/shard_map/ppermute | solution.py:59
  39.2 11.7 %collective-permute-start.9 = (bf16[512,256]{1,0:T(8,128)(2,1)S(1)}, bf16[512,256]{1,0:T(8,128)(2,1)S(1)}, u32[]{:S(2)}, u32[]{:S(2)}) collective-permute-start(bf16[512,256]{1,0:T(8,128)(2,1)S(1)} %fusion.1), channel_id=1, source_target_pairs={{0,2},{1,15},{2,4},{3,1},{4,6},{5,3},{6,8},{7,5},{8,10},{9,7},{10,... | collective-permute-start | bytes 786440 | tf_op jit(solution)/shard_map/ppermute | solution.py:59
  51.0 5.6 %collective-permute-start.10 = (bf16[256,256]{1,0:T(8,128)(2,1)S(1)}, bf16[256,256]{1,0:T(8,128)(2,1)S(1)}, u32[]{:S(2)}, u32[]{:S(2)}) collective-permute-start(bf16[256,256]{1,0:T(8,128)(2,1)S(1)} %slice.27), channel_id=1, source_target_pairs={{0,4},{1,13},{2,6},{3,15},{4,8},{5,1},{6,10},{7,3},{8,12},{9,5},{1... | collective-permute-start | bytes 393224 | tf_op jit(solution)/shard_map/ppermute | solution.py:59
  53.4 7.0 %collective-permute-start.12 = (bf16[256,256]{1,0:T(8,128)(2,1)S(1)}, bf16[256,256]{1,0:T(8,128)(2,1)S(1)}, u32[]{:S(2)}, u32[]{:S(2)}) collective-permute-start(bf16[256,256]{1,0:T(8,128)(2,1)S(1)} %get-tuple-element.24), channel_id=1, source_target_pairs={{0,3},{1,14},{2,5},{3,0},{4,7},{5,2},{6,9},{7,4},{8,11},{9,6},{10,... | collective-permute-start | bytes 393224 | tf_op jit(solution)/shard_map/ppermute | solution.py:59
  53.9 7.0 %collective-permute-start.11 = (bf16[256,256]{1,0:T(8,128)(2,1)S(1)}, bf16[256,256]{1,0:T(8,128)(2,1)S(1)}, u32[]{:S(2)}, u32[]{:S(2)}) collective-permute-start(bf16[256,256]{1,0:T(8,128)(2,1)S(1)} %get-tuple-element.22), channel_id=1, source_target_pairs={{0,2},{1,15},{2,4},{3,1},{4,6},{5,3},{6,8},{7,5},{8,10},{9,7},{10,... | collective-permute-start | bytes 393224 | tf_op jit(solution)/shard_map/ppermute | solution.py:59

commit v7 on v6

--- a/solution.py
+++ b/solution.py
@@ -16,7 +16,7 @@
 NZ = 8
 NCORE = 2
 SLAB = 32
-WAYS = 4
+WAYS = 6
 GROUPS = 4
 LIST = 36
 COUNTS = 2 * GROUPS * LIST

time: 61.9 us -> 61.8 us (level)
  transfers between devices with their start and end apart: 13 -> 13, of which waited for: 9 -> 10; matrix products, arithmetic and copies ran while one was open for 0% -> 0% of each run, Pallas kernels for 10% -> 11%
where the time goes in v7:
time: 61.8 us; the launch traced here: 61.5 us
  waiting for transfers between devices  25.9 us (42%)
  starting transfers between devices  25 us (40%)
  Pallas kernels  9.42 us (15%)
  other arithmetic  0.88 us (1%)
    ppermute x5, waiting for transfers between devices, along_z(): return lax.ppermute(value, 'col', pairs)  15.8 us
    ppermute x5, starting transfers between devices, along_z(): return lax.ppermute(value, 'col', pairs)  11.8 us
    ppermute x6, waiting for transfers between devices, hop(): return lax.ppermute(value, ('row', 'col'), pairs)  10 us
    ppermute x6, starting transfers between devices, hop(): return lax.ppermute(value, ('row', 'col'), pairs)  9.59 us
    ppermute x2, starting transfers between devices, other_core(): return lax.ppermute(value, 'col', [(d, d ^ 1) for d in range(NZ * NCORE)])  3.6 us
    pallas_call x1, Pallas kernels, prepare(): pl.pallas_call(prepare_kernel, out_shape=(pltpu.VMEM((NB, LEAF, 2 * RMAX)...  3.09 us
    pallas_call x1, Pallas kernels, blocks(): pl.pallas_call(first_kernel, out_shape=TOTAL, in_specs=[SMEM] + [VMEM] *...  1.41 us
    pallas_call x1, Pallas kernels, blocks(): pl.pallas_call(third_kernel, out_shape=(TOTAL, pltpu.VMEM((16, 2 * LEAF,...  1.32 us
  transfers between devices with their start and end apart: 13, of which 10 were waited for; matrix products, arithmetic and copies ran while one was open for 0% of the time, Pallas kernels for 11%

profile of v7, /device:TPU:1, one launch (start us, length us, event | category | flops | bytes accessed | tf_op | source)
XLA Modules:
  0.0 61.5 jit_solution(3733138888166942683)
XLA Ops:
  0.0 0.0 copy-start
  0.0 1.3 %shard_map.101.refs_0_ = bf16[256,256]{1,0:T(8,128)(2,1)S(1)} custom-call(s32[2,128]{1,0:T(2,128)} %perm_hbm.1, bf16[256,256]{1,0:T(8,128)(2,1)} %x_hbm.1), custom_call_target="tpu_custom_call" | custom-call | tf_op jit(solution)/shard_map/pallas_call | solution.py:91
  1.3 3.8 %collective-permute-start.2 = (bf16[256,256]{1,0:T(8,128)(2,1)S(1)}, bf16[256,256]{1,0:T(8,128)(2,1)S(1)}, u32[]{:S(2)}, u32[]{:S(2)}) collective-permute-start(bf16[256,256]{1,0:T(8,128)(2,1)S(1)} %shard_map.101.refs_0_), channel_id=1, source_target_pairs={{0,128},{1,33},{2,130},{3,35},{4,132},{5,37},{6,134},{7,39},{8,136... | collective-permute-start | bytes 393224 | tf_op jit(solution)/shard_map/ppermute | solution.py:50
  5.1 0.8 %collective-permute-start.1 = (bf16[256,256]{1,0:T(8,128)(2,1)S(1)}, bf16[256,256]{1,0:T(8,128)(2,1)S(1)}, u32[]{:S(2)}, u32[]{:S(2)}) collective-permute-start(bf16[256,256]{1,0:T(8,128)(2,1)S(1)} %shard_map.101.refs_0_), channel_id=1, source_target_pairs={{0,192},{1,49},{2,194},{3,51},{4,196},{5,53},{6,198},{7,55},{8,200... | collective-permute-start | bytes 393224 | tf_op jit(solution)/shard_map/ppermute | solution.py:50
  5.9 0.7 %collective-permute-start = (bf16[256,256]{1,0:T(8,128)(2,1)S(1)}, bf16[256,256]{1,0:T(8,128)(2,1)S(1)}, u32[]{:S(2)}, u32[]{:S(2)}) collective-permute-start(bf16[256,256]{1,0:T(8,128)(2,1)S(1)} %shard_map.101.refs_0_), channel_id=1, source_target_pairs={{0,64},{1,17},{2,66},{3,19},{4,68},{5,21},{6,70},{7,23},{8,72},{9,... | collective-permute-start | bytes 393224 | tf_op jit(solution)/shard_map/ppermute | solution.py:50
  6.6 0.9 %collective-permute-done.2.refs_3_ = bf16[256,256]{1,0:T(8,128)(2,1)S(1)} collective-permute-done((bf16[256,256]{1,0:T(8,128)(2,1)S(1)}, bf16[256,256]{1,0:T(8,128)(2,1)S(1)}, u32[]{:S(2)}, u32[]{:S(2)}) %collective-permute-start.2) | collective-permute-done | bytes 131104 | tf_op jit(solution)/shard_map/ppermute | solution.py:50
  7.5 2.1 %collective-permute-done.1.refs_2_ = bf16[256,256]{1,0:T(8,128)(2,1)S(1)} collective-permute-done((bf16[256,256]{1,0:T(8,128)(2,1)S(1)}, bf16[256,256]{1,0:T(8,128)(2,1)S(1)}, u32[]{:S(2)}, u32[]{:S(2)}) %collective-permute-start.1) | collective-permute-done | bytes 131104 | tf_op jit(solution)/shard_map/ppermute | solution.py:50
  9.6 1.4 %collective-permute-done.refs_1_ = bf16[256,256]{1,0:T(8,128)(2,1)S(1)} collective-permute-done((bf16[256,256]{1,0:T(8,128)(2,1)S(1)}, bf16[256,256]{1,0:T(8,128)(2,1)S(1)}, u32[]{:S(2)}, u32[]{:S(2)}) %collective-permute-start) | collective-permute-done | bytes 131104 | tf_op jit(solution)/shard_map/ppermute | solution.py:50
  11.0 2.8 %collective-permute-start.5 = (bf16[1024,256]{1,0:T(8,128)(2,1)S(1)}, bf16[1024,256]{1,0:T(8,128)(2,1)S(1)}, u32[]{:S(2)}, u32[]{:S(2)}) collective-permute-start(bf16[1024,256]{1,0:T(8,128)(2,1)S(1)} %shard_map.102.piece), channel_id=1, source_target_pairs={{0,32},{1,129},{2,34},{3,131},{4,36},{5,133},{6,38},{7,135},{8,40}... | collective-permute-start | bytes 1572872 | tf_op jit(solution)/shard_map/ppermute | solution.py:50
  13.8 0.9 %collective-permute-start.4 = (bf16[1024,256]{1,0:T(8,128)(2,1)S(1)}, bf16[1024,256]{1,0:T(8,128)(2,1)S(1)}, u32[]{:S(2)}, u32[]{:S(2)}) collective-permute-start(bf16[1024,256]{1,0:T(8,128)(2,1)S(1)} %shard_map.102.piece), channel_id=1, source_target_pairs={{0,48},{1,193},{2,50},{3,195},{4,52},{5,197},{6,54},{7,199},{8,56}... | collective-permute-start | bytes 1572872 | tf_op jit(solution)/shard_map/ppermute | solution.py:50
  14.6 0.6 collective-permute-start.3
  15.3 3.1 %shard_map.100 = (bf16[32,128,128]{2,1,0:T(8,128)(2,1)S(1)}, bf16[32,64,256]{2,1,0:T(8,128)(2,1)S(1)}, s32[296]{0:T(512)S(4)}) custom-call(s32[32]{0:T(128)} %rank_hbm.1, s32[32]{0:T(128)} %far_rows_hbm.1, s32[32]{0:T(128)} %far_cols_hbm.1, s32[28]{0:T(128)} %near_rows_hbm.1, s32[28]{0:T(128)} %near_cols_hbm.1, bf16[32,2,64,128]{3,2,1,0:T(8,128)(2,1)} %bitcast.20, ...), custom_call_target="tpu_custom_call" | custom-call | bytes 8388608 | tf_op jit(solution)/shard_map/pallas_call | solution.py:221
  18.4 0.0 copy-done
  18.4 1.4 %shard_map.103._ = f32[33,128,256]{2,1,0:T(8,128)S(1)} custom-call(s32[296]{0:T(512)S(4)} %get-tuple-element.15.lists, bf16[32,128,128]{2,1,0:T(8,128)(2,1)S(1)} %get-tuple-element.16.u_ref, bf16[32,64,256]{2,1,0:T(8,128)(2,1)S(1)} %get-tuple-element.17.v_ref, bf16[28,2,128,128]{3,2,1,0:T(8,128)(2,1)S(1)} %copy-done, bf16[1024,256]{1,0:T(8,128)(2,1)S(1)} %shard_map.102.piece), custom_call_target="tpu_custom_call" | custom-call | bytes 8388608 | tf_op jit(solution)/shard_map/pallas_call | solution.py:315
  19.8 1.1 %collective-permute-done.5.piece = bf16[1024,256]{1,0:T(8,128)(2,1)S(1)} collective-permute-done((bf16[1024,256]{1,0:T(8,128)(2,1)S(1)}, bf16[1024,256]{1,0:T(8,128)(2,1)S(1)}, u32[]{:S(2)}, u32[]{:S(2)}) %collective-permute-start.5) | collective-permute-done | bytes 524320 | tf_op jit(solution)/shard_map/ppermute | solution.py:50
  20.9 1.1 %shard_map.104._ = f32[33,128,256]{2,1,0:T(8,128)S(1)} custom-call(s32[296]{0:T(512)S(4)} %get-tuple-element.15.lists, bf16[32,128,128]{2,1,0:T(8,128)(2,1)S(1)} %get-tuple-element.16.u_ref, bf16[32,64,256]{2,1,0:T(8,128)(2,1)S(1)} %get-tuple-element.17.v_ref, bf16[28,2,128,128]{3,2,1,0:T(8,128)(2,1)S(1)} %copy-done, ...), custom_call_target="tpu_custom_call", output_to_operand_aliasing={{}: (5, {})} | custom-call | bytes 6291456 | tf_op jit(solution)/shard_map/pallas_call | solution.py:324
  22.1 4.6 %collective-permute-done.4.back = bf16[1024,256]{1,0:T(8,128)(2,1)S(1)} collective-permute-done((bf16[1024,256]{1,0:T(8,128)(2,1)S(1)}, bf16[1024,256]{1,0:T(8,128)(2,1)S(1)}, u32[]{:S(2)}, u32[]{:S(2)}) %collective-permute-start.4) | collective-permute-done | bytes 524320 | tf_op jit(solution)/shard_map/ppermute | solution.py:50
  26.6 0.0 collective-permute-done.3.ahead
  26.6 1.3 %shard_map.105 = (f32[33,128,256]{2,1,0:T(8,128)S(1)}, bf16[16,256,256]{2,1,0:T(8,128)(2,1)S(1)}, bf16[768,256]{1,0:T(8,128)(2,1)S(1)}, bf16[1280,256]{1,0:T(8,128)(2,1)S(1)}) custom-call(s32[296]{0:T(512)S(4)} %get-tuple-element.15.lists, bf16[32,128,128]{2,1,0:T(8,128)(2,1)S(1)} %get-tuple-element.16.u_ref, ...), custom_call_target="tpu_custom_call", output_to_operand_aliasing={{0}: (6, {})} | custom-call | bytes 8388608 | tf_op jit(solution)/shard_map/pallas_call | solution.py:334
  28.0 3.5 %collective-permute-start.7 = (bf16[768,256]{1,0:T(8,128)(2,1)S(1)}, bf16[768,256]{1,0:T(8,128)(2,1)S(1)}, u32[]{:S(2)}, u32[]{:S(2)}) collective-permute-start(bf16[768,256]{1,0:T(8,128)(2,1)S(1)} %get-tuple-element.21), channel_id=1, source_target_pairs={{0,1},{1,0},{2,3},{3,2},{4,5},{5,4},{6,7},{7,6},{8,9},{9,8},{10,11... | collective-permute-start | bytes 1179656 | tf_op jit(solution)/shard_map/ppermute | solution.py:63
  31.5 0.1 collective-permute-start.6
  31.6 1.0 %shard_map.106.own = f32[33,128,256]{2,1,0:T(8,128)S(1)} custom-call(s32[296]{0:T(512)S(4)} %get-tuple-element.15.lists, bf16[32,128,128]{2,1,0:T(8,128)(2,1)S(1)} %get-tuple-element.16.u_ref, bf16[32,64,256]{2,1,0:T(8,128)(2,1)S(1)} %get-tuple-element.17.v_ref, bf16[28,2,128,128]{3,2,1,0:T(8,128)(2,1)S(1)} %copy-done, ...), custom_call_target="tpu_custom_call", output_to_operand_aliasing={{}: (5, {})} | custom-call | bytes 6291456 | tf_op jit(solution)/shard_map/pallas_call | solution.py:348
  32.6 0.1 slice.26
  32.7 0.1 collective-permute-done.7
  32.8 0.1 fusion
  32.9 6.1 %collective-permute-start.8 = (bf16[768,256]{1,0:T(8,128)(2,1)S(1)}, bf16[768,256]{1,0:T(8,128)(2,1)S(1)}, u32[]{:S(2)}, u32[]{:S(2)}) collective-permute-start(bf16[768,256]{1,0:T(8,128)(2,1)S(1)} %fusion), channel_id=1, source_target_pairs={{0,4},{1,13},{2,6},{3,15},{4,8},{5,1},{6,10},{7,3},{8,12},{9,5},{1... | collective-permute-start | bytes 1179656 | tf_op jit(solution)/shard_map/ppermute | solution.py:59
  39.0 0.0 collective-permute-done.6.swapped
  39.0 0.1 fusion.1
  39.0 0.4 collective-permute-start.9
  39.4 8.5 %collective-permute-done.8.middle = bf16[768,256]{1,0:T(8,128)(2,1)S(1)} collective-permute-done((bf16[768,256]{1,0:T(8,128)(2,1)S(1)}, bf16[768,256]{1,0:T(8,128)(2,1)S(1)}, u32[]{:S(2)}, u32[]{:S(2)}) %collective-permute-start.8) | collective-permute-done | bytes 393248 | tf_op jit(solution)/shard_map/ppermute | solution.py:59
  47.9 2.9 %collective-permute-done.9.close = bf16[512,256]{1,0:T(8,128)(2,1)S(1)} collective-permute-done((bf16[512,256]{1,0:T(8,128)(2,1)S(1)}, bf16[512,256]{1,0:T(8,128)(2,1)S(1)}, u32[]{:S(2)}, u32[]{:S(2)}) %collective-permute-start.9) | collective-permute-done | bytes 262176 | tf_op jit(solution)/shard_map/ppermute | solution.py:59
  50.8 0.1 shard_map.107
  50.9 2.2 %collective-permute-start.10 = (bf16[256,256]{1,0:T(8,128)(2,1)S(1)}, bf16[256,256]{1,0:T(8,128)(2,1)S(1)}, u32[]{:S(2)}, u32[]{:S(2)}) collective-permute-start(bf16[256,256]{1,0:T(8,128)(2,1)S(1)} %slice.27), channel_id=1, source_target_pairs={{0,4},{1,13},{2,6},{3,15},{4,8},{5,1},{6,10},{7,3},{8,12},{9,5},{1... | collective-permute-start | bytes 393224 | tf_op jit(solution)/shard_map/ppermute | solution.py:59
  53.1 0.8 %collective-permute-start.12 = (bf16[256,256]{1,0:T(8,128)(2,1)S(1)}, bf16[256,256]{1,0:T(8,128)(2,1)S(1)}, u32[]{:S(2)}, u32[]{:S(2)}) collective-permute-start(bf16[256,256]{1,0:T(8,128)(2,1)S(1)} %get-tuple-element.24), channel_id=1, source_target_pairs={{0,3},{1,14},{2,5},{3,0},{4,7},{5,2},{6,9},{7,4},{8,11},{9,6},{10,... | collective-permute-start | bytes 393224 | tf_op jit(solution)/shard_map/ppermute | solution.py:59
  53.9 2.3 %collective-permute-start.11 = (bf16[256,256]{1,0:T(8,128)(2,1)S(1)}, bf16[256,256]{1,0:T(8,128)(2,1)S(1)}, u32[]{:S(2)}, u32[]{:S(2)}) collective-permute-start(bf16[256,256]{1,0:T(8,128)(2,1)S(1)} %get-tuple-element.22), channel_id=1, source_target_pairs={{0,2},{1,15},{2,4},{3,1},{4,6},{5,3},{6,8},{7,5},{8,10},{9,7},{10,... | collective-permute-start | bytes 393224 | tf_op jit(solution)/shard_map/ppermute | solution.py:59
  56.2 0.0 collective-permute-done.10
  56.2 3.9 %collective-permute-done.12 = bf16[256,256]{1,0:T(8,128)(2,1)S(1)} collective-permute-done((bf16[256,256]{1,0:T(8,128)(2,1)S(1)}, bf16[256,256]{1,0:T(8,128)(2,1)S(1)}, u32[]{:S(2)}, u32[]{:S(2)}) %collective-permute-start.12) | collective-permute-done | bytes 131104 | tf_op jit(solution)/shard_map/ppermute | solution.py:59
  60.1 0.6 collective-permute-done.11
  60.7 0.7 %fusion.5 = bf16[256,256]{1,0:T(8,128)(2,1)} fusion(f32[2,128,256]{2,1,0:T(8,128)S(1)} %slice.24, bf16[256,256]{1,0:T(8,128)(2,1)S(1)} %collective-permute-done.12, bf16[256,256]{1,0:T(8,128)(2,1)S(1)} %collective-permute-done.11, bf16[256,256]{1,0:T(8,128)(2,1)S(1)} %collective-permute-done.10, bf16[1280,256]{1,0:T(8,128)(2,1)S(1)} %collective-permute-done.6.swapped), kind=kLoop, calls=%fused_computation.8 | loop fusion | flops 589824 | bytes 917504 | tf_op jit(solution)/shard_map/convert_element_type | solution.py:407
  (4 shorter events, 0.1 us)
Async XLA Ops:
  0.0 18.4 %copy-start = (bf16[28,2,128,128]{3,2,1,0:T(8,128)(2,1)S(1)}, bf16[28,2,128,128]{3,2,1,0:T(8,128)(2,1)}, u32[]{:S(2)}) copy-start(bf16[28,2,128,128]{3,2,1,0:T(8,128)(2,1)} %near_ref.7) | copy-start | bytes 5505028
  1.3 6.2 %collective-permute-start.2 = (bf16[256,256]{1,0:T(8,128)(2,1)S(1)}, bf16[256,256]{1,0:T(8,128)(2,1)S(1)}, u32[]{:S(2)}, u32[]{:S(2)}) collective-permute-start(bf16[256,256]{1,0:T(8,128)(2,1)S(1)} %shard_map.101.refs_0_), channel_id=1, source_target_pairs={{0,128},{1,33},{2,130},{3,35},{4,132},{5,37},{6,134},{7,39},{8,136... | collective-permute-start | bytes 393224 | tf_op jit(solution)/shard_map/ppermute | solution.py:50
  5.1 4.4 %collective-permute-start.1 = (bf16[256,256]{1,0:T(8,128)(2,1)S(1)}, bf16[256,256]{1,0:T(8,128)(2,1)S(1)}, u32[]{:S(2)}, u32[]{:S(2)}) collective-permute-start(bf16[256,256]{1,0:T(8,128)(2,1)S(1)} %shard_map.101.refs_0_), channel_id=1, source_target_pairs={{0,192},{1,49},{2,194},{3,51},{4,196},{5,53},{6,198},{7,55},{8,200... | collective-permute-start | bytes 393224 | tf_op jit(solution)/shard_map/ppermute | solution.py:50
  5.9 5.0 %collective-permute-start = (bf16[256,256]{1,0:T(8,128)(2,1)S(1)}, bf16[256,256]{1,0:T(8,128)(2,1)S(1)}, u32[]{:S(2)}, u32[]{:S(2)}) collective-permute-start(bf16[256,256]{1,0:T(8,128)(2,1)S(1)} %shard_map.101.refs_0_), channel_id=1, source_target_pairs={{0,64},{1,17},{2,66},{3,19},{4,68},{5,21},{6,70},{7,23},{8,72},{9,... | collective-permute-start | bytes 393224 | tf_op jit(solution)/shard_map/ppermute | solution.py:50
  11.0 10.0 %collective-permute-start.5 = (bf16[1024,256]{1,0:T(8,128)(2,1)S(1)}, bf16[1024,256]{1,0:T(8,128)(2,1)S(1)}, u32[]{:S(2)}, u32[]{:S(2)}) collective-permute-start(bf16[1024,256]{1,0:T(8,128)(2,1)S(1)} %shard_map.102.piece), channel_id=1, source_target_pairs={{0,32},{1,129},{2,34},{3,131},{4,36},{5,133},{6,38},{7,135},{8,40}... | collective-permute-start | bytes 1572872 | tf_op jit(solution)/shard_map/ppermute | solution.py:50
  13.8 12.8 %collective-permute-start.4 = (bf16[1024,256]{1,0:T(8,128)(2,1)S(1)}, bf16[1024,256]{1,0:T(8,128)(2,1)S(1)}, u32[]{:S(2)}, u32[]{:S(2)}) collective-permute-start(bf16[1024,256]{1,0:T(8,128)(2,1)S(1)} %shard_map.102.piece), channel_id=1, source_target_pairs={{0,48},{1,193},{2,50},{3,195},{4,52},{5,197},{6,54},{7,199},{8,56}... | collective-permute-start | bytes 1572872 | tf_op jit(solution)/shard_map/ppermute | solution.py:50
  14.6 12.0 %collective-permute-start.3 = (bf16[1024,256]{1,0:T(8,128)(2,1)S(1)}, bf16[1024,256]{1,0:T(8,128)(2,1)S(1)}, u32[]{:S(2)}, u32[]{:S(2)}) collective-permute-start(bf16[1024,256]{1,0:T(8,128)(2,1)S(1)} %shard_map.102.piece), channel_id=1, source_target_pairs={{0,16},{1,65},{2,18},{3,67},{4,20},{5,69},{6,22},{7,71},{8,24},{9,... | collective-permute-start | bytes 1572872 | tf_op jit(solution)/shard_map/ppermute | solution.py:50
  28.0 4.8 %collective-permute-start.7 = (bf16[768,256]{1,0:T(8,128)(2,1)S(1)}, bf16[768,256]{1,0:T(8,128)(2,1)S(1)}, u32[]{:S(2)}, u32[]{:S(2)}) collective-permute-start(bf16[768,256]{1,0:T(8,128)(2,1)S(1)} %get-tuple-element.21), channel_id=1, source_target_pairs={{0,1},{1,0},{2,3},{3,2},{4,5},{5,4},{6,7},{7,6},{8,9},{9,8},{10,11... | collective-permute-start | bytes 1179656 | tf_op jit(solution)/shard_map/ppermute | solution.py:63
  31.5 7.5 %collective-permute-start.6 = (bf16[1280,256]{1,0:T(8,128)(2,1)S(1)}, bf16[1280,256]{1,0:T(8,128)(2,1)S(1)}, u32[]{:S(2)}, u32[]{:S(2)}) collective-permute-start(bf16[1280,256]{1,0:T(8,128)(2,1)S(1)} %get-tuple-element.20), channel_id=1, source_target_pairs={{0,1},{1,0},{2,3},{3,2},{4,5},{5,4},{6,7},{7,6},{8,9},{9,8},{10,11... | collective-permute-start | bytes 1966088 | tf_op jit(solution)/shard_map/ppermute | solution.py:63
  32.9 15.0 %collective-permute-start.8 = (bf16[768,256]{1,0:T(8,128)(2,1)S(1)}, bf16[768,256]{1,0:T(8,128)(2,1)S(1)}, u32[]{:S(2)}, u32[]{:S(2)}) collective-permute-start(bf16[768,256]{1,0:T(8,128)(2,1)S(1)} %fusion), channel_id=1, source_target_pairs={{0,4},{1,13},{2,6},{3,15},{4,8},{5,1},{6,10},{7,3},{8,12},{9,5},{1... | collective-permute-start | bytes 1179656 | tf_op jit(solution)/shard_map/ppermute | solution.py:59
  39.0 11.7 %collective-permute-start.9 = (bf16[512,256]{1,0:T(8,128)(2,1)S(1)}, bf16[512,256]{1,0:T(8,128)(2,1)S(1)}, u32[]{:S(2)}, u32[]{:S(2)}) collective-permute-start(bf16[512,256]{1,0:T(8,128)(2,1)S(1)} %fusion.1), channel_id=1, source_target_pairs={{0,2},{1,15},{2,4},{3,1},{4,6},{5,3},{6,8},{7,5},{8,10},{9,7},{10,... | collective-permute-start | bytes 786440 | tf_op jit(solution)/shard_map/ppermute | solution.py:59
  50.9 5.3 %collective-permute-start.10 = (bf16[256,256]{1,0:T(8,128)(2,1)S(1)}, bf16[256,256]{1,0:T(8,128)(2,1)S(1)}, u32[]{:S(2)}, u32[]{:S(2)}) collective-permute-start(bf16[256,256]{1,0:T(8,128)(2,1)S(1)} %slice.27), channel_id=1, source_target_pairs={{0,4},{1,13},{2,6},{3,15},{4,8},{5,1},{6,10},{7,3},{8,12},{9,5},{1... | collective-permute-start | bytes 393224 | tf_op jit(solution)/shard_map/ppermute | solution.py:59
  53.1 7.0 %collective-permute-start.12 = (bf16[256,256]{1,0:T(8,128)(2,1)S(1)}, bf16[256,256]{1,0:T(8,128)(2,1)S(1)}, u32[]{:S(2)}, u32[]{:S(2)}) collective-permute-start(bf16[256,256]{1,0:T(8,128)(2,1)S(1)} %get-tuple-element.24), channel_id=1, source_target_pairs={{0,3},{1,14},{2,5},{3,0},{4,7},{5,2},{6,9},{7,4},{8,11},{9,6},{10,... | collective-permute-start | bytes 393224 | tf_op jit(solution)/shard_map/ppermute | solution.py:59
  53.9 6.8 %collective-permute-start.11 = (bf16[256,256]{1,0:T(8,128)(2,1)S(1)}, bf16[256,256]{1,0:T(8,128)(2,1)S(1)}, u32[]{:S(2)}, u32[]{:S(2)}) collective-permute-start(bf16[256,256]{1,0:T(8,128)(2,1)S(1)} %get-tuple-element.22), channel_id=1, source_target_pairs={{0,2},{1,15},{2,4},{3,1},{4,6},{5,3},{6,8},{7,5},{8,10},{9,7},{10,... | collective-permute-start | bytes 393224 | tf_op jit(solution)/shard_map/ppermute | solution.py:59

commit v8 on v7

--- a/solution.py
+++ b/solution.py
@@ -169,9 +169,9 @@
         near = jnp.where(straight, 14 - 14 * (dz >> 2) + i, 14 - 4 * steps + owner * 2 + i)
         own = jnp.where(handler == my_core, 1, 0)
         target = own * 16 + near
-        late = (piece == 1) | (piece == 2)
+        late = (piece == 2) | (piece == 3)
         group = jnp.where(late, 2 + own, jnp.where(piece == 0, 0, 1))
-        slot = jnp.where(piece == 2, 8 + place, place)
+        slot = jnp.where(piece == 3, 8 + place, place)
         return group, b | (slot << 6) | (target << 11)
 
     def fill(count, rows, cols, kind):
@@ -295,9 +295,9 @@
     work(1, lists, u_ref, v_ref, near_ref, trial, total)
 
 
-def third_kernel(lists, u_ref, v_ref, near_ref, ahead, back, _, total, trial, one_ref, two_ref):
-    load(ahead, trial, 0)
-    load(back, trial, 8)
+def third_kernel(lists, u_ref, v_ref, near_ref, back, two, _, total, trial, one_ref, two_ref):
+    load(back, trial, 0)
+    load(two, trial, 8)
     work(2, lists, u_ref, v_ref, near_ref, trial, total)
     for t in range(FIRST):
         one_ref[t * LEAF : (t + 1) * LEAF, :] = total[t].astype(BF16)
@@ -330,7 +330,7 @@
         input_output_aliases={5: 0},
         compiler_params=limit(6),
         cost_estimate=cost(6),
-    )(*common, two, total)
+    )(*common, ahead, total)
     total, trial, one, other = pl.pallas_call(
         third_kernel,
         out_shape=(
@@ -344,7 +344,7 @@
         input_output_aliases={6: 0},
         compiler_params=limit(6),
         cost_estimate=cost(8),
-    )(*common, ahead, back, total)
+    )(*common, back, two, total)
     total = pl.pallas_call(
         fourth_kernel,
         out_shape=TOTAL,
@@ -358,9 +358,9 @@
 
 
 def gather(mine):
-    two, back, ahead = [hop(0, step, mine) for step in (2, -1, 1)]
+    ahead, back, two = [hop(0, step, mine) for step in (1, -1, 2)]
     first = weave([mine, ahead, back, two])
-    two, back, ahead = [hop(1, step, first) for step in (2, -1, 1)]
+    ahead, back, two = [hop(1, step, first) for step in (1, -1, 2)]
     return [first, ahead, back, two]
 
 

time: 61.8 us -> 62.6 us (1.013)
    ppermute x5, starting transfers between devices: 11.8 us -> 10.8 us  [along_z(): return lax.ppermute(value, 'col', pairs)]
  transfers between devices with their start and end apart: 13 -> 13, of which waited for: 10 -> 9; matrix products, arithmetic and copies ran while one was open for 0% -> 0% of each run, Pallas kernels for 11% -> 11%
where the time goes in v8:
time: 62.6 us; the launch traced here: 62 us
  waiting for transfers between devices  26.3 us (42%)
  starting transfers between devices  25.1 us (40%)
  Pallas kernels  9.42 us (15%)
  other arithmetic  0.88 us (1%)
    ppermute x5, waiting for transfers between devices, along_z(): return lax.ppermute(value, 'col', pairs)  15.8 us
    ppermute x5, starting transfers between devices, along_z(): return lax.ppermute(value, 'col', pairs)  10.8 us
    ppermute x6, waiting for transfers between devices, hop(): return lax.ppermute(value, ('row', 'col'), pairs)  10.5 us
    ppermute x6, starting transfers between devices, hop(): return lax.ppermute(value, ('row', 'col'), pairs)  10.2 us
    ppermute x2, starting transfers between devices, other_core(): return lax.ppermute(value, 'col', [(d, d ^ 1) for d in range(NZ * NCORE)])  4.12 us
    pallas_call x1, Pallas kernels, prepare(): pl.pallas_call(prepare_kernel, out_shape=(pltpu.VMEM((NB, LEAF, 2 * RMAX)...  3.09 us
    pallas_call x1, Pallas kernels, blocks(): pl.pallas_call(fourth_kernel, out_shape=TOTAL, in_specs=[SMEM] + [VMEM] *...  1.57 us
    pallas_call x1, Pallas kernels, blocks(): pl.pallas_call(first_kernel, out_shape=TOTAL, in_specs=[SMEM] + [VMEM] *...  1.41 us
  transfers between devices with their start and end apart: 13, of which 9 were waited for; matrix products, arithmetic and copies ran while one was open for 0% of the time, Pallas kernels for 11%

profile of v8, /device:TPU:1, one launch (start us, length us, event | category | flops | bytes accessed | tf_op | source)
XLA Modules:
  0.0 62.0 jit_solution(10733437191074489913)
XLA Ops:
  0.0 0.0 copy-start
  0.0 1.3 %shard_map.101.refs_0_ = bf16[256,256]{1,0:T(8,128)(2,1)S(1)} custom-call(s32[2,128]{1,0:T(2,128)} %perm_hbm.1, bf16[256,256]{1,0:T(8,128)(2,1)} %x_hbm.1), custom_call_target="tpu_custom_call" | custom-call | tf_op jit(solution)/shard_map/pallas_call | solution.py:91
  1.3 3.8 %collective-permute-start.2 = (bf16[256,256]{1,0:T(8,128)(2,1)S(1)}, bf16[256,256]{1,0:T(8,128)(2,1)S(1)}, u32[]{:S(2)}, u32[]{:S(2)}) collective-permute-start(bf16[256,256]{1,0:T(8,128)(2,1)S(1)} %shard_map.101.refs_0_), channel_id=1, source_target_pairs={{0,128},{1,33},{2,130},{3,35},{4,132},{5,37},{6,134},{7,39},{8,136... | collective-permute-start | bytes 393224 | tf_op jit(solution)/shard_map/ppermute | solution.py:50
  5.1 0.8 %collective-permute-start.1 = (bf16[256,256]{1,0:T(8,128)(2,1)S(1)}, bf16[256,256]{1,0:T(8,128)(2,1)S(1)}, u32[]{:S(2)}, u32[]{:S(2)}) collective-permute-start(bf16[256,256]{1,0:T(8,128)(2,1)S(1)} %shard_map.101.refs_0_), channel_id=1, source_target_pairs={{0,192},{1,49},{2,194},{3,51},{4,196},{5,53},{6,198},{7,55},{8,200... | collective-permute-start | bytes 393224 | tf_op jit(solution)/shard_map/ppermute | solution.py:50
  5.9 0.7 %collective-permute-start = (bf16[256,256]{1,0:T(8,128)(2,1)S(1)}, bf16[256,256]{1,0:T(8,128)(2,1)S(1)}, u32[]{:S(2)}, u32[]{:S(2)}) collective-permute-start(bf16[256,256]{1,0:T(8,128)(2,1)S(1)} %shard_map.101.refs_0_), channel_id=1, source_target_pairs={{0,64},{1,17},{2,66},{3,19},{4,68},{5,21},{6,70},{7,23},{8,72},{9,... | collective-permute-start | bytes 393224 | tf_op jit(solution)/shard_map/ppermute | solution.py:50
  6.6 0.9 %collective-permute-done.2.refs_3_ = bf16[256,256]{1,0:T(8,128)(2,1)S(1)} collective-permute-done((bf16[256,256]{1,0:T(8,128)(2,1)S(1)}, bf16[256,256]{1,0:T(8,128)(2,1)S(1)}, u32[]{:S(2)}, u32[]{:S(2)}) %collective-permute-start.2) | collective-permute-done | bytes 131104 | tf_op jit(solution)/shard_map/ppermute | solution.py:50
  7.5 2.1 %collective-permute-done.1.refs_2_ = bf16[256,256]{1,0:T(8,128)(2,1)S(1)} collective-permute-done((bf16[256,256]{1,0:T(8,128)(2,1)S(1)}, bf16[256,256]{1,0:T(8,128)(2,1)S(1)}, u32[]{:S(2)}, u32[]{:S(2)}) %collective-permute-start.1) | collective-permute-done | bytes 131104 | tf_op jit(solution)/shard_map/ppermute | solution.py:50
  9.6 1.4 %collective-permute-done.refs_1_ = bf16[256,256]{1,0:T(8,128)(2,1)S(1)} collective-permute-done((bf16[256,256]{1,0:T(8,128)(2,1)S(1)}, bf16[256,256]{1,0:T(8,128)(2,1)S(1)}, u32[]{:S(2)}, u32[]{:S(2)}) %collective-permute-start) | collective-permute-done | bytes 131104 | tf_op jit(solution)/shard_map/ppermute | solution.py:50
  11.0 1.3 %collective-permute-start.5 = (bf16[1024,256]{1,0:T(8,128)(2,1)S(1)}, bf16[1024,256]{1,0:T(8,128)(2,1)S(1)}, u32[]{:S(2)}, u32[]{:S(2)}) collective-permute-start(bf16[1024,256]{1,0:T(8,128)(2,1)S(1)} %shard_map.102.piece), channel_id=1, source_target_pairs={{0,16},{1,65},{2,18},{3,67},{4,20},{5,69},{6,22},{7,71},{8,24},{9,... | collective-permute-start | bytes 1572872 | tf_op jit(solution)/shard_map/ppermute | solution.py:50
  12.2 2.4 %collective-permute-start.4 = (bf16[1024,256]{1,0:T(8,128)(2,1)S(1)}, bf16[1024,256]{1,0:T(8,128)(2,1)S(1)}, u32[]{:S(2)}, u32[]{:S(2)}) collective-permute-start(bf16[1024,256]{1,0:T(8,128)(2,1)S(1)} %shard_map.102.piece), channel_id=1, source_target_pairs={{0,32},{1,129},{2,34},{3,131},{4,36},{5,133},{6,38},{7,135},{8,40}... | collective-permute-start | bytes 1572872 | tf_op jit(solution)/shard_map/ppermute | solution.py:50
  14.7 1.2 %collective-permute-start.3 = (bf16[1024,256]{1,0:T(8,128)(2,1)S(1)}, bf16[1024,256]{1,0:T(8,128)(2,1)S(1)}, u32[]{:S(2)}, u32[]{:S(2)}) collective-permute-start(bf16[1024,256]{1,0:T(8,128)(2,1)S(1)} %shard_map.102.piece), channel_id=1, source_target_pairs={{0,48},{1,193},{2,50},{3,195},{4,52},{5,197},{6,54},{7,199},{8,56}... | collective-permute-start | bytes 1572872 | tf_op jit(solution)/shard_map/ppermute | solution.py:50
  15.8 3.1 %shard_map.100 = (bf16[32,128,128]{2,1,0:T(8,128)(2,1)S(1)}, bf16[32,64,256]{2,1,0:T(8,128)(2,1)S(1)}, s32[296]{0:T(512)S(4)}) custom-call(s32[32]{0:T(128)} %rank_hbm.1, s32[32]{0:T(128)} %far_rows_hbm.1, s32[32]{0:T(128)} %far_cols_hbm.1, s32[28]{0:T(128)} %near_rows_hbm.1, s32[28]{0:T(128)} %near_cols_hbm.1, bf16[32,2,64,128]{3,2,1,0:T(8,128)(2,1)} %bitcast.20, ...), custom_call_target="tpu_custom_call" | custom-call | bytes 8388608 | tf_op jit(solution)/shard_map/pallas_call | solution.py:221
  18.9 0.0 copy-done
  19.0 1.4 %shard_map.103._ = f32[33,128,256]{2,1,0:T(8,128)S(1)} custom-call(s32[296]{0:T(512)S(4)} %get-tuple-element.15.lists, bf16[32,128,128]{2,1,0:T(8,128)(2,1)S(1)} %get-tuple-element.16.u_ref, bf16[32,64,256]{2,1,0:T(8,128)(2,1)S(1)} %get-tuple-element.17.v_ref, bf16[28,2,128,128]{3,2,1,0:T(8,128)(2,1)S(1)} %copy-done, bf16[1024,256]{1,0:T(8,128)(2,1)S(1)} %shard_map.102.piece), custom_call_target="tpu_custom_call" | custom-call | bytes 8388608 | tf_op jit(solution)/shard_map/pallas_call | solution.py:315
  20.4 0.2 collective-permute-done.5.piece
  20.6 0.6 shard_map.104._
  21.2 6.0 %collective-permute-done.4.two = bf16[1024,256]{1,0:T(8,128)(2,1)S(1)} collective-permute-done((bf16[1024,256]{1,0:T(8,128)(2,1)S(1)}, bf16[1024,256]{1,0:T(8,128)(2,1)S(1)}, u32[]{:S(2)}, u32[]{:S(2)}) %collective-permute-start.4) | collective-permute-done | bytes 524320 | tf_op jit(solution)/shard_map/ppermute | solution.py:50
  27.2 0.0 collective-permute-done.3.back
  27.2 1.3 %shard_map.105 = (f32[33,128,256]{2,1,0:T(8,128)S(1)}, bf16[16,256,256]{2,1,0:T(8,128)(2,1)S(1)}, bf16[768,256]{1,0:T(8,128)(2,1)S(1)}, bf16[1280,256]{1,0:T(8,128)(2,1)S(1)}) custom-call(s32[296]{0:T(512)S(4)} %get-tuple-element.15.lists, bf16[32,128,128]{2,1,0:T(8,128)(2,1)S(1)} %get-tuple-element.16.u_ref, ...), custom_call_target="tpu_custom_call", output_to_operand_aliasing={{0}: (6, {})} | custom-call | bytes 8388608 | tf_op jit(solution)/shard_map/pallas_call | solution.py:334
  28.5 4.0 %collective-permute-start.7 = (bf16[768,256]{1,0:T(8,128)(2,1)S(1)}, bf16[768,256]{1,0:T(8,128)(2,1)S(1)}, u32[]{:S(2)}, u32[]{:S(2)}) collective-permute-start(bf16[768,256]{1,0:T(8,128)(2,1)S(1)} %get-tuple-element.21), channel_id=1, source_target_pairs={{0,1},{1,0},{2,3},{3,2},{4,5},{5,4},{6,7},{7,6},{8,9},{9,8},{10,11... | collective-permute-start | bytes 1179656 | tf_op jit(solution)/shard_map/ppermute | solution.py:63
  32.5 0.1 collective-permute-start.6
  32.6 1.6 %shard_map.106.own = f32[33,128,256]{2,1,0:T(8,128)S(1)} custom-call(s32[296]{0:T(512)S(4)} %get-tuple-element.15.lists, bf16[32,128,128]{2,1,0:T(8,128)(2,1)S(1)} %get-tuple-element.16.u_ref, bf16[32,64,256]{2,1,0:T(8,128)(2,1)S(1)} %get-tuple-element.17.v_ref, bf16[28,2,128,128]{3,2,1,0:T(8,128)(2,1)S(1)} %copy-done, ...), custom_call_target="tpu_custom_call", output_to_operand_aliasing={{}: (5, {})} | custom-call | bytes 6291456 | tf_op jit(solution)/shard_map/pallas_call | solution.py:348
  34.3 0.1 slice.26
  34.3 0.0 collective-permute-done.7
  34.3 0.1 fusion
  34.4 4.6 %collective-permute-start.8 = (bf16[768,256]{1,0:T(8,128)(2,1)S(1)}, bf16[768,256]{1,0:T(8,128)(2,1)S(1)}, u32[]{:S(2)}, u32[]{:S(2)}) collective-permute-start(bf16[768,256]{1,0:T(8,128)(2,1)S(1)} %fusion), channel_id=1, source_target_pairs={{0,4},{1,13},{2,6},{3,15},{4,8},{5,1},{6,10},{7,3},{8,12},{9,5},{1... | collective-permute-start | bytes 1179656 | tf_op jit(solution)/shard_map/ppermute | solution.py:59
  39.0 0.0 collective-permute-done.6.swapped
  39.0 0.1 fusion.1
  39.1 1.3 %collective-permute-start.9 = (bf16[512,256]{1,0:T(8,128)(2,1)S(1)}, bf16[512,256]{1,0:T(8,128)(2,1)S(1)}, u32[]{:S(2)}, u32[]{:S(2)}) collective-permute-start(bf16[512,256]{1,0:T(8,128)(2,1)S(1)} %fusion.1), channel_id=1, source_target_pairs={{0,2},{1,15},{2,4},{3,1},{4,6},{5,3},{6,8},{7,5},{8,10},{9,7},{10,... | collective-permute-start | bytes 786440 | tf_op jit(solution)/shard_map/ppermute | solution.py:59
  40.4 5.9 %collective-permute-done.8.middle = bf16[768,256]{1,0:T(8,128)(2,1)S(1)} collective-permute-done((bf16[768,256]{1,0:T(8,128)(2,1)S(1)}, bf16[768,256]{1,0:T(8,128)(2,1)S(1)}, u32[]{:S(2)}, u32[]{:S(2)}) %collective-permute-start.8) | collective-permute-done | bytes 393248 | tf_op jit(solution)/shard_map/ppermute | solution.py:59
  46.3 5.4 %collective-permute-done.9.close = bf16[512,256]{1,0:T(8,128)(2,1)S(1)} collective-permute-done((bf16[512,256]{1,0:T(8,128)(2,1)S(1)}, bf16[512,256]{1,0:T(8,128)(2,1)S(1)}, u32[]{:S(2)}, u32[]{:S(2)}) %collective-permute-start.9) | collective-permute-done | bytes 262176 | tf_op jit(solution)/shard_map/ppermute | solution.py:59
  51.7 0.1 shard_map.107
  51.8 2.4 %collective-permute-start.10 = (bf16[256,256]{1,0:T(8,128)(2,1)S(1)}, bf16[256,256]{1,0:T(8,128)(2,1)S(1)}, u32[]{:S(2)}, u32[]{:S(2)}) collective-permute-start(bf16[256,256]{1,0:T(8,128)(2,1)S(1)} %slice.27), channel_id=1, source_target_pairs={{0,4},{1,13},{2,6},{3,15},{4,8},{5,1},{6,10},{7,3},{8,12},{9,5},{1... | collective-permute-start | bytes 393224 | tf_op jit(solution)/shard_map/ppermute | solution.py:59
  54.2 0.2 collective-permute-start.12
  54.5 2.3 %collective-permute-start.11 = (bf16[256,256]{1,0:T(8,128)(2,1)S(1)}, bf16[256,256]{1,0:T(8,128)(2,1)S(1)}, u32[]{:S(2)}, u32[]{:S(2)}) collective-permute-start(bf16[256,256]{1,0:T(8,128)(2,1)S(1)} %get-tuple-element.22), channel_id=1, source_target_pairs={{0,2},{1,15},{2,4},{3,1},{4,6},{5,3},{6,8},{7,5},{8,10},{9,7},{10,... | collective-permute-start | bytes 393224 | tf_op jit(solution)/shard_map/ppermute | solution.py:59
  56.7 0.0 collective-permute-done.10
  56.7 4.0 %collective-permute-done.12 = bf16[256,256]{1,0:T(8,128)(2,1)S(1)} collective-permute-done((bf16[256,256]{1,0:T(8,128)(2,1)S(1)}, bf16[256,256]{1,0:T(8,128)(2,1)S(1)}, u32[]{:S(2)}, u32[]{:S(2)}) %collective-permute-start.12) | collective-permute-done | bytes 131104 | tf_op jit(solution)/shard_map/ppermute | solution.py:59
  60.7 0.5 collective-permute-done.11
  61.2 0.7 %fusion.5 = bf16[256,256]{1,0:T(8,128)(2,1)} fusion(f32[2,128,256]{2,1,0:T(8,128)S(1)} %slice.24, bf16[256,256]{1,0:T(8,128)(2,1)S(1)} %collective-permute-done.12, bf16[256,256]{1,0:T(8,128)(2,1)S(1)} %collective-permute-done.11, bf16[256,256]{1,0:T(8,128)(2,1)S(1)} %collective-permute-done.10, bf16[1280,256]{1,0:T(8,128)(2,1)S(1)} %collective-permute-done.6.swapped), kind=kLoop, calls=%fused_computation.8 | loop fusion | flops 589824 | bytes 917504 | tf_op jit(solution)/shard_map/convert_element_type | solution.py:407
  (4 shorter events, 0.1 us)
Async XLA Ops:
  0.0 18.9 %copy-start = (bf16[28,2,128,128]{3,2,1,0:T(8,128)(2,1)S(1)}, bf16[28,2,128,128]{3,2,1,0:T(8,128)(2,1)}, u32[]{:S(2)}) copy-start(bf16[28,2,128,128]{3,2,1,0:T(8,128)(2,1)} %near_ref.7) | copy-start | bytes 5505028
  1.3 6.2 %collective-permute-start.2 = (bf16[256,256]{1,0:T(8,128)(2,1)S(1)}, bf16[256,256]{1,0:T(8,128)(2,1)S(1)}, u32[]{:S(2)}, u32[]{:S(2)}) collective-permute-start(bf16[256,256]{1,0:T(8,128)(2,1)S(1)} %shard_map.101.refs_0_), channel_id=1, source_target_pairs={{0,128},{1,33},{2,130},{3,35},{4,132},{5,37},{6,134},{7,39},{8,136... | collective-permute-start | bytes 393224 | tf_op jit(solution)/shard_map/ppermute | solution.py:50
  5.1 4.4 %collective-permute-start.1 = (bf16[256,256]{1,0:T(8,128)(2,1)S(1)}, bf16[256,256]{1,0:T(8,128)(2,1)S(1)}, u32[]{:S(2)}, u32[]{:S(2)}) collective-permute-start(bf16[256,256]{1,0:T(8,128)(2,1)S(1)} %shard_map.101.refs_0_), channel_id=1, source_target_pairs={{0,192},{1,49},{2,194},{3,51},{4,196},{5,53},{6,198},{7,55},{8,200... | collective-permute-start | bytes 393224 | tf_op jit(solution)/shard_map/ppermute | solution.py:50
  5.9 5.0 %collective-permute-start = (bf16[256,256]{1,0:T(8,128)(2,1)S(1)}, bf16[256,256]{1,0:T(8,128)(2,1)S(1)}, u32[]{:S(2)}, u32[]{:S(2)}) collective-permute-start(bf16[256,256]{1,0:T(8,128)(2,1)S(1)} %shard_map.101.refs_0_), channel_id=1, source_target_pairs={{0,64},{1,17},{2,66},{3,19},{4,68},{5,21},{6,70},{7,23},{8,72},{9,... | collective-permute-start | bytes 393224 | tf_op jit(solution)/shard_map/ppermute | solution.py:50
  11.0 9.6 %collective-permute-start.5 = (bf16[1024,256]{1,0:T(8,128)(2,1)S(1)}, bf16[1024,256]{1,0:T(8,128)(2,1)S(1)}, u32[]{:S(2)}, u32[]{:S(2)}) collective-permute-start(bf16[1024,256]{1,0:T(8,128)(2,1)S(1)} %shard_map.102.piece), channel_id=1, source_target_pairs={{0,16},{1,65},{2,18},{3,67},{4,20},{5,69},{6,22},{7,71},{8,24},{9,... | collective-permute-start | bytes 1572872 | tf_op jit(solution)/shard_map/ppermute | solution.py:50
  12.2 14.9 %collective-permute-start.4 = (bf16[1024,256]{1,0:T(8,128)(2,1)S(1)}, bf16[1024,256]{1,0:T(8,128)(2,1)S(1)}, u32[]{:S(2)}, u32[]{:S(2)}) collective-permute-start(bf16[1024,256]{1,0:T(8,128)(2,1)S(1)} %shard_map.102.piece), channel_id=1, source_target_pairs={{0,32},{1,129},{2,34},{3,131},{4,36},{5,133},{6,38},{7,135},{8,40}... | collective-permute-start | bytes 1572872 | tf_op jit(solution)/shard_map/ppermute | solution.py:50
  14.7 12.5 %collective-permute-start.3 = (bf16[1024,256]{1,0:T(8,128)(2,1)S(1)}, bf16[1024,256]{1,0:T(8,128)(2,1)S(1)}, u32[]{:S(2)}, u32[]{:S(2)}) collective-permute-start(bf16[1024,256]{1,0:T(8,128)(2,1)S(1)} %shard_map.102.piece), channel_id=1, source_target_pairs={{0,48},{1,193},{2,50},{3,195},{4,52},{5,197},{6,54},{7,199},{8,56}... | collective-permute-start | bytes 1572872 | tf_op jit(solution)/shard_map/ppermute | solution.py:50
  28.5 5.8 %collective-permute-start.7 = (bf16[768,256]{1,0:T(8,128)(2,1)S(1)}, bf16[768,256]{1,0:T(8,128)(2,1)S(1)}, u32[]{:S(2)}, u32[]{:S(2)}) collective-permute-start(bf16[768,256]{1,0:T(8,128)(2,1)S(1)} %get-tuple-element.21), channel_id=1, source_target_pairs={{0,1},{1,0},{2,3},{3,2},{4,5},{5,4},{6,7},{7,6},{8,9},{9,8},{10,11... | collective-permute-start | bytes 1179656 | tf_op jit(solution)/shard_map/ppermute | solution.py:63
  32.5 6.5 %collective-permute-start.6 = (bf16[1280,256]{1,0:T(8,128)(2,1)S(1)}, bf16[1280,256]{1,0:T(8,128)(2,1)S(1)}, u32[]{:S(2)}, u32[]{:S(2)}) collective-permute-start(bf16[1280,256]{1,0:T(8,128)(2,1)S(1)} %get-tuple-element.20), channel_id=1, source_target_pairs={{0,1},{1,0},{2,3},{3,2},{4,5},{5,4},{6,7},{7,6},{8,9},{9,8},{10,11... | collective-permute-start | bytes 1966088 | tf_op jit(solution)/shard_map/ppermute | solution.py:63
  34.4 11.8 %collective-permute-start.8 = (bf16[768,256]{1,0:T(8,128)(2,1)S(1)}, bf16[768,256]{1,0:T(8,128)(2,1)S(1)}, u32[]{:S(2)}, u32[]{:S(2)}) collective-permute-start(bf16[768,256]{1,0:T(8,128)(2,1)S(1)} %fusion), channel_id=1, source_target_pairs={{0,4},{1,13},{2,6},{3,15},{4,8},{5,1},{6,10},{7,3},{8,12},{9,5},{1... | collective-permute-start | bytes 1179656 | tf_op jit(solution)/shard_map/ppermute | solution.py:59
  39.1 12.6 %collective-permute-start.9 = (bf16[512,256]{1,0:T(8,128)(2,1)S(1)}, bf16[512,256]{1,0:T(8,128)(2,1)S(1)}, u32[]{:S(2)}, u32[]{:S(2)}) collective-permute-start(bf16[512,256]{1,0:T(8,128)(2,1)S(1)} %fusion.1), channel_id=1, source_target_pairs={{0,2},{1,15},{2,4},{3,1},{4,6},{5,3},{6,8},{7,5},{8,10},{9,7},{10,... | collective-permute-start | bytes 786440 | tf_op jit(solution)/shard_map/ppermute | solution.py:59
  51.8 4.9 %collective-permute-start.10 = (bf16[256,256]{1,0:T(8,128)(2,1)S(1)}, bf16[256,256]{1,0:T(8,128)(2,1)S(1)}, u32[]{:S(2)}, u32[]{:S(2)}) collective-permute-start(bf16[256,256]{1,0:T(8,128)(2,1)S(1)} %slice.27), channel_id=1, source_target_pairs={{0,4},{1,13},{2,6},{3,15},{4,8},{5,1},{6,10},{7,3},{8,12},{9,5},{1... | collective-permute-start | bytes 393224 | tf_op jit(solution)/shard_map/ppermute | solution.py:59
  54.2 6.5 %collective-permute-start.12 = (bf16[256,256]{1,0:T(8,128)(2,1)S(1)}, bf16[256,256]{1,0:T(8,128)(2,1)S(1)}, u32[]{:S(2)}, u32[]{:S(2)}) collective-permute-start(bf16[256,256]{1,0:T(8,128)(2,1)S(1)} %get-tuple-element.24), channel_id=1, source_target_pairs={{0,3},{1,14},{2,5},{3,0},{4,7},{5,2},{6,9},{7,4},{8,11},{9,6},{10,... | collective-permute-start | bytes 393224 | tf_op jit(solution)/shard_map/ppermute | solution.py:59
  54.5 6.8 %collective-permute-start.11 = (bf16[256,256]{1,0:T(8,128)(2,1)S(1)}, bf16[256,256]{1,0:T(8,128)(2,1)S(1)}, u32[]{:S(2)}, u32[]{:S(2)}) collective-permute-start(bf16[256,256]{1,0:T(8,128)(2,1)S(1)} %get-tuple-element.22), channel_id=1, source_target_pairs={{0,2},{1,15},{2,4},{3,1},{4,6},{5,3},{6,8},{7,5},{8,10},{9,7},{10,... | collective-permute-start | bytes 393224 | tf_op jit(solution)/shard_map/ppermute | solution.py:59
